TPU v7x, 256 devices: a whole 4x4x8 slice. The times are simulated.
256 devices in a mesh: grp: 8 (over x, core), row: 32 (over z, y).
Axes of the slice: x: 4, y: 4, z: 8, core: 2. Of those that a mesh axis runs over, the one named last changes fastest.
Arguments:
- a_blocks: bfloat16 [8192, 8, 4096], P(('grp', 'row')), may hold values from -1.1953125 to 1.1953125
- p_blocks: bfloat16 [8192, 4096], P(('grp', 'row')), may hold values from -0.75 to 0.75
- a_cols: int32 [8192, 8], P(('grp', 'row')), may hold values from 0 to 8191, as said below
- a_count: int32 [8192], P(('grp', 'row')), may hold values from 4 to 8
- tile_slot: int32 [8192, 8], P(('grp', 'row')), may hold values from 0 to 2047, as said below
Outputs:
- coarse: float32 [2048, 4096], P(('grp', 'row'))
Inputs may be any that keep to these rules, and one draw needn't show every extreme that they name: `a_cols`: A block row held by the device at grp index g and row index r has all its block columns on block rows of devices of grp g, or of the two devices at grp g - 1 and g + 1 (cyclically) with row index r. Among the live entries of one device's block rows, those on another device of the same group name at most 4 distinct block rows of that device, and exactly 4 for some device, for every device. `tile_slot`: every live entry of a block row held in grp g names a coarse block held by a device of grp g, the holder of coarse block s being device s // 8. Among one device's live entries at most 4 distinct coarse blocks are held by any one device, and exactly 4 for some holder, for every device.
All inputs are finite; a program needn't handle non-finite values.
Results may differ from a plain program's by a relative error of at most 0.0029.
Values may be sent and summed in bfloat16 or wider, within the bound.
No kernel may reach another device: no remote copies, remote signals or barrier semaphores. Data moves between devices by JAX's collectives and lax.ppermute only.
A program may use at most 64 MiB of HBM per device.

v0:
```python
import math

import jax
import jax.numpy as jnp
from jax import lax
from jax.sharding import PartitionSpec as P

SLOT_DEV = 8


def extended(block, sides, width):
    for axis, dim in sides:
        count = lax.axis_size(axis)
        forward = [(i, i + 1) for i in range(count - 1)]
        forward.append((count - 1, 0))
        backward = [(target, source) for source, target in forward]
        low = lax.ppermute(
            lax.slice_in_dim(block, block.shape[dim] - width, None, axis=dim), axis, forward
        )
        high = lax.ppermute(lax.slice_in_dim(block, 0, width, axis=dim), axis, backward)
        block = jnp.concatenate([low, block, high], axis=dim)
    return block


def body(a_blocks, p_blocks, a_cols, a_count, tile_slot):
    row_count = p_blocks.shape[0]
    col_count = a_blocks.shape[1]
    block_area = p_blocks.shape[1]
    block_order = math.isqrt(block_area)
    members = lax.axis_size("row")
    groups = lax.axis_size("grp")
    group_at = lax.axis_index("grp")
    active_mask = jnp.arange(col_count, dtype=jnp.int32)[None, :] < a_count[:, None]
    device_of = a_cols // row_count
    col_group = device_of // members
    col_row = device_of % members
    col_local = a_cols % row_count
    in_group = col_group == group_at
    below = col_group == (group_at + groups - 1) % groups
    padded = extended(p_blocks, (("grp", 0),), row_count)
    lower_rows = padded[:row_count]
    upper_rows = padded[2 * row_count :]
    group_rows = lax.all_gather(p_blocks, "row", axis=0, tiled=True)
    p_table = jnp.concatenate([group_rows, lower_rows, upper_rows], axis=0)
    base_at = members * row_count
    lookup = jnp.where(
        in_group,
        col_row * row_count + col_local,
        jnp.where(below, base_at + col_local, base_at + row_count + col_local),
    )
    picked = p_table[lookup]
    a_times_p = jnp.einsum(
        "rkab,rkbc->rkac",
        a_blocks.reshape(row_count, col_count, block_order, block_order),
        picked.reshape(row_count, col_count, block_order, block_order),
        preferred_element_type=jnp.float32,
    ).astype(jnp.bfloat16)
    block_tiles = jnp.einsum(
        "rba,rkbc->rkac",
        p_blocks.reshape(row_count, block_order, block_order),
        a_times_p,
        preferred_element_type=jnp.float32,
    )
    block_tiles = (block_tiles * active_mask[:, :, None, None].astype(jnp.float32)).reshape(
        row_count * col_count, block_area
    )
    owner_of = tile_slot // SLOT_DEV % members
    local_slot = tile_slot % SLOT_DEV
    spill_at = members * SLOT_DEV
    segment_index = jnp.where(active_mask, owner_of * SLOT_DEV + local_slot, spill_at).reshape(-1)
    partial_value = jax.ops.segment_sum(block_tiles, segment_index, spill_at + 1)[:spill_at]
    coarse = lax.psum_scatter(partial_value, "row", scatter_dimension=0, tiled=True)
    return coarse


def solution(mesh):
    placed = (
        P(("grp", "row"), None, None),
        P(("grp", "row"), None),
        P(("grp", "row"), None),
        P(("grp", "row")),
        P(("grp", "row"), None),
    )
    return jax.shard_map(
        body, mesh=mesh, in_specs=placed, out_specs=P(("grp", "row"), None), check_vma=False
    )
```

profile of v0, /device:TPU:38, one launch (start us, length us, event | category | flops | bytes accessed | tf_op | source)
XLA Modules:
  0.0 396.1 jit_solution(3664666926381283731)
XLA Ops:
  6.5 0.0 copy-start.1
  6.5 0.0 copy-start
  6.5 0.0 all-gather.2.cloned.1.call-start
  6.5 0.7 all-gather.2.cloned.1.call-update
  7.3 0.0 reduce-scatter.2.cloned.1.call-start
  7.3 0.0 collective-permute-start
  7.3 1.7 collective-permute-start.1
  9.1 1.5 reshape.58
  10.6 0.7 compare_select_fusion
  11.3 0.1 copy.8
  11.4 0.1 reshape.40
  11.5 6.9 %reshape.35 = bf16[32,8,64,64]{3,2,1,0:T(8,128)(2,1)} reshape(bf16[32,8,4096]{2,1,0:T(8,128)(2,1)} %param.5) | data formatting | bytes 4194304 | tf_op jit(solution)/shard_map/reshape | solution.py:54
  18.4 0.0 copy-done.1
  18.4 0.1 copy.9
  18.5 0.0 copy-done
  18.5 0.1 copy.7
  18.6 0.1 reshape.48
  18.7 0.0 collective-permute-done
  18.7 0.0 collective-permute-done.1
  18.7 90.6 %all-gather.2.cloned.1.call-done = bf16[1024,4096]{1,0:T(8,128)(2,1)} async-done(((bf16[32,4096]{1,0:T(8,128)(2,1)}), bf16[1024,4096]{1,0:T(8,128)(2,1)}) %all-gather.2.cloned.1.call-update) | async-done | bytes 8388624 | tf_op jit(solution)/shard_map/all_gather | solution.py:43
  109.3 7.5 %pad_maximum_fusion = bf16[1088,4096]{1,0:T(8,128)(2,1)} fusion(bf16[32,4096]{1,0:T(8,128)(2,1)S(1)} %collective-permute-done.1, bf16[32,4096]{1,0:T(8,128)(2,1)S(1)} %collective-permute-done, bf16[1024,4096]{1,0:T(8,128)(2,1)} %all-gather.2.cloned.1.call-done), kind=kLoop, calls=%fused_computation.2 | loop fusion | flops 26738688 | bytes 17825792 | tf_op jit(solution)/shard_map/concatenate | solution.py:44
  116.8 8.6 %gather_fusion = bf16[256,4096]{1,0:T(8,128)(2,1)S(1)} fusion(bf16[1088,4096]{1,0:T(8,128)(2,1)} %pad_maximum_fusion, s32[1024]{0:T(1024)S(1)} %pad_clamp_fusion), kind=kCustom, calls=%fused_computation | custom fusion | bytes 4195328 | tf_op jit(solution)/shard_map/gather | solution.py:51
  125.3 5.5 %reshape.34 = bf16[32,8,64,64]{3,2,1,0:T(8,128)(2,1)} reshape(bf16[256,4096]{1,0:T(8,128)(2,1)S(1)} %gather_fusion) | data formatting | bytes 4194304 | tf_op jit(solution)/shard_map/reshape | solution.py:55
  130.9 7.8 %multiply_bitcast_fusion = f32[32,8,64,64]{2,3,1,0:T(8,128)} fusion(f32[32,8]{1,0:T(8,128)S(1)} %copy.9, bf16[32,8,64,64]{3,2,1,0:T(8,128)(2,1)} %reshape.34, bf16[32,8,64,64]{3,2,1,0:T(8,128)(2,1)} %reshape.35, bf16[32,64,64,1]{2,1,0,3:T(8,128)(2,1)S(1)} %reshape.58), kind=kOutput, calls=%fused_computation.3 | convolution fusion | flops 270532608 | bytes 8651776 | tf_op jit(solution)/shard_map/rba,rkbc->rkac/dot_general | solution.py:58
  138.7 9.0 %copy.10 = f32[32,8,64,64]{3,2,1,0:T(8,128)} copy(f32[32,8,64,64]{2,3,1,0:T(8,128)} %multiply_bitcast_fusion) | data formatting | bytes 8388608 | tf_op jit(solution)/shard_map/mul | solution.py:64
  147.7 7.9 %reshape.50 = f32[256,4096]{1,0:T(8,128)} reshape(f32[32,8,64,64]{3,2,1,0:T(8,128)} %copy.10) | data formatting | bytes 8388608 | tf_op jit(solution)/shard_map/reshape | solution.py:64
  155.6 9.9 %scatter_custom_fusion = f32[257,4096]{1,0:T(8,128)} fusion(s32[256]{0:T(256)S(1)} %reshape.48, f32[256,4096]{1,0:T(8,128)} %reshape.50, f32[]{:T(128)} %constant.77.clone.1), kind=kCustom, calls=%fused_computation.8 | custom fusion | flops 1048576 | bytes 4211200 | tf_op jit(solution)/shard_map/scatter-add | solution.py:71
  165.5 4.6 %slice.6 = f32[256,4096]{1,0:T(8,128)} slice(f32[257,4096]{1,0:T(8,128)} %scatter_custom_fusion), slice={[0:256], [0:4096]} | slice | bytes 8388608 | tf_op jit(solution)/shard_map/slice | solution.py:71
  170.1 0.0 reduce-scatter.2.cloned.1.call-update
  170.1 219.2 %reduce-scatter.2.cloned.1.call-done = f32[8,4096]{1,0:T(8,128)} async-done(((f32[256,4096]{1,0:T(8,128)}), f32[8,4096]{1,0:T(8,128)}) %reduce-scatter.2.cloned.1.call-update) | async-done | bytes 131088 | tf_op jit(solution)/shard_map/reduce_scatter | solution.py:72
  (3 shorter events, 0.0 us)
Async XLA Ops:
  6.5 11.8 %copy-start.1 = (s32[32]{0:T(128)S(1)}, s32[32]{0:T(128)}, u32[]{:S(2)}) copy-start(s32[32]{0:T(128)} %param.8) | copy-start | bytes 388
  6.5 11.9 %copy-start = (s32[32,8]{0,1:T(8,128)S(1)}, s32[32,8]{0,1:T(8,128)}, u32[]{:S(2)}) copy-start(s32[32,8]{0,1:T(8,128)} %param.9) | copy-start | bytes 3076
  6.5 102.8 %all-gather.2.cloned.1.call-start = ((), (), s32[]{:S(2)}) async-start(), calls=%async_computation.1 | async-start | bytes 8650752 | tf_op jit(solution)/shard_map/all_gather | solution.py:43
  7.3 382.0 %reduce-scatter.2.cloned.1.call-start = ((), (), s32[]{:S(2)}) async-start(), calls=%async_computation.2 | async-start | bytes 4325376 | tf_op jit(solution)/shard_map/reduce_scatter | solution.py:72
  7.3 11.4 %collective-permute-start = (bf16[32,4096]{1,0:T(8,128)(2,1)}, bf16[32,4096]{1,0:T(8,128)(2,1)S(1)}, u32[]{:S(2)}, u32[]{:S(2)}) collective-permute-start(bf16[32,4096]{1,0:T(8,128)(2,1)} %param.6), channel_id=1, source_target_pairs={{0,32},{32,64},{64,96},{96,128},{128,160},{160,192},{192,224},{224... | collective-permute-start | bytes 786440 | tf_op jit(solution)/shard_map/ppermute | solution.py:17
  7.3 11.3 %collective-permute-start.1 = (bf16[32,4096]{1,0:T(8,128)(2,1)}, bf16[32,4096]{1,0:T(8,128)(2,1)S(1)}, u32[]{:S(2)}, u32[]{:S(2)}) collective-permute-start(bf16[32,4096]{1,0:T(8,128)(2,1)} %param.6), channel_id=1, source_target_pairs={{32,0},{64,32},{96,64},{128,96},{160,128},{192,160},{224,192},{0,2... | collective-permute-start | bytes 786440 | tf_op jit(solution)/shard_map/ppermute | solution.py:20
Sparse Core Ops, SparseCore 0:
  9.9 99.3 all-gather.1
  170.3 218.9 reduce-scatter.1
where the time goes:
time: 398 us; the launch traced here: 396 us
  waiting for transfers between devices  311 us (78%)
  local copies, waits for them, and re-layouts  44.4 us (11%)
  other arithmetic  18.1 us (5%)
  between operations  13.5 us (3%)
  matrix products  7.84 us (2%)
    reduce_scatter x1, waiting for transfers between devices, body(): lax.psum_scatter(partial_value, 'row', scatter_dimension=0, tiled=True)  219 us
    all_gather x1, waiting for transfers between devices, body(): group_rows = lax.all_gather(p_blocks, 'row', axis=0, tiled=True)  90.6 us
    scatter-add x1, other arithmetic, body(): jax.ops.segment_sum(block_tiles, segment_index, spill_at + 1)[:spill_at]  9.9 us
    mul x1, local copies, waits for them, and re-layouts, body(): block_tiles * active_mask[:, :, None, None].astype(jnp.float32)  9 us
    gather x1, local copies, waits for them, and re-layouts, body(): picked = p_table[lookup]  8.56 us
  transfers between devices with their start and end apart: 4, of which 2 were waited for; matrix products, arithmetic and copies ran while one was open for 2% of the time, Pallas kernels for 0%

commit v1 on v0

v1 whole, which is shorter than its diff:
```python
import functools

import jax
import jax.numpy as jnp
from jax import lax
from jax.experimental import pallas as pl
from jax.experimental.pallas import tpu as pltpu
from jax.sharding import PartitionSpec as P

BS = 64
LANES = 128
PAIRS = 32
CAP = 4
SLOT_DEV = 8
CAP2 = 4
VMEM_LIMIT = 32 * 1024 * 1024


def lane_of(shape):
    return lax.broadcasted_iota(jnp.int32, shape, len(shape) - 1)


def distinct(keep, owner, local, members, width):
    lanes = lane_of((owner.shape[0], LANES))
    of_owner = jnp.where((lanes == owner) & keep, 1.0, 0.0).astype(jnp.bfloat16)
    of_local = jnp.where(lanes == local, 1.0, 0.0).astype(jnp.bfloat16)
    counts = lax.dot_general(
        of_owner, of_local, (((0,), (0,)), ((), ())), preferred_element_type=jnp.float32
    )[:members]
    present = counts > 0.5
    below = lax.broadcasted_iota(jnp.int32, (LANES, LANES), 0) < lane_of((LANES, LANES))
    rank = jnp.dot(
        jnp.where(present, 1.0, 0.0).astype(jnp.bfloat16),
        jnp.where(below, 1.0, 0.0).astype(jnp.bfloat16),
        preferred_element_type=jnp.float32,
    )
    ranks_of_owner = jnp.dot(
        of_owner[:, :members], rank.astype(jnp.bfloat16), preferred_element_type=jnp.float32
    )
    own_rank = jnp.sum(
        jnp.where(lanes == local, ranks_of_owner, 0.0), axis=1, keepdims=True
    ).astype(jnp.int32)
    return own_rank, present, rank.astype(jnp.int32)


def plan_kernel(members, groups, place_ref, cols_ref, count_ref, slot_ref, p_ref, want_ref, index_ref, pq_ref, stage):
    rows, per_row = cols_ref.shape
    group_at, member_at = place_ref[0], place_ref[1]

    def as_rows(ref):
        return jnp.concatenate([ref[:, k : k + 1] for k in range(per_row)], axis=0)

    cols, slots = as_rows(cols_ref), as_rows(slot_ref)
    live = jnp.concatenate([count_ref[...] > k for k in range(per_row)], axis=0)
    device_of = cols // rows
    local = cols % rows
    col_group = device_of // members
    col_member = device_of % members
    in_group = col_group == group_at
    own = in_group & (col_member == member_at)
    wanted = live & in_group & (col_member != member_at)
    low = col_group == lax.rem(group_at + groups - 1, groups)
    rank, present, ranks = distinct(wanted, col_member, local, members, rows)
    base = members * CAP
    source = jnp.where(
        in_group,
        jnp.where(own, base + local, col_member * CAP + jnp.clip(rank, 0, CAP - 1)),
        jnp.where(low, base + rows + local, base + 2 * rows + local),
    )
    source = jnp.where(live, source, base)

    owner = slots // SLOT_DEV % members
    slot = slots % SLOT_DEV
    slot_rank, slot_present, slot_ranks = distinct(live, owner, slot, members, SLOT_DEV)
    target = jnp.where(live, owner * CAP2 + jnp.clip(slot_rank, 0, CAP2 - 1), members * CAP2)

    lanes = lane_of((members, LANES))
    want = jnp.zeros((members, LANES), jnp.int32)
    for s in range(CAP):
        row = jnp.sum(jnp.where(present & (ranks == s), lanes, 0), axis=1, keepdims=True)
        want = jnp.where(lanes == s, row, want)
    for s in range(CAP2):
        row = jnp.sum(jnp.where(slot_present & (slot_ranks == s), lanes, 0), axis=1, keepdims=True)
        want = jnp.where(lanes == CAP + s, row, want)
    want_ref[...] = want

    lanes = lane_of((rows, LANES))
    index = jnp.zeros((rows, LANES), jnp.int32)
    for k in range(per_row):
        index = jnp.where(lanes == k, source[k * rows : (k + 1) * rows], index)
        index = jnp.where(lanes == per_row + k, target[k * rows : (k + 1) * rows], index)
    index_ref[...] = index

    left = lanes < BS
    for h in range(PAIRS // 2):
        a = p_ref[:, h * LANES : (h + 1) * LANES].astype(jnp.float32)
        b = p_ref[:, (h + PAIRS // 2) * LANES : (h + PAIRS // 2 + 1) * LANES].astype(jnp.float32)
        a_swap, b_swap = pltpu.roll(a, BS, 1), pltpu.roll(b, BS, 1)
        stage[pl.ds(2 * h * rows, rows), :] = jnp.where(left, a, b_swap)
        stage[pl.ds((2 * h + 1) * rows, rows), :] = jnp.where(left, a_swap, b)
    for j in range(rows):
        pq_ref[j] = stage[pl.ds(j, PAIRS, stride=rows), :].astype(jnp.bfloat16)


def pack_kernel(members, asked_ref, pq_ref, out_ref):
    for member in range(members):
        for s in range(CAP):
            out_ref[member * CAP + s] = pq_ref[asked_ref[member, s]]


def tiles_kernel(members, index_ref, a_ref, p_ref, got_ref, pq_ref, low_ref, high_ref, out_ref,
                 table, stage, own_stage, own, total, sem):
    rows, per_row, _ = a_ref.shape
    base = members * CAP
    copies = [
        pltpu.make_async_copy(got_ref, table.at[pl.ds(0, base)], sem.at[0]),
        pltpu.make_async_copy(pq_ref, table.at[pl.ds(base, rows)], sem.at[1]),
        pltpu.make_async_copy(low_ref, table.at[pl.ds(base + rows, rows)], sem.at[2]),
        pltpu.make_async_copy(high_ref, table.at[pl.ds(base + 2 * rows, rows)], sem.at[3]),
    ]
    for copy in copies:
        copy.start()

    row_at = lax.broadcasted_iota(jnp.int32, (LANES, LANES), 0)
    lane_at = lane_of((LANES, LANES))
    col_at = row_at % BS
    order = (row_at // BS) * BS + (col_at % 2) * (BS // 2) + col_at // 2
    shuffle = jnp.where(lane_at == order, 1.0, 0.0).astype(jnp.bfloat16)
    for r in range(PAIRS):
        own_stage[pl.ds(r * rows, rows), :] = jnp.dot(
            p_ref[:, r * LANES : (r + 1) * LANES], shuffle, preferred_element_type=jnp.float32
        )
    for j in range(rows):
        own[j] = own_stage[pl.ds(j, PAIRS, stride=rows), :].astype(jnp.bfloat16)

    def clear(at, carry):
        total[at] = jnp.zeros((PAIRS, LANES), jnp.float32)
        return carry

    lax.fori_loop(0, members * CAP2 + 1, clear, 0, unroll=8)
    for copy in copies:
        copy.wait()

    left = lane_of((PAIRS, LANES)) < BS
    zero = jnp.zeros((PAIRS, LANES), jnp.bfloat16)

    def one(i, carry):
        at = lax.rem(i, 2)
        for r in range(PAIRS):
            stage[at, pl.ds(r * per_row, per_row), :] = a_ref[i, :, r * LANES : (r + 1) * LANES].astype(jnp.float32)
        halves = []
        for k in range(per_row):
            a_pairs = stage[at, pl.ds(k, PAIRS, stride=per_row), :].astype(jnp.bfloat16)
            block = table[index_ref[i, k]]
            swap = jnp.concatenate([block[:, BS:], block[:, :BS]], axis=1)
            both = jnp.concatenate(
                [
                    jnp.where(left, block, zero),
                    jnp.where(left, swap, zero),
                    jnp.where(left, zero, swap),
                    jnp.where(left, zero, block),
                ],
                axis=0,
            )
            halves.append(jnp.dot(a_pairs, both, preferred_element_type=jnp.float32).astype(jnp.bfloat16))
        product = lax.dot_general(
            own[i], jnp.concatenate(halves, axis=1), (((0,), (0,)), ((), ())), preferred_element_type=jnp.float32
        )
        for k in range(per_row):
            part = product[:, k * LANES : (k + 1) * LANES]
            kept = jnp.where(left, part[:PAIRS], part[3 * PAIRS :])
            moved = jnp.where(left, part[PAIRS : 2 * PAIRS], part[2 * PAIRS : 3 * PAIRS])
            to = index_ref[i, per_row + k]
            total[to] += kept + pltpu.roll(moved, BS, 1)
        return carry

    lax.fori_loop(0, rows, one, 0, unroll=2)
    out_ref[...] = total[pl.ds(0, members * CAP2)].astype(jnp.bfloat16)


def sum_kernel(members, asked_ref, got_ref, out_ref, total):
    total[...] = jnp.zeros_like(total)
    for member in range(members):
        for s in range(CAP2):
            to = pl.multiple_of(asked_ref[member, CAP + s] * PAIRS, PAIRS)
            total[pl.ds(to, PAIRS), :] += got_ref[member * CAP2 + s].astype(jnp.float32)
    for r in range(PAIRS):
        out_ref[:, r * LANES : (r + 1) * LANES] = total[pl.ds(r, SLOT_DEV, stride=PAIRS), :]


def body(a_blocks, p_blocks, a_cols, a_count, tile_slot):
    rows, per_row, area = a_blocks.shape
    members = lax.axis_size("row")
    groups = lax.axis_size("grp")
    place = jnp.stack([lax.axis_index("grp"), lax.axis_index("row")]).astype(jnp.int32)
    smem = pl.BlockSpec(memory_space=pltpu.SMEM)
    vmem = pl.BlockSpec(memory_space=pltpu.VMEM)
    anywhere = pl.BlockSpec(memory_space=pl.ANY)
    params = pltpu.CompilerParams(vmem_limit_bytes=VMEM_LIMIT)
    blocks = lambda n: jax.ShapeDtypeStruct((n, PAIRS, LANES), jnp.bfloat16)

    want, index, pq = pl.pallas_call(
        functools.partial(plan_kernel, members, groups),
        out_shape=(
            jax.ShapeDtypeStruct((members, LANES), jnp.int32),
            jax.ShapeDtypeStruct((rows, LANES), jnp.int32),
            blocks(rows),
        ),
        in_specs=[smem, vmem, vmem, vmem, vmem],
        out_specs=(vmem, vmem, vmem),
        scratch_shapes=[pltpu.VMEM((PAIRS * rows, LANES), jnp.float32)],
        compiler_params=params,
        name="plan",
    )(place, a_cols, a_count.reshape(rows, 1), tile_slot, p_blocks)

    forward = [(i, (i + 1) % groups) for i in range(groups)]
    low = lax.ppermute(pq, "grp", forward)
    high = lax.ppermute(pq, "grp", [(target, source) for source, target in forward])

    asked = lax.all_to_all(want.reshape(members, 1, LANES), "row", 0, 0, tiled=True).reshape(members, LANES)
    send = pl.pallas_call(
        functools.partial(pack_kernel, members),
        out_shape=blocks(members * CAP),
        in_specs=[smem, vmem],
        out_specs=vmem,
        compiler_params=params,
        name="pack",
    )(asked, pq)
    got = lax.all_to_all(
        send.reshape(members, CAP, PAIRS, LANES), "row", 0, 0, tiled=True
    ).reshape(members * CAP, PAIRS, LANES)

    sums = pl.pallas_call(
        functools.partial(tiles_kernel, members),
        out_shape=blocks(members * CAP2),
        in_specs=[smem, vmem, vmem, anywhere, anywhere, anywhere, anywhere],
        out_specs=vmem,
        scratch_shapes=[
            pltpu.VMEM((members * CAP + 3 * rows, PAIRS, LANES), jnp.bfloat16),
            pltpu.VMEM((2, PAIRS * per_row, LANES), jnp.float32),
            pltpu.VMEM((PAIRS * rows, LANES), jnp.float32),
            pltpu.VMEM((rows, PAIRS, LANES), jnp.bfloat16),
            pltpu.VMEM((members * CAP2 + 1, PAIRS, LANES), jnp.float32),
            pltpu.SemaphoreType.DMA((4,)),
        ],
        compiler_params=params,
        name="tiles",
    )(index, a_blocks, p_blocks, got, pq, low, high)
    parts = lax.all_to_all(
        sums.reshape(members, CAP2, PAIRS, LANES), "row", 0, 0, tiled=True
    ).reshape(members * CAP2, PAIRS, LANES)

    return pl.pallas_call(
        functools.partial(sum_kernel, members),
        out_shape=jax.ShapeDtypeStruct((SLOT_DEV, area), jnp.float32),
        in_specs=[smem, vmem],
        out_specs=vmem,
        scratch_shapes=[pltpu.VMEM((SLOT_DEV * PAIRS, LANES), jnp.float32)],
        compiler_params=params,
        name="holders",
    )(asked, parts)


def solution(mesh):
    placed = (
        P(("grp", "row"), None, None),
        P(("grp", "row"), None),
        P(("grp", "row"), None),
        P(("grp", "row")),
        P(("grp", "row"), None),
    )
    return jax.shard_map(
        body, mesh=mesh, in_specs=placed, out_specs=P(("grp", "row"), None), check_vma=False
    )
```

time: 398 us -> 110 us (0.28)
  waiting for transfers between devices: 311 us -> 23.3 us
  blocking collectives: 0 us -> 51.5 us
  local copies, waits for them, and re-layouts: 44.4 us -> 8.33 us
  Pallas kernels: 0 us -> 18.8 us
  other arithmetic: 18.1 us -> 0.07 us
  between operations: 13.5 us -> 0.05 us
  matrix products: 7.84 us -> 0 us
  starting transfers between devices: 1.79 us -> 6.76 us
    reduce_scatter x1 -> x0, waiting for transfers between devices: 219 us -> none  [body(): lax.psum_scatter(partial_value, 'row', scatter_dimension=0, tiled=True)]
    all_gather x1 -> x0, waiting for transfers between devices: 90.6 us -> none  [body(): group_rows = lax.all_gather(p_blocks, 'row', axis=0, tiled=True)]
    all_to_all x0 -> x2, blocking collectives: none -> 51.5 us  [the longest x1 31.8 us: body(): lax.all_to_all(sums.reshape(members, CAP2, PAIRS, LANES), 'row', 0, 0, ti...]
    reshape x4 -> x1, local copies, waits for them, and re-layouts: 21.8 us -> 0.88 us  [body(): a_count.reshape(rows, 1)]
    all_to_all x0 -> x1, waiting for transfers between devices: none -> 19.1 us  [body(): lax.all_to_all(send.reshape(members, CAP, PAIRS, LANES), 'row', 0, 0, til...]
    pallas_call x0 -> x4, Pallas kernels: none -> 18.8 us  [the longest x1 12.9 us: body(): pl.pallas_call(functools.partial(tiles_kernel, members), out_shape=blocks...]
    scatter-add x1 -> x0, other arithmetic: 9.9 us -> none  [body(): jax.ops.segment_sum(block_tiles, segment_index, spill_at + 1)[:spill_at]]
    mul x1 -> x0, local copies, waits for them, and re-layouts: 9 us -> none  [body(): block_tiles * active_mask[:, :, None, None].astype(jnp.float32)]
  transfers between devices with their start and end apart: 4 -> 3, of which waited for: 2 -> 2; matrix products, arithmetic and copies ran while one was open for 2% -> 0% of each run, Pallas kernels for 0% -> 0%
where the time goes in v1:
time: 110 us; the launch traced here: 109 us
  blocking collectives  51.5 us (47%)
  waiting for transfers between devices  23.3 us (21%)
  Pallas kernels  18.8 us (17%)
  local copies, waits for them, and re-layouts  8.33 us (8%)
  starting transfers between devices  6.76 us (6%)
    all_to_all x1, blocking collectives, body(): lax.all_to_all(sums.reshape(members, CAP2, PAIRS, LANES), 'row', 0, 0, ti...  31.8 us
    all_to_all x1, blocking collectives, body(): lax.all_to_all(want.reshape(members, 1, LANES), 'row', 0, 0, tiled=True)  19.7 us
    all_to_all x1, waiting for transfers between devices, body(): lax.all_to_all(send.reshape(members, CAP, PAIRS, LANES), 'row', 0, 0, til...  19.1 us
    pallas_call x1, Pallas kernels, body(): pl.pallas_call(functools.partial(tiles_kernel, members), out_shape=blocks...  12.9 us
    unnamed x20, local copies, waits for them, and re-layouts  7.45 us
    all_to_all x1, starting transfers between devices, body(): lax.all_to_all(send.reshape(members, CAP, PAIRS, LANES), 'row', 0, 0, til...  5.01 us
    ppermute x1, waiting for transfers between devices, body(): low = lax.ppermute(pq, 'grp', forward)  4.26 us
  transfers between devices with their start and end apart: 3, of which 2 were waited for; matrix products, arithmetic and copies ran while one was open for 0% of the time, Pallas kernels for 0%

profile of v1, /device:TPU:38, one launch (start us, length us, event | category | flops | bytes accessed | tf_op | source)
XLA Modules:
  0.0 108.9 jit_solution(14339085913784348518)
XLA Ops:
  0.0 0.0 copy-start
  0.0 0.9 copy.10.count_ref
  0.9 0.8 copy.11.slot_ref
  1.6 0.8 copy.9.cols_ref
  2.4 0.1 pad_add_fusion.place_ref
  2.5 0.0 copy-start.1
  2.5 0.9 copy-done.1
  3.4 0.0 copy-start.2
  3.4 1.9 %plan.1 = (s32[32,128]{1,0:T(8,128)S(1)}, s32[32,128]{1,0:T(8,128)S(1)}, bf16[32,32,128]{2,1,0:T(8,128)(2,1)S(1)}) custom-call(s32[2]{0:T(128)S(1)} %pad_add_fusion.place_ref, s32[32,8]{1,0:T(8,128)S(1)} %copy.9.cols_ref, s32[32,1]{1,0:T(8,128)S(1)} %copy.10.count_ref, s32[32,8]{1,0:T(8,128)S(1)} %copy.11.slot_ref, bf16[32,4096]{1,0:T(8,128)(2,1)S(1)} %copy-done.1), custom_call_target="tpu_custom_call" | custom-call | tf_op jit(solution)/shard_map/plan/pallas_call | solution.py:202
  5.4 19.7 %all_to_all.15 = s32[32,1,128]{2,1,0:T(1,128)S(1)} all-to-all(s32[32,1,128]{2,1,0:T(1,128)S(1)} %bitcast.16), channel_id=1, replica_groups=mesh['grp'=8,'row'=32] {'row'}, dimensions={0} | all-to-all | bytes 32768 | tf_op jit(solution)/shard_map/all_to_all | solution.py:220
  25.1 1.9 %pack.1 = bf16[128,32,128]{2,1,0:T(8,128)(2,1)} custom-call(s32[32,128]{1,0:T(8,128)S(1)} %bitcast.14, bf16[32,32,128]{2,1,0:T(8,128)(2,1)S(1)} %get-tuple-element.10.pq_ref), custom_call_target="tpu_custom_call" | custom-call | tf_op jit(solution)/shard_map/pack/pallas_call | solution.py:221
  26.9 0.0 copy-start.3
  26.9 0.7 copy-done.3
  27.7 5.0 %all-to-all-start.1 = ((bf16[32,4,32,128]{3,2,1,0:T(8,128)(2,1)}), bf16[32,4,32,128]{3,2,1,0:T(8,128)(2,1)S(1)}, u32[]{:S(2)}, u32[]{:S(2)}) async-start(bf16[32,4,32,128]{3,2,1,0:T(8,128)(2,1)} %bitcast.6), calls=%async_computation.1 | async-start | bytes 2097152 | tf_op jit(solution)/shard_map/all_to_all | solution.py:229
  32.7 0.0 collective-permute-start
  32.7 1.7 %collective-permute-start.1 = (bf16[32,32,128]{2,1,0:T(8,128)(2,1)}, bf16[32,32,128]{2,1,0:T(8,128)(2,1)S(1)}, u32[]{:S(2)}, u32[]{:S(2)}) collective-permute-start(bf16[32,32,128]{2,1,0:T(8,128)(2,1)} %copy-done.3), channel_id=1, source_target_pairs={{32,0},{64,32},{96,64},{128,96},{160,128},{192,160},{224,192},{0,2... | collective-permute-start | bytes 786440 | tf_op jit(solution)/shard_map/ppermute | solution.py:218
  34.4 4.3 %collective-permute-done.low_ref = bf16[32,32,128]{2,1,0:T(8,128)(2,1)S(1)} collective-permute-done((bf16[32,32,128]{2,1,0:T(8,128)(2,1)}, bf16[32,32,128]{2,1,0:T(8,128)(2,1)S(1)}, u32[]{:S(2)}, u32[]{:S(2)}) %collective-permute-start) | collective-permute-done | bytes 262176 | tf_op jit(solution)/shard_map/ppermute | solution.py:217
  38.7 0.0 copy-start.5
  38.7 0.7 copy-done.5
  39.4 0.0 collective-permute-done.1.high_ref
  39.4 0.0 copy-start.7
  39.4 0.7 copy-done.7
  40.1 19.1 %all-to-all-done.1 = bf16[32,4,32,128]{3,2,1,0:T(8,128)(2,1)S(1)} async-done(((bf16[32,4,32,128]{3,2,1,0:T(8,128)(2,1)}), bf16[32,4,32,128]{3,2,1,0:T(8,128)(2,1)S(1)}, u32[]{:S(2)}, u32[]{:S(2)}) %all-to-all-start.1) | async-done | bytes 1048608 | tf_op jit(solution)/shard_map/all_to_all | solution.py:229
  59.2 0.0 copy-done
  59.2 0.0 copy-done.2
  59.2 0.0 copy-start.4
  59.2 0.9 copy-done.4
  60.1 0.0 copy-start.6
  60.1 0.9 copy-done.6
  61.1 0.0 copy-start.8
  61.1 0.9 copy-done.8
  62.0 12.9 %tiles.1 = bf16[128,32,128]{2,1,0:T(8,128)(2,1)S(1)} custom-call(s32[32,128]{1,0:T(8,128)S(1)} %get-tuple-element.9.index_ref, bf16[32,8,4096]{2,1,0:T(8,128)(2,1)S(1)} %copy-done, bf16[32,4096]{1,0:T(8,128)(2,1)S(1)} %copy-done.2, bf16[128,32,128]{2,1,0:T(8,128)(2,1)S(1)} %bitcast.11, bf16[32,32,128]{2,1,0:T(8,128)(2,1)S(1)} %copy-done.4, ...), custom_call_target="tpu_custom_call" | custom-call | tf_op jit(solution)/shard_map/tiles/pallas_call | solution.py:233
  75.0 31.8 %all_to_all.16 = bf16[32,4,32,128]{3,2,1,0:T(8,128)(2,1)S(1)} all-to-all(bf16[32,4,32,128]{3,2,1,0:T(8,128)(2,1)S(1)} %bitcast.12), channel_id=1, replica_groups=mesh['grp'=8,'row'=32] {'row'}, dimensions={0} | all-to-all | bytes 2097152 | tf_op jit(solution)/shard_map/all_to_all | solution.py:249
  106.8 2.1 %holders.1 = f32[8,4096]{1,0:T(8,128)} custom-call(s32[32,128]{1,0:T(8,128)S(1)} %bitcast.15, bf16[128,32,128]{2,1,0:T(8,128)(2,1)S(1)} %bitcast.13), custom_call_target="tpu_custom_call" | custom-call | tf_op jit(solution)/shard_map/holders/pallas_call | solution.py:253
Async XLA Ops:
  0.0 59.2 %copy-start = (bf16[32,8,4096]{2,1,0:T(8,128)(2,1)S(1)}, bf16[32,8,4096]{2,1,0:T(8,128)(2,1)}, u32[]{:S(2)}) copy-start(bf16[32,8,4096]{2,1,0:T(8,128)(2,1)} %a_ref.1) | copy-start | bytes 6291460
  2.5 0.9 copy-start.1
  3.4 55.7 %copy-start.2 = (bf16[32,4096]{1,0:T(8,128)(2,1)S(1)}, bf16[32,4096]{1,0:T(8,128)(2,1)}, u32[]{:S(2)}) copy-start(bf16[32,4096]{1,0:T(8,128)(2,1)} %p_ref.3) | copy-start | bytes 786436
  26.9 0.7 copy-start.3
  27.7 31.5 %all-to-all-start.1 = ((bf16[32,4,32,128]{3,2,1,0:T(8,128)(2,1)}), bf16[32,4,32,128]{3,2,1,0:T(8,128)(2,1)S(1)}, u32[]{:S(2)}, u32[]{:S(2)}) async-start(bf16[32,4,32,128]{3,2,1,0:T(8,128)(2,1)} %bitcast.6), calls=%async_computation.1 | async-start | bytes 2097152 | tf_op jit(solution)/shard_map/all_to_all | solution.py:229
  32.7 6.0 %collective-permute-start = (bf16[32,32,128]{2,1,0:T(8,128)(2,1)}, bf16[32,32,128]{2,1,0:T(8,128)(2,1)S(1)}, u32[]{:S(2)}, u32[]{:S(2)}) collective-permute-start(bf16[32,32,128]{2,1,0:T(8,128)(2,1)} %copy-done.3), channel_id=1, source_target_pairs={{0,32},{32,64},{64,96},{96,128},{128,160},{160,192},{192,224},{224... | collective-permute-start | bytes 786440 | tf_op jit(solution)/shard_map/ppermute | solution.py:217
  32.7 6.7 %collective-permute-start.1 = (bf16[32,32,128]{2,1,0:T(8,128)(2,1)}, bf16[32,32,128]{2,1,0:T(8,128)(2,1)S(1)}, u32[]{:S(2)}, u32[]{:S(2)}) collective-permute-start(bf16[32,32,128]{2,1,0:T(8,128)(2,1)} %copy-done.3), channel_id=1, source_target_pairs={{32,0},{64,32},{96,64},{128,96},{160,128},{192,160},{224,192},{0,2... | collective-permute-start | bytes 786440 | tf_op jit(solution)/shard_map/ppermute | solution.py:218
  38.7 0.7 copy-start.5
  39.4 0.7 copy-start.7
  59.2 1.0 copy-start.4
  60.1 0.9 copy-start.6
  61.1 0.9 copy-start.8

commit v2 on v0

v2 whole, which is shorter than its diff:
```python
import functools

import jax
import jax.numpy as jnp
from jax import lax
from jax.experimental import pallas as pl
from jax.experimental.pallas import tpu as pltpu
from jax.sharding import PartitionSpec as P

BS = 64
LANES = 128
PAIRS = 32
CAP = 4
SLOT_DEV = 8
CAP2 = 4
GROUP = 16
VMEM_LIMIT = 12 * 1024 * 1024
WIDE_LIMIT = 40 * 1024 * 1024
SPARE = 1664
BF16 = jnp.bfloat16
F32 = jnp.float32


def lane_of(shape):
    return lax.broadcasted_iota(jnp.int32, shape, len(shape) - 1)


def row_of(shape):
    return lax.broadcasted_iota(jnp.int32, shape, len(shape) - 2)


def ones(mask):
    return jnp.where(mask, 1.0, 0.0).astype(BF16)


def dot(a, b, contract):
    return lax.dot_general(a, b, ((contract[:1], contract[1:]), ((), ())), preferred_element_type=F32)


def table_of(owner, local, keep, members, width):
    per_row, rows = owner.shape
    counts = jnp.zeros((members, width), F32)
    for k in range(per_row):
        of_owner = ones((row_of((members, rows)) == owner[k : k + 1]) & keep[k : k + 1])
        of_local = ones(row_of((width, rows)) == local[k : k + 1])
        counts += dot(of_owner, of_local, (1, 1))
    present = counts > 0.5
    before = ones(row_of((width, width)) < lane_of((width, width)))
    return present, dot(ones(present), before, (1, 0))


def rank_of(owner, local, rank):
    per_row, rows = owner.shape
    members, width = rank.shape
    result = jnp.zeros((per_row, rows), jnp.int32)
    for k in range(per_row):
        of_owner = ones(row_of((members, rows)) == owner[k : k + 1])
        ranks = dot(rank.astype(BF16), of_owner, (0, 0))
        mine = jnp.sum(jnp.where(row_of((width, rows)) == local[k : k + 1], ranks, 0.0), axis=0, keepdims=True)
        result = jnp.where(row_of((per_row, rows)) == k, mine.astype(jnp.int32), result)
    return result


def chosen(present, rank, cap, first, result):
    members, width = present.shape
    ids, lanes = lane_of((members, width)), lane_of((members, LANES))
    for s in range(cap):
        one = jnp.sum(jnp.where(present & (rank == float(s)), ids, 0), axis=1, keepdims=True)
        result = jnp.where(lanes == first + s, one, result)
    return result


def split_cols(cols, rows, members):
    device_of = cols // rows
    return cols % rows, device_of // members, device_of % members


def read_entries(entry_ref):
    per_row, rows = SLOT_DEV, entry_ref.shape[1]
    cols, slots, count = (entry_ref[n * per_row : (n + 1) * per_row, :] for n in range(3))
    return cols, slots, row_of((per_row, rows)) < count, per_row, rows


def plan_kernel(members, place_ref, entry_ref, want_ref):
    cols, slots, live, per_row, rows = read_entries(entry_ref)
    local, group, member = split_cols(cols, rows, members)
    wanted = live & (group == place_ref[0]) & (member != place_ref[1])
    present, rank = table_of(member, local, wanted, members, rows)
    want = chosen(present, rank, CAP, 0, jnp.zeros((members, LANES), jnp.int32))
    present, rank = table_of(slots // SLOT_DEV % members, slots % SLOT_DEV, live, members, SLOT_DEV)
    want_ref[...] = chosen(present, rank, CAP2, CAP, want)


def lists_kernel(members, groups, place_ref, entry_ref, lists_ref):
    cols, slots, live, per_row, rows = read_entries(entry_ref)
    entries = per_row * rows
    local, group, member = split_cols(cols, rows, members)
    at_k = row_of((per_row, rows))
    in_group = group == place_ref[0]
    far = in_group & (member != place_ref[1])
    _, rank = table_of(member, local, live & far, members, rows)
    far_source = member * CAP + jnp.clip(rank_of(member, local, rank), 0, CAP - 1)
    low = group == lax.rem(place_ref[0] + groups - 1, groups)
    near_source = jnp.where(in_group, local, jnp.where(low, rows + local, 2 * rows + local))
    source = jnp.where(far, far_source, near_source)

    owner, slot = slots // SLOT_DEV % members, slots % SLOT_DEV
    _, rank = table_of(owner, slot, live, members, SLOT_DEV)
    target = owner * CAP2 + jnp.clip(rank_of(owner, slot, rank), 0, CAP2 - 1)

    entry = lane_of((per_row, rows)) * per_row + at_k
    before = ones(row_of((rows, rows)) < lane_of((rows, rows)))
    above = ones(lane_of((per_row, per_row)) < row_of((per_row, per_row)))
    result = jnp.zeros((SLOT_DEV, entries), jnp.int32)
    for which, mask in enumerate((live & ~far, live & far)):
        inside = dot(ones(mask), before, (1, 0))
        totals = jnp.sum(jnp.where(mask, 1.0, 0.0), axis=1, keepdims=True)
        earlier = dot(above, jnp.broadcast_to(totals, (per_row, LANES)).astype(BF16), (1, 0))[:, :1]
        at = jnp.where(mask, (inside + earlier).astype(jnp.int32), -1)
        count = jnp.sum(totals, axis=0, keepdims=True).astype(jnp.int32)
        placed = jnp.zeros((SLOT_DEV, entries), F32)
        for k in range(per_row):
            here = ones(row_of((entries, rows)) == at[k : k + 1])
            kind = row_of((SLOT_DEV, rows))
            value = jnp.where(kind == 0, entry[k : k + 1], jnp.where(kind == 1, source[k : k + 1], target[k : k + 1]))
            placed += dot(value.astype(F32).astype(BF16), here, (1, 1))
        placed = placed.astype(jnp.int32)
        code = placed[:1] * 65536 + placed[1:2] * 256 + placed[2:3]
        lanes = lane_of((1, entries))
        code = jnp.where(lanes < count, code, members * CAP2)
        kind = row_of((SLOT_DEV, entries))
        result = jnp.where(kind == which, code, result)
        result = jnp.where(kind == 2 + which, count, result)
    lists_ref[...] = result


def prepare_kernel(p_ref, pq_ref, stage):
    rows = p_ref.shape[0]
    left = lane_of((rows, LANES)) < BS
    for h in range(PAIRS // 2):
        a = p_ref[:, h * LANES : (h + 1) * LANES].astype(F32)
        b = p_ref[:, (h + PAIRS // 2) * LANES : (h + PAIRS // 2 + 1) * LANES].astype(F32)
        stage[pl.ds(2 * h * rows, rows), :] = jnp.where(left, a, pltpu.roll(b, BS, 1))
        stage[pl.ds((2 * h + 1) * rows, rows), :] = jnp.where(left, pltpu.roll(a, BS, 1), b)
    for j in range(rows):
        pq_ref[j] = stage[pl.ds(j, PAIRS, stride=rows), :].astype(BF16)


def relay(a_ref, p_ref, pairs_ref, own_ref, stage, own_stage):
    rows, per_row, _ = a_ref.shape
    row_at, lane_at = row_of((LANES, LANES)), lane_of((LANES, LANES))
    col_at = row_at % BS
    order = (col_at % 2) * BS + (row_at // BS) * (BS // 2) + col_at // 2
    shuffle = ones(lane_at == order)
    for r in range(PAIRS):
        own_stage[pl.ds(r * rows, rows), :] = jnp.dot(
            p_ref[:, r * LANES : (r + 1) * LANES], shuffle, preferred_element_type=F32
        )
    at_once = LANES // PAIRS
    for first in range(0, rows, at_once):
        turned = jnp.concatenate(
            [own_stage[pl.ds(first + j, PAIRS, stride=rows), :] for j in range(at_once)], axis=0
        ).T
        for j in range(at_once):
            mine = turned[:, j * PAIRS : (j + 1) * PAIRS]
            own_ref[first + j] = jnp.concatenate(
                [mine[n * PAIRS : (n + 1) * PAIRS] for n in range(at_once)], axis=1
            ).astype(BF16)

    def one(i, carry):
        at = lax.rem(i, 2)
        for r in range(PAIRS):
            stage[at, pl.ds(r * per_row, per_row), :] = a_ref[i, :, r * LANES : (r + 1) * LANES].astype(F32)
        for k in range(per_row):
            pairs_ref[i * per_row + k] = stage[at, pl.ds(k, PAIRS, stride=per_row), :].astype(BF16)
        return carry

    lax.fori_loop(0, rows, one, 0, unroll=2)


def twice(block):
    left, zero = lane_of(block.shape) < BS, jnp.zeros(block.shape, block.dtype)
    swap = jnp.concatenate([block[:, BS:], block[:, :BS]], axis=1)
    parts = [
        jnp.where(left, block, zero),
        jnp.where(left, swap, zero),
        jnp.where(left, zero, swap),
        jnp.where(left, zero, block),
    ]
    return jnp.concatenate(parts, axis=0)


def add_tiles(lists_ref, which, group, per_row, table_ref, pairs_ref, own_ref, total_ref):
    def one(step, carry):
        codes = [lists_ref[which, step * group + n] for n in range(group)]
        rights = [twice(table_ref[(code >> 8) & 255]) for code in codes]
        halves = [
            jnp.dot(pairs_ref[code >> 16], right, preferred_element_type=F32).astype(BF16)
            for code, right in zip(codes, rights)
        ]
        rights = [twice(half) for half in halves]
        tiles = [
            jnp.dot(own_ref[(code >> 16) // per_row], right, preferred_element_type=F32)
            for code, right in zip(codes, rights)
        ]
        for code, tile in zip(codes, tiles):
            total_ref[code & 255] += tile
        return carry

    lax.fori_loop(0, (lists_ref[2 + which, 0] + group - 1) // group, one, 0)


def views(work_ref, entries, per_row):
    return work_ref.at[pl.ds(0, entries)], work_ref.at[pl.ds(entries, entries // per_row)]


def clear(total_ref):
    def one(at, carry):
        total_ref[at] = jnp.zeros((PAIRS, LANES), F32)
        return carry

    lax.fori_loop(0, total_ref.shape[0], one, 0, unroll=8)


def near_kernel(per_row, lists_ref, a_ref, p_ref, pq_ref, low_ref, high_ref, work_ref, near_ref,
                table, stage, own_stage, total_ref, sem):
    pairs_ref, own_ref = views(work_ref, lists_ref.shape[1], per_row)
    relay(a_ref, p_ref, pairs_ref, own_ref, stage, own_stage)
    rows = pq_ref.shape[0]
    for at, ref in enumerate((pq_ref, low_ref, high_ref)):
        table[pl.ds(at * rows, rows)] = ref[...]
    clear(total_ref)
    add_tiles(lists_ref, 0, GROUP, per_row, table, pairs_ref, own_ref, total_ref)
    sums = total_ref.shape[0] - 1
    copy = pltpu.make_async_copy(total_ref.at[pl.ds(0, sums)], near_ref.at[pl.ds(0, sums)], sem)
    copy.start()
    copy.wait()


def far_kernel(per_row, lists_ref, work_ref, got_ref, near_ref, out_ref, total, near, sem):
    copy = pltpu.make_async_copy(near_ref.at[pl.ds(0, near.shape[0])], near, sem)
    copy.start()
    pairs_ref, own_ref = views(work_ref, lists_ref.shape[1], per_row)
    clear(total)
    add_tiles(lists_ref, 1, GROUP, per_row, got_ref, pairs_ref, own_ref, total)
    copy.wait()

    def one(at, carry):
        out_ref[at] = (total[at] + near[at]).astype(BF16)
        return carry

    lax.fori_loop(0, out_ref.shape[0], one, 0, unroll=8)


def pack_kernel(members, asked_ref, pq_ref, out_ref):
    for member in range(members):
        for s in range(CAP):
            out_ref[member * CAP + s] = pq_ref[asked_ref[member, s]]


def sum_kernel(members, asked_ref, got_ref, out_ref, *totals):
    for total in totals:
        total[...] = jnp.zeros_like(total)
    for member in range(members):
        for s, total in enumerate(totals):
            to = pl.multiple_of(asked_ref[member, CAP + s] * PAIRS, PAIRS)
            total[pl.ds(to, PAIRS), :] += got_ref[member * CAP2 + s].astype(F32)
    for r in range(PAIRS):
        out_ref[:, r * LANES : (r + 1) * LANES] = sum(
            total[pl.ds(r, SLOT_DEV, stride=PAIRS), :] for total in totals
        )


def body(a_blocks, p_blocks, a_cols, a_count, tile_slot):
    rows, per_row, area = a_blocks.shape
    members = lax.axis_size("row")
    groups = lax.axis_size("grp")
    entries = rows * per_row
    place = jnp.stack([lax.axis_index("grp"), lax.axis_index("row")]).astype(jnp.int32)
    smem = pl.BlockSpec(memory_space=pltpu.SMEM)
    vmem = pl.BlockSpec(memory_space=pltpu.VMEM)
    hbm = pl.BlockSpec(memory_space=pltpu.HBM)
    blocks = lambda n, dtype=BF16: jax.ShapeDtypeStruct((n, PAIRS, LANES), dtype)
    ints = lambda *shape: jax.ShapeDtypeStruct(shape, jnp.int32)

    def call(kernel, name, ins, outs, scratch, us, out_specs=vmem, limit=VMEM_LIMIT):
        return pl.pallas_call(
            kernel,
            out_shape=outs,
            in_specs=ins,
            out_specs=out_specs,
            scratch_shapes=scratch,
            compiler_params=pltpu.CompilerParams(vmem_limit_bytes=limit),
            cost_estimate=pl.CostEstimate(flops=0, bytes_accessed=int(us * 3e6), transcendentals=0),
            name=name,
        )

    entry = jnp.concatenate(
        [a_cols.T, tile_slot.T, jnp.broadcast_to(a_count[None], (per_row, rows))], axis=0
    )
    want = call(
        functools.partial(plan_kernel, members), "plan", [smem, vmem], ints(members, LANES), [], 2
    )(place, entry)
    asked = lax.all_to_all(want.reshape(members, 1, LANES), "row", 0, 0, tiled=True).reshape(members, LANES)

    pq = call(
        prepare_kernel, "prepare", [vmem], blocks(rows), [pltpu.VMEM((PAIRS * rows, LANES), F32)], 0.1
    )(p_blocks)
    forward = [(i, (i + 1) % groups) for i in range(groups)]
    low = lax.ppermute(pq, "grp", forward)
    high = lax.ppermute(pq, "grp", [(target, source) for source, target in forward])

    send = call(
        functools.partial(pack_kernel, members), "pack", [smem, vmem], blocks(members * CAP), [], 2
    )(asked, pq)
    got = lax.all_to_all(
        send.reshape(members, CAP, PAIRS, LANES), "row", 0, 0, tiled=True
    ).reshape(members * CAP, PAIRS, LANES)

    lists = call(
        functools.partial(lists_kernel, members, groups),
        "lists",
        [smem, vmem],
        ints(SLOT_DEV, entries),
        [],
        0.1,
    )(place, entry)
    work, near = call(
        functools.partial(near_kernel, per_row),
        "near",
        [smem, vmem, vmem, vmem, vmem, vmem],
        (blocks(entries + rows), blocks(SPARE, F32)),
        [
            pltpu.VMEM((3 * rows, PAIRS, LANES), BF16),
            pltpu.VMEM((2, PAIRS * per_row, LANES), F32),
            pltpu.VMEM((PAIRS * rows, LANES), F32),
            pltpu.VMEM((members * CAP2 + 1, PAIRS, LANES), F32),
            pltpu.SemaphoreType.DMA,
        ],
        0.1,
        (vmem, hbm),
        WIDE_LIMIT,
    )(lists, a_blocks, p_blocks, pq, low, high)
    sums = call(
        functools.partial(far_kernel, per_row),
        "far",
        [smem, vmem, vmem, hbm],
        blocks(members * CAP2),
        [
            pltpu.VMEM((members * CAP2 + 1, PAIRS, LANES), F32),
            pltpu.VMEM((members * CAP2, PAIRS, LANES), F32),
            pltpu.SemaphoreType.DMA,
        ],
        6,
        limit=WIDE_LIMIT,
    )(lists, work, got, near)
    parts = lax.all_to_all(
        sums.reshape(members, CAP2, PAIRS, LANES), "row", 0, 0, tiled=True
    ).reshape(members * CAP2, PAIRS, LANES)

    return call(
        functools.partial(sum_kernel, members),
        "holders",
        [smem, vmem],
        jax.ShapeDtypeStruct((SLOT_DEV, area), F32),
        [pltpu.VMEM((SLOT_DEV * PAIRS, LANES), F32)] * CAP2,
        2,
    )(asked, parts)


def solution(mesh):
    placed = (
        P(("grp", "row"), None, None),
        P(("grp", "row"), None),
        P(("grp", "row"), None),
        P(("grp", "row")),
        P(("grp", "row"), None),
    )
    return jax.shard_map(
        body, mesh=mesh, in_specs=placed, out_specs=P(("grp", "row"), None), check_vma=False
    )
```

time: 398 us -> 96.3 us (0.24)
  waiting for transfers between devices: 311 us -> 20.2 us
  local copies, waits for them, and re-layouts: 44.4 us -> 5.1 us
  blocking collectives: 0 us -> 31.8 us
  Pallas kernels: 0 us -> 20.2 us
  other arithmetic: 18.1 us -> 0.78 us
  starting transfers between devices: 1.79 us -> 16.9 us
  between operations: 13.5 us -> 0.08 us
  matrix products: 7.84 us -> 0 us
    reduce_scatter x1 -> x0, waiting for transfers between devices: 219 us -> none  [body(): lax.psum_scatter(partial_value, 'row', scatter_dimension=0, tiled=True)]
    all_gather x1 -> x0, waiting for transfers between devices: 90.6 us -> none  [body(): group_rows = lax.all_gather(p_blocks, 'row', axis=0, tiled=True)]
    all_to_all x0 -> x1, blocking collectives: none -> 31.8 us  [body(): lax.all_to_all(sums.reshape(members, CAP2, PAIRS, LANES), 'row', 0, 0, ti...]
    reshape x4 -> x0, local copies, waits for them, and re-layouts: 21.8 us -> none  [the longest x1 7.9 us: body(): (block_tiles * active_mask[:, :, None, None].astype(jnp.float32)).reshape...]
    pallas_call x0 -> x7, Pallas kernels: none -> 20.2 us  [the longest x1 7.44 us: body(): call(functools.partial(near_kernel, per_row), 'near', [smem, vmem, vmem,...]
    all_to_all x0 -> x2, waiting for transfers between devices: none -> 16.8 us  [the longest x1 9.72 us: body(): lax.all_to_all(send.reshape(members, CAP, PAIRS, LANES), 'row', 0, 0, til...]
    all_to_all x0 -> x2, starting transfers between devices: none -> 16.4 us  [the longest x1 11.4 us: body(): lax.all_to_all(want.reshape(members, 1, LANES), 'row', 0, 0, tiled=True)]
    scatter-add x1 -> x0, other arithmetic: 9.9 us -> none  [body(): jax.ops.segment_sum(block_tiles, segment_index, spill_at + 1)[:spill_at]]
  transfers between devices with their start and end apart: 4 -> 4, of which waited for: 2 -> 4; matrix products, arithmetic and copies ran while one was open for 2% -> 0% of each run, Pallas kernels for 0% -> 10%
where the time goes in v2:
time: 96.3 us; the launch traced here: 95 us
  blocking collectives  31.8 us (33%)
  Pallas kernels  20.2 us (21%)
  waiting for transfers between devices  20.2 us (21%)
  starting transfers between devices  16.9 us (18%)
  local copies, waits for them, and re-layouts  5.1 us (5%)
    all_to_all x1, blocking collectives, body(): lax.all_to_all(sums.reshape(members, CAP2, PAIRS, LANES), 'row', 0, 0, ti...  31.8 us
    all_to_all x1, starting transfers between devices, body(): lax.all_to_all(want.reshape(members, 1, LANES), 'row', 0, 0, tiled=True)  11.4 us
    all_to_all x1, waiting for transfers between devices, body(): lax.all_to_all(send.reshape(members, CAP, PAIRS, LANES), 'row', 0, 0, til...  9.72 us
    pallas_call x1, Pallas kernels, body(): call(functools.partial(near_kernel, per_row), 'near', [smem, vmem, vmem,...  7.44 us
    all_to_all x1, waiting for transfers between devices, body(): lax.all_to_all(want.reshape(members, 1, LANES), 'row', 0, 0, tiled=True)  7.05 us
    all_to_all x1, starting transfers between devices, body(): lax.all_to_all(send.reshape(members, CAP, PAIRS, LANES), 'row', 0, 0, til...  5.01 us
    pallas_call x1, Pallas kernels, body(): call(functools.partial(far_kernel, per_row), 'far', [smem, vmem, vmem, hb...  4.74 us
    unnamed x10, local copies, waits for them, and re-layouts  4.44 us
  transfers between devices with their start and end apart: 4, of which 4 were waited for; matrix products, arithmetic and copies ran while one was open for 0% of the time, Pallas kernels for 10%

profile of v2, /device:TPU:38, one launch (start us, length us, event | category | flops | bytes accessed | tf_op | source)
XLA Modules:
  0.0 95.0 jit_solution(1435209013790234548)
XLA Ops:
  0.0 0.1 pad_add_fusion.1.place_ref
  0.1 0.7 broadcast_in_dim.2
  0.7 0.7 pad_add_fusion.entry_ref
  1.4 1.7 %plan.1 = s32[32,128]{1,0:T(8,128)} custom-call(s32[2]{0:T(128)S(1)} %pad_add_fusion.1.place_ref, s32[24,32]{1,0:T(8,128)S(1)} %pad_add_fusion.entry_ref), custom_call_target="tpu_custom_call" | custom-call | bytes 6000000 | tf_op jit(solution)/shard_map/plan/pallas_call | solution.py:301
  3.2 11.4 %all-to-all-start = ((s32[32,1,128]{2,1,0:T(1,128)}), s32[32,1,128]{2,1,0:T(1,128)S(1)}, u32[]{:S(2)}, u32[]{:S(2)}) async-start(s32[32,1,128]{2,1,0:T(1,128)} %bitcast.5), calls=%async_computation | async-start | bytes 32768 | tf_op jit(solution)/shard_map/all_to_all | solution.py:304
  14.5 0.0 copy-start.3
  14.5 0.9 copy-done.3
  15.5 0.5 prepare.1.pq_ref
  16.0 0.0 copy-start
  16.0 7.0 %all-to-all-done = s32[32,1,128]{2,1,0:T(1,128)S(1)} async-done(((s32[32,1,128]{2,1,0:T(1,128)}), s32[32,1,128]{2,1,0:T(1,128)S(1)}, u32[]{:S(2)}, u32[]{:S(2)}) %all-to-all-start) | async-done | bytes 16416 | tf_op jit(solution)/shard_map/all_to_all | solution.py:304
  23.0 1.9 %pack.1 = bf16[128,32,128]{2,1,0:T(8,128)(2,1)} custom-call(s32[32,128]{1,0:T(8,128)S(1)} %bitcast.15, bf16[32,32,128]{2,1,0:T(8,128)(2,1)S(1)} %prepare.1.pq_ref), custom_call_target="tpu_custom_call" | custom-call | bytes 6000000 | tf_op jit(solution)/shard_map/pack/pallas_call | solution.py:313
  24.9 5.0 %all-to-all-start.1 = ((bf16[32,4,32,128]{3,2,1,0:T(8,128)(2,1)}), bf16[32,4,32,128]{3,2,1,0:T(8,128)(2,1)S(1)}, u32[]{:S(2)}, u32[]{:S(2)}) async-start(bf16[32,4,32,128]{3,2,1,0:T(8,128)(2,1)} %bitcast.7), calls=%async_computation.1 | async-start | bytes 2097152 | tf_op jit(solution)/shard_map/all_to_all | solution.py:316
  29.9 0.0 collective-permute-start.1
  29.9 0.5 collective-permute-start
  30.4 1.9 %lists.1.lists_ref = s32[8,256]{1,0:T(8,128)S(1)} custom-call(s32[2]{0:T(128)S(1)} %pad_add_fusion.1.place_ref, s32[24,32]{1,0:T(8,128)S(1)} %pad_add_fusion.entry_ref), custom_call_target="tpu_custom_call" | custom-call | bytes 300000 | tf_op jit(solution)/shard_map/lists/pallas_call | solution.py:320
  32.3 1.5 %collective-permute-done.1.high_ref = bf16[32,32,128]{2,1,0:T(8,128)(2,1)S(1)} collective-permute-done((bf16[32,32,128]{2,1,0:T(8,128)(2,1)S(1)}, bf16[32,32,128]{2,1,0:T(8,128)(2,1)S(1)}, u32[]{:S(2)}, u32[]{:S(2)}) %collective-permute-start.1) | collective-permute-done | bytes 262176 | tf_op jit(solution)/shard_map/ppermute | solution.py:311
  33.8 0.0 copy-done
  33.8 1.9 %collective-permute-done.low_ref = bf16[32,32,128]{2,1,0:T(8,128)(2,1)S(1)} collective-permute-done((bf16[32,32,128]{2,1,0:T(8,128)(2,1)S(1)}, bf16[32,32,128]{2,1,0:T(8,128)(2,1)S(1)}, u32[]{:S(2)}, u32[]{:S(2)}) %collective-permute-start) | collective-permute-done | bytes 262176 | tf_op jit(solution)/shard_map/ppermute | solution.py:310
  35.8 0.0 copy-start.1
  35.8 0.9 copy-done.1
  36.7 0.0 copy-start.2
  36.7 1.6 %copy-done.2 = bf16[32,8,4096]{2,1,0:T(8,128)(2,1)S(1)} copy-done((bf16[32,8,4096]{2,1,0:T(8,128)(2,1)S(1)}, bf16[32,8,4096]{2,1,0:T(8,128)(2,1)}, u32[]{:S(2)}) %copy-start.2) | copy-done | bytes 2097176
  38.3 0.0 copy-start.4
  38.3 0.9 copy-done.4
  39.2 7.4 %near.1 = (bf16[288,32,128]{2,1,0:T(8,128)(2,1)S(1)}, f32[1664,32,128]{2,1,0:T(8,128)}) custom-call(s32[8,256]{1,0:T(8,128)S(1)} %lists.1.lists_ref, bf16[32,8,4096]{2,1,0:T(8,128)(2,1)S(1)} %copy-done.2, bf16[32,4096]{1,0:T(8,128)(2,1)S(1)} %copy-done.4, bf16[32,32,128]{2,1,0:T(8,128)(2,1)S(1)} %copy-done.1, ...), custom_call_target="tpu_custom_call" | custom-call | bytes 300000 | tf_op jit(solution)/shard_map/near/pallas_call | solution.py:328
  46.7 9.7 %all-to-all-done.1 = bf16[32,4,32,128]{3,2,1,0:T(8,128)(2,1)S(1)} async-done(((bf16[32,4,32,128]{3,2,1,0:T(8,128)(2,1)}), bf16[32,4,32,128]{3,2,1,0:T(8,128)(2,1)S(1)}, u32[]{:S(2)}, u32[]{:S(2)}) %all-to-all-start.1) | async-done | bytes 1048608 | tf_op jit(solution)/shard_map/all_to_all | solution.py:316
  56.4 4.7 %far.1 = bf16[128,32,128]{2,1,0:T(8,128)(2,1)S(1)} custom-call(s32[8,256]{1,0:T(8,128)S(1)} %lists.1.lists_ref, bf16[288,32,128]{2,1,0:T(8,128)(2,1)S(1)} %get-tuple-element.7.work_ref, bf16[128,32,128]{2,1,0:T(8,128)(2,1)S(1)} %bitcast.12, f32[1664,32,128]{2,1,0:T(8,128)} %get-tuple-element.8.near_ref), custom_call_target="tpu_custom_call" | custom-call | bytes 18000000 | tf_op jit(solution)/shard_map/far/pallas_call | solution.py:344
  61.2 31.8 %all_to_all.15 = bf16[32,4,32,128]{3,2,1,0:T(8,128)(2,1)S(1)} all-to-all(bf16[32,4,32,128]{3,2,1,0:T(8,128)(2,1)S(1)} %bitcast.13), channel_id=1, replica_groups=mesh['grp'=8,'row'=32] {'row'}, dimensions={0} | all-to-all | bytes 2097152 | tf_op jit(solution)/shard_map/all_to_all | solution.py:357
  93.0 2.0 %holders.1 = f32[8,4096]{1,0:T(8,128)} custom-call(s32[32,128]{1,0:T(8,128)S(1)} %bitcast.16, bf16[128,32,128]{2,1,0:T(8,128)(2,1)S(1)} %bitcast.14), custom_call_target="tpu_custom_call" | custom-call | bytes 6000000 | tf_op jit(solution)/shard_map/holders/pallas_call | solution.py:361
Async XLA Ops:
  3.2 19.8 %all-to-all-start = ((s32[32,1,128]{2,1,0:T(1,128)}), s32[32,1,128]{2,1,0:T(1,128)S(1)}, u32[]{:S(2)}, u32[]{:S(2)}) async-start(s32[32,1,128]{2,1,0:T(1,128)} %bitcast.5), calls=%async_computation | async-start | bytes 32768 | tf_op jit(solution)/shard_map/all_to_all | solution.py:304
  14.5 1.0 %copy-start.3 = (bf16[32,4096]{1,0:T(8,128)(2,1)S(1)}, bf16[32,4096]{1,0:T(8,128)(2,1)}, u32[]{:S(2)}) copy-start(bf16[32,4096]{1,0:T(8,128)(2,1)} %p_ref.3) | copy-start | bytes 786436
  16.0 17.9 %copy-start = (bf16[32,32,128]{2,1,0:T(8,128)(2,1)}, bf16[32,32,128]{2,1,0:T(8,128)(2,1)S(1)}, u32[]{:S(2)}) copy-start(bf16[32,32,128]{2,1,0:T(8,128)(2,1)S(1)} %prepare.1.pq_ref) | copy-start | bytes 786436
  24.9 31.5 %all-to-all-start.1 = ((bf16[32,4,32,128]{3,2,1,0:T(8,128)(2,1)}), bf16[32,4,32,128]{3,2,1,0:T(8,128)(2,1)S(1)}, u32[]{:S(2)}, u32[]{:S(2)}) async-start(bf16[32,4,32,128]{3,2,1,0:T(8,128)(2,1)} %bitcast.7), calls=%async_computation.1 | async-start | bytes 2097152 | tf_op jit(solution)/shard_map/all_to_all | solution.py:316
  29.9 3.9 %collective-permute-start.1 = (bf16[32,32,128]{2,1,0:T(8,128)(2,1)S(1)}, bf16[32,32,128]{2,1,0:T(8,128)(2,1)S(1)}, u32[]{:S(2)}, u32[]{:S(2)}) collective-permute-start(bf16[32,32,128]{2,1,0:T(8,128)(2,1)S(1)} %prepare.1.pq_ref), channel_id=1, source_target_pairs={{32,0},{64,32},{96,64},{128,96},{160,128},{192,160},{224,192},{0,2... | collective-permute-start | bytes 786440 | tf_op jit(solution)/shard_map/ppermute | solution.py:311
  29.9 5.8 %collective-permute-start = (bf16[32,32,128]{2,1,0:T(8,128)(2,1)S(1)}, bf16[32,32,128]{2,1,0:T(8,128)(2,1)S(1)}, u32[]{:S(2)}, u32[]{:S(2)}) collective-permute-start(bf16[32,32,128]{2,1,0:T(8,128)(2,1)S(1)} %prepare.1.pq_ref), channel_id=1, source_target_pairs={{0,32},{32,64},{64,96},{96,128},{128,160},{160,192},{192,224},{224... | collective-permute-start | bytes 786440 | tf_op jit(solution)/shard_map/ppermute | solution.py:310
  35.8 1.0 %copy-start.1 = (bf16[32,32,128]{2,1,0:T(8,128)(2,1)S(1)}, bf16[32,32,128]{2,1,0:T(8,128)(2,1)}, u32[]{:S(2)}) copy-start(bf16[32,32,128]{2,1,0:T(8,128)(2,1)} %copy-done) | copy-start | bytes 786436
  36.7 1.6 %copy-start.2 = (bf16[32,8,4096]{2,1,0:T(8,128)(2,1)S(1)}, bf16[32,8,4096]{2,1,0:T(8,128)(2,1)}, u32[]{:S(2)}) copy-start(bf16[32,8,4096]{2,1,0:T(8,128)(2,1)} %a_ref.1) | copy-start | bytes 6291460
  38.3 0.9 %copy-start.4 = (bf16[32,4096]{1,0:T(8,128)(2,1)S(1)}, bf16[32,4096]{1,0:T(8,128)(2,1)}, u32[]{:S(2)}) copy-start(bf16[32,4096]{1,0:T(8,128)(2,1)} %p_ref.3) | copy-start | bytes 786436

commit v3 on v2

--- a/solution.py
+++ b/solution.py
@@ -13,9 +13,11 @@
 CAP = 4
 SLOT_DEV = 8
 CAP2 = 4
-GROUP = 16
+STEPS = (64, 32)
+QUARTERS = 4
 VMEM_LIMIT = 12 * 1024 * 1024
 WIDE_LIMIT = 40 * 1024 * 1024
+PLAN_LIMIT = 60 * 1024 * 1024
 SPARE = 1664
 BF16 = jnp.bfloat16
 F32 = jnp.float32
@@ -75,32 +77,41 @@
     return cols % rows, device_of // members, device_of % members
 
 
-def read_entries(entry_ref):
-    per_row, rows = SLOT_DEV, entry_ref.shape[1]
-    cols, slots, count = (entry_ref[n * per_row : (n + 1) * per_row, :] for n in range(3))
-    return cols, slots, row_of((per_row, rows)) < count, per_row, rows
-
-
-def plan_kernel(members, place_ref, entry_ref, want_ref):
-    cols, slots, live, per_row, rows = read_entries(entry_ref)
-    local, group, member = split_cols(cols, rows, members)
-    wanted = live & (group == place_ref[0]) & (member != place_ref[1])
+def plan_kernel(members, cols_ref, count_ref, slot_ref, want_ref):
+    per_row, rows = cols_ref.shape
+    local, group, member = split_cols(cols_ref[...], rows, members)
+    live = row_of((per_row, rows)) < count_ref[...]
+    slots = slot_ref[...]
+    wanted = live & (group == lax.axis_index("grp")) & (member != lax.axis_index("row"))
     present, rank = table_of(member, local, wanted, members, rows)
     want = chosen(present, rank, CAP, 0, jnp.zeros((members, LANES), jnp.int32))
     present, rank = table_of(slots // SLOT_DEV % members, slots % SLOT_DEV, live, members, SLOT_DEV)
     want_ref[...] = chosen(present, rank, CAP2, CAP, want)
 
 
-def lists_kernel(members, groups, place_ref, entry_ref, lists_ref):
-    cols, slots, live, per_row, rows = read_entries(entry_ref)
+def lists_kernel(members, groups, cols_ref, count_ref, slot_ref, asked_ref, lists_ref, spread_ref):
+    places = members * CAP2 * QUARTERS
+    from_member = ones(row_of((members, places)) == lane_of((members, places)) // (CAP2 * QUARTERS))
+    names = asked_ref[...][:, :SLOT_DEV].astype(F32).astype(BF16)
+    named = dot(names, from_member, (0, 0))
+    at = lane_of((SLOT_DEV, places))
+    mine = row_of((SLOT_DEV, places)) == CAP + at // QUARTERS % CAP2
+    slot_at = jnp.sum(jnp.where(mine, named, 0.0), axis=0, keepdims=True).astype(jnp.int32)
+    at, to = lane_of((QUARTERS * SLOT_DEV, places)), row_of((QUARTERS * SLOT_DEV, places))
+    spread_ref[...] = ones((to % SLOT_DEV == slot_at) & (to // SLOT_DEV == at % QUARTERS))
+
+    per_row, rows = cols_ref.shape
     entries = per_row * rows
-    local, group, member = split_cols(cols, rows, members)
     at_k = row_of((per_row, rows))
-    in_group = group == place_ref[0]
-    far = in_group & (member != place_ref[1])
+    local, group, member = split_cols(cols_ref[...], rows, members)
+    live = at_k < count_ref[...]
+    slots = slot_ref[...]
+    group_at = lax.axis_index("grp")
+    in_group = group == group_at
+    far = in_group & (member != lax.axis_index("row"))
     _, rank = table_of(member, local, live & far, members, rows)
     far_source = member * CAP + jnp.clip(rank_of(member, local, rank), 0, CAP - 1)
-    low = group == lax.rem(place_ref[0] + groups - 1, groups)
+    low = group == lax.rem(group_at + groups - 1, groups)
     near_source = jnp.where(in_group, local, jnp.where(low, rows + local, 2 * rows + local))
     source = jnp.where(far, far_source, near_source)
 
@@ -190,24 +201,40 @@
     return jnp.concatenate(parts, axis=0)
 
 
-def add_tiles(lists_ref, which, group, per_row, table_ref, pairs_ref, own_ref, total_ref):
-    def one(step, carry):
-        codes = [lists_ref[which, step * group + n] for n in range(group)]
-        rights = [twice(table_ref[(code >> 8) & 255]) for code in codes]
-        halves = [
-            jnp.dot(pairs_ref[code >> 16], right, preferred_element_type=F32).astype(BF16)
-            for code, right in zip(codes, rights)
-        ]
-        rights = [twice(half) for half in halves]
-        tiles = [
-            jnp.dot(own_ref[(code >> 16) // per_row], right, preferred_element_type=F32)
-            for code, right in zip(codes, rights)
-        ]
+def two_products(lefts, rights):
+    both = jnp.dot(
+        jnp.concatenate(lefts, axis=0), jnp.concatenate(rights, axis=1), preferred_element_type=F32
+    )
+    return [both[:PAIRS, :LANES], both[PAIRS:, LANES:]]
+
+
+def add_tiles(codes_ref, count, per_row, table_ref, pairs_ref, own_ref, total_ref):
+    def step(start, group):
+        codes = [codes_ref[start + n] for n in range(group)]
+        halves, tiles = [], []
+        for n in range(0, group, 2):
+            rights = [twice(table_ref[(code >> 8) & 255]) for code in codes[n : n + 2]]
+            halves += two_products([pairs_ref[code >> 16] for code in codes[n : n + 2]], rights)
+        for n in range(0, group, 2):
+            rights = [twice(half.astype(BF16)) for half in halves[n : n + 2]]
+            tiles += two_products([own_ref[(code >> 16) // per_row] for code in codes[n : n + 2]], rights)
         for code, tile in zip(codes, tiles):
             total_ref[code & 255] += tile
+
+    large, small = STEPS
+    whole = (count + large - 1 - small) // large
+    rest = jnp.maximum(count - whole * large, 0)
+
+    def one_large(n, carry):
+        step(n * large, large)
         return carry
 
-    lax.fori_loop(0, (lists_ref[2 + which, 0] + group - 1) // group, one, 0)
+    def one_small(n, carry):
+        step(whole * large + n * small, small)
+        return carry
+
+    lax.fori_loop(0, whole, one_large, 0)
+    lax.fori_loop(0, (rest + small - 1) // small, one_small, 0)
 
 
 def views(work_ref, entries, per_row):
@@ -230,26 +257,32 @@
     for at, ref in enumerate((pq_ref, low_ref, high_ref)):
         table[pl.ds(at * rows, rows)] = ref[...]
     clear(total_ref)
-    add_tiles(lists_ref, 0, GROUP, per_row, table, pairs_ref, own_ref, total_ref)
+    add_tiles(lists_ref.at[0], lists_ref[2, 0], per_row, table, pairs_ref, own_ref, total_ref)
     sums = total_ref.shape[0] - 1
     copy = pltpu.make_async_copy(total_ref.at[pl.ds(0, sums)], near_ref.at[pl.ds(0, sums)], sem)
     copy.start()
     copy.wait()
 
 
-def far_kernel(per_row, lists_ref, work_ref, got_ref, near_ref, out_ref, total, near, sem):
-    copy = pltpu.make_async_copy(near_ref.at[pl.ds(0, near.shape[0])], near, sem)
-    copy.start()
+def far_kernel(per_row, lists_from, work_ref, got_ref, near_ref, out_ref, total, lists_ref, sem):
+    blocks = total.shape[0] - 1
+    copies = [
+        pltpu.make_async_copy(near_ref.at[pl.ds(0, blocks)], total.at[pl.ds(0, blocks)], sem.at[0]),
+        pltpu.make_async_copy(lists_from, lists_ref, sem.at[1]),
+    ]
+    for copy in copies:
+        copy.start()
+    total[blocks] = jnp.zeros((PAIRS, LANES), F32)
     pairs_ref, own_ref = views(work_ref, lists_ref.shape[1], per_row)
-    clear(total)
-    add_tiles(lists_ref, 1, GROUP, per_row, got_ref, pairs_ref, own_ref, total)
-    copy.wait()
-
-    def one(at, carry):
-        out_ref[at] = (total[at] + near[at]).astype(BF16)
-        return carry
-
-    lax.fori_loop(0, out_ref.shape[0], one, 0, unroll=8)
+    for copy in copies:
+        copy.wait()
+    add_tiles(lists_ref.at[1], lists_ref[3, 0], per_row, got_ref, pairs_ref, own_ref, total)
+    for member in range(out_ref.shape[0]):
+        for at in range(PAIRS // QUARTERS):
+            rows = total.at[pl.ds(member * CAP2, CAP2)].reshape(CAP2 * PAIRS, LANES)[
+                pl.ds(at, CAP2 * QUARTERS, stride=PAIRS // QUARTERS), :
+            ]
+            out_ref[member, :, at * LANES : (at + 1) * LANES] = rows.astype(BF16)
 
 
 def pack_kernel(members, asked_ref, pq_ref, out_ref):
@@ -258,17 +291,11 @@
             out_ref[member * CAP + s] = pq_ref[asked_ref[member, s]]
 
 
-def sum_kernel(members, asked_ref, got_ref, out_ref, *totals):
-    for total in totals:
-        total[...] = jnp.zeros_like(total)
-    for member in range(members):
-        for s, total in enumerate(totals):
-            to = pl.multiple_of(asked_ref[member, CAP + s] * PAIRS, PAIRS)
-            total[pl.ds(to, PAIRS), :] += got_ref[member * CAP2 + s].astype(F32)
-    for r in range(PAIRS):
-        out_ref[:, r * LANES : (r + 1) * LANES] = sum(
-            total[pl.ds(r, SLOT_DEV, stride=PAIRS), :] for total in totals
-        )
+def sum_kernel(spread_ref, got_ref, out_ref):
+    result = jnp.dot(spread_ref[...], got_ref[...], preferred_element_type=F32)
+    width = got_ref.shape[1]
+    for n in range(QUARTERS):
+        out_ref[:, n * width : (n + 1) * width] = result[n * SLOT_DEV : (n + 1) * SLOT_DEV]
 
 
 def body(a_blocks, p_blocks, a_cols, a_count, tile_slot):
@@ -276,7 +303,6 @@
     members = lax.axis_size("row")
     groups = lax.axis_size("grp")
     entries = rows * per_row
-    place = jnp.stack([lax.axis_index("grp"), lax.axis_index("row")]).astype(jnp.int32)
     smem = pl.BlockSpec(memory_space=pltpu.SMEM)
     vmem = pl.BlockSpec(memory_space=pltpu.VMEM)
     hbm = pl.BlockSpec(memory_space=pltpu.HBM)
@@ -295,12 +321,10 @@
             name=name,
         )
 
-    entry = jnp.concatenate(
-        [a_cols.T, tile_slot.T, jnp.broadcast_to(a_count[None], (per_row, rows))], axis=0
-    )
+    entry = (a_cols.T, a_count.reshape(1, rows), tile_slot.T)
     want = call(
-        functools.partial(plan_kernel, members), "plan", [smem, vmem], ints(members, LANES), [], 2
-    )(place, entry)
+        functools.partial(plan_kernel, members), "plan", [vmem] * 3, ints(members, LANES), [], 2, limit=PLAN_LIMIT
+    )(*entry)
     asked = lax.all_to_all(want.reshape(members, 1, LANES), "row", 0, 0, tiled=True).reshape(members, LANES)
 
     pq = call(
@@ -317,14 +341,15 @@
         send.reshape(members, CAP, PAIRS, LANES), "row", 0, 0, tiled=True
     ).reshape(members * CAP, PAIRS, LANES)
 
-    lists = call(
+    lists, spread = call(
         functools.partial(lists_kernel, members, groups),
         "lists",
-        [smem, vmem],
-        ints(SLOT_DEV, entries),
+        [vmem] * 4,
+        (ints(SLOT_DEV, entries), jax.ShapeDtypeStruct((QUARTERS * SLOT_DEV, members * CAP2 * QUARTERS), BF16)),
         [],
         0.1,
-    )(place, entry)
+        (vmem, vmem),
+    )(*entry, asked)
     work, near = call(
         functools.partial(near_kernel, per_row),
         "near",
@@ -344,28 +369,21 @@
     sums = call(
         functools.partial(far_kernel, per_row),
         "far",
-        [smem, vmem, vmem, hbm],
-        blocks(members * CAP2),
+        [vmem, vmem, vmem, hbm],
+        jax.ShapeDtypeStruct((members, CAP2 * QUARTERS, area // QUARTERS), BF16),
         [
             pltpu.VMEM((members * CAP2 + 1, PAIRS, LANES), F32),
-            pltpu.VMEM((members * CAP2, PAIRS, LANES), F32),
-            pltpu.SemaphoreType.DMA,
+            pltpu.SMEM((SLOT_DEV, entries), jnp.int32),
+            pltpu.SemaphoreType.DMA((2,)),
         ],
         6,
         limit=WIDE_LIMIT,
     )(lists, work, got, near)
-    parts = lax.all_to_all(
-        sums.reshape(members, CAP2, PAIRS, LANES), "row", 0, 0, tiled=True
-    ).reshape(members * CAP2, PAIRS, LANES)
+    parts = lax.all_to_all(sums, "row", 0, 0, tiled=True).reshape(-1, area // QUARTERS)
 
     return call(
-        functools.partial(sum_kernel, members),
-        "holders",
-        [smem, vmem],
-        jax.ShapeDtypeStruct((SLOT_DEV, area), F32),
-        [pltpu.VMEM((SLOT_DEV * PAIRS, LANES), F32)] * CAP2,
-        2,
-    )(asked, parts)
+        sum_kernel, "holders", [vmem, vmem], jax.ShapeDtypeStruct((SLOT_DEV, area), F32), [], 2
+    )(spread, parts)
 
 
 def solution(mesh):

time: 96.3 us -> 93.4 us (0.970)
  Pallas kernels: 20.2 us -> 16.3 us
  waiting for transfers between devices: 20.2 us -> 22.1 us
    pallas_call x4, Pallas kernels: 10.4 us -> 8.01 us  [the longest x1 3.7 us: body(): call(functools.partial(far_kernel, per_row), 'far', [vmem, vmem, vmem, hb...]
    pallas_call x1, Pallas kernels: 7.44 us -> 5.96 us  [body(): call(functools.partial(near_kernel, per_row), 'near', [smem, vmem, vmem,...]
    all_to_all x1, waiting for transfers between devices: 9.72 us -> 11.2 us  [body(): lax.all_to_all(send.reshape(members, CAP, PAIRS, LANES), 'row', 0, 0, til...]
    unnamed x10 -> x16, local copies, waits for them, and re-layouts: 4.44 us -> 4.45 us
  transfers between devices with their start and end apart: 4 -> 4, of which waited for: 4 -> 4; matrix products, arithmetic and copies ran while one was open for 0% -> 0% of each run, Pallas kernels for 10% -> 9%
where the time goes in v3:
time: 93.4 us; the launch traced here: 92 us
  blocking collectives  32.2 us (34%)
  waiting for transfers between devices  22.1 us (24%)
  starting transfers between devices  16.9 us (18%)
  Pallas kernels  16.3 us (17%)
  local copies, waits for them, and re-layouts  4.45 us (5%)
    all_to_all x1, blocking collectives, body(): lax.all_to_all(sums, 'row', 0, 0, tiled=True).reshape(-1, area // QUARTERS)  32.2 us
    all_to_all x1, starting transfers between devices, body(): lax.all_to_all(want.reshape(members, 1, LANES), 'row', 0, 0, tiled=True)  11.4 us
    all_to_all x1, waiting for transfers between devices, body(): lax.all_to_all(send.reshape(members, CAP, PAIRS, LANES), 'row', 0, 0, til...  11.2 us
    all_to_all x1, waiting for transfers between devices, body(): lax.all_to_all(want.reshape(members, 1, LANES), 'row', 0, 0, tiled=True)  7.05 us
    pallas_call x1, Pallas kernels, body(): call(functools.partial(near_kernel, per_row), 'near', [smem, vmem, vmem,...  5.96 us
    all_to_all x1, starting transfers between devices, body(): lax.all_to_all(send.reshape(members, CAP, PAIRS, LANES), 'row', 0, 0, til...  5.01 us
    unnamed x16, local copies, waits for them, and re-layouts  4.45 us
    pallas_call x1, Pallas kernels, body(): call(functools.partial(far_kernel, per_row), 'far', [vmem, vmem, vmem, hb...  3.7 us
  transfers between devices with their start and end apart: 4, of which 4 were waited for; matrix products, arithmetic and copies ran while one was open for 0% of the time, Pallas kernels for 9%

profile of v3, /device:TPU:38, one launch (start us, length us, event | category | flops | bytes accessed | tf_op | source)
XLA Modules:
  0.0 92.0 jit_solution(2392499688337451051)
XLA Ops:
  0.0 0.0 copy-start.6
  0.0 0.0 copy-start.7
  0.0 0.0 copy-start.5
  0.0 1.9 %plan.1 = s32[32,128]{1,0:T(8,128)} custom-call(s32[8,32]{1,0:T(8,128)} %bitcast.14, s32[1,32]{1,0:T(1,128)} %bitcast.18, s32[8,32]{1,0:T(8,128)} %bitcast.16), custom_call_target="tpu_custom_call" | custom-call | bytes 6000000 | tf_op jit(solution)/shard_map/plan/pallas_call | solution.py:325
  2.0 11.4 %all-to-all-start = ((s32[32,1,128]{2,1,0:T(1,128)}), s32[32,1,128]{2,1,0:T(1,128)S(1)}, u32[]{:S(2)}, u32[]{:S(2)}) async-start(s32[32,1,128]{2,1,0:T(1,128)} %bitcast.20), calls=%async_computation | async-start | bytes 32768 | tf_op jit(solution)/shard_map/all_to_all | solution.py:328
  13.3 0.0 copy-start.3
  13.3 0.9 %copy-done.3 = bf16[32,4096]{1,0:T(8,128)(2,1)S(1)} copy-done((bf16[32,4096]{1,0:T(8,128)(2,1)S(1)}, bf16[32,4096]{1,0:T(8,128)(2,1)}, u32[]{:S(2)}) %copy-start.3) | copy-done | bytes 262168
  14.3 0.5 prepare.1.pq_ref
  14.8 0.0 copy-start
  14.8 7.0 %all-to-all-done = s32[32,1,128]{2,1,0:T(1,128)S(1)} async-done(((s32[32,1,128]{2,1,0:T(1,128)}), s32[32,1,128]{2,1,0:T(1,128)S(1)}, u32[]{:S(2)}, u32[]{:S(2)}) %all-to-all-start) | async-done | bytes 16416 | tf_op jit(solution)/shard_map/all_to_all | solution.py:328
  21.8 1.9 %pack.1 = bf16[128,32,128]{2,1,0:T(8,128)(2,1)} custom-call(s32[32,128]{1,0:T(8,128)S(1)} %bitcast.12, bf16[32,32,128]{2,1,0:T(8,128)(2,1)S(1)} %prepare.1.pq_ref), custom_call_target="tpu_custom_call" | custom-call | bytes 6000000 | tf_op jit(solution)/shard_map/pack/pallas_call | solution.py:337
  23.7 5.0 %all-to-all-start.1 = ((bf16[32,4,32,128]{3,2,1,0:T(8,128)(2,1)}), bf16[32,4,32,128]{3,2,1,0:T(8,128)(2,1)S(1)}, u32[]{:S(2)}, u32[]{:S(2)}) async-start(bf16[32,4,32,128]{3,2,1,0:T(8,128)(2,1)} %bitcast.6), calls=%async_computation.1 | async-start | bytes 2097152 | tf_op jit(solution)/shard_map/all_to_all | solution.py:340
  28.7 0.0 collective-permute-start.1
  28.7 0.5 collective-permute-start
  29.2 0.0 copy-done.6
  29.2 0.0 copy-done.7
  29.2 0.0 copy-done.5
  29.2 1.4 %lists.1 = (s32[8,256]{1,0:T(8,128)S(1)}, bf16[32,512]{1,0:T(8,128)(2,1)S(1)}) custom-call(s32[8,32]{1,0:T(8,128)S(1)} %bitcast.15, s32[1,32]{1,0:T(1,128)S(1)} %bitcast.19, s32[8,32]{1,0:T(8,128)S(1)} %bitcast.17, s32[32,128]{1,0:T(8,128)S(1)} %bitcast.13), custom_call_target="tpu_custom_call" | custom-call | bytes 300000 | tf_op jit(solution)/shard_map/lists/pallas_call | solution.py:344
  30.7 2.0 %collective-permute-done.1.high_ref = bf16[32,32,128]{2,1,0:T(8,128)(2,1)S(1)} collective-permute-done((bf16[32,32,128]{2,1,0:T(8,128)(2,1)S(1)}, bf16[32,32,128]{2,1,0:T(8,128)(2,1)S(1)}, u32[]{:S(2)}, u32[]{:S(2)}) %collective-permute-start.1) | collective-permute-done | bytes 262176 | tf_op jit(solution)/shard_map/ppermute | solution.py:335
  32.6 1.9 %collective-permute-done.low_ref = bf16[32,32,128]{2,1,0:T(8,128)(2,1)S(1)} collective-permute-done((bf16[32,32,128]{2,1,0:T(8,128)(2,1)S(1)}, bf16[32,32,128]{2,1,0:T(8,128)(2,1)S(1)}, u32[]{:S(2)}, u32[]{:S(2)}) %collective-permute-start) | collective-permute-done | bytes 262176 | tf_op jit(solution)/shard_map/ppermute | solution.py:334
  34.5 0.0 copy-done
  34.5 0.0 copy-start.1
  34.5 0.9 %copy-done.1 = bf16[32,32,128]{2,1,0:T(8,128)(2,1)S(1)} copy-done((bf16[32,32,128]{2,1,0:T(8,128)(2,1)S(1)}, bf16[32,32,128]{2,1,0:T(8,128)(2,1)}, u32[]{:S(2)}) %copy-start.1) | copy-done | bytes 262168
  35.5 0.0 copy-start.2
  35.5 1.6 %copy-done.2 = bf16[32,8,4096]{2,1,0:T(8,128)(2,1)S(1)} copy-done((bf16[32,8,4096]{2,1,0:T(8,128)(2,1)S(1)}, bf16[32,8,4096]{2,1,0:T(8,128)(2,1)}, u32[]{:S(2)}) %copy-start.2) | copy-done | bytes 2097176
  37.1 0.0 copy-start.4
  37.1 0.9 %copy-done.4 = bf16[32,4096]{1,0:T(8,128)(2,1)S(1)} copy-done((bf16[32,4096]{1,0:T(8,128)(2,1)S(1)}, bf16[32,4096]{1,0:T(8,128)(2,1)}, u32[]{:S(2)}) %copy-start.4) | copy-done | bytes 262168
  38.0 6.0 %near.1 = (bf16[288,32,128]{2,1,0:T(8,128)(2,1)S(1)}, f32[1664,32,128]{2,1,0:T(8,128)}) custom-call(s32[8,256]{1,0:T(8,128)S(1)} %get-tuple-element.10.lists_ref.lists_from, bf16[32,8,4096]{2,1,0:T(8,128)(2,1)S(1)} %copy-done.2, bf16[32,4096]{1,0:T(8,128)(2,1)S(1)} %copy-done.4, bf16[32,32,128]{2,1,0:T(8,128)(2,1)S(1)} %copy-done.1, ...), custom_call_target="tpu_custom_call" | custom-call | bytes 300000 | tf_op jit(solution)/shard_map/near/pallas_call | solution.py:353
  44.0 11.2 %all-to-all-done.1 = bf16[32,4,32,128]{3,2,1,0:T(8,128)(2,1)S(1)} async-done(((bf16[32,4,32,128]{3,2,1,0:T(8,128)(2,1)}), bf16[32,4,32,128]{3,2,1,0:T(8,128)(2,1)S(1)}, u32[]{:S(2)}, u32[]{:S(2)}) %all-to-all-start.1) | async-done | bytes 1048608 | tf_op jit(solution)/shard_map/all_to_all | solution.py:340
  55.2 3.7 %far.1 = bf16[32,16,1024]{2,1,0:T(8,128)(2,1)S(1)} custom-call(s32[8,256]{1,0:T(8,128)S(1)} %get-tuple-element.10.lists_ref.lists_from, bf16[288,32,128]{2,1,0:T(8,128)(2,1)S(1)} %get-tuple-element.11.work_ref, bf16[128,32,128]{2,1,0:T(8,128)(2,1)S(1)} %bitcast.10, f32[1664,32,128]{2,1,0:T(8,128)} %get-tuple-element.12.near_ref), custom_call_target="tpu_custom_call" | custom-call | bytes 18000000 | tf_op jit(solution)/shard_map/far/pallas_call | solution.py:369
  58.9 32.2 %all_to_all.15 = bf16[32,16,1024]{2,1,0:T(8,128)(2,1)S(1)} all-to-all(bf16[32,16,1024]{2,1,0:T(8,128)(2,1)S(1)} %far.1), channel_id=1, replica_groups=mesh['grp'=8,'row'=32] {'row'}, dimensions={0} | all-to-all | bytes 2097152 | tf_op jit(solution)/shard_map/all_to_all | solution.py:382
  91.1 0.9 %holders.1 = f32[8,4096]{1,0:T(8,128)} custom-call(bf16[32,512]{1,0:T(8,128)(2,1)S(1)} %get-tuple-element.9.spread_ref, bf16[512,1024]{1,0:T(8,128)(2,1)S(1)} %bitcast.11), custom_call_target="tpu_custom_call" | custom-call | bytes 6000000 | tf_op jit(solution)/shard_map/holders/pallas_call | solution.py:384
Async XLA Ops:
  0.0 29.2 %copy-start.6 = (s32[32,8]{0,1:T(8,128)S(1)}, s32[32,8]{0,1:T(8,128)}, u32[]{:S(2)}) copy-start(s32[32,8]{0,1:T(8,128)} %param.9) | copy-start | bytes 3076
  0.0 29.2 %copy-start.7 = (s32[32]{0:T(128)S(1)}, s32[32]{0:T(128)}, u32[]{:S(2)}) copy-start(s32[32]{0:T(128)} %param.8) | copy-start | bytes 388
  0.0 29.2 %copy-start.5 = (s32[32,8]{0,1:T(8,128)S(1)}, s32[32,8]{0,1:T(8,128)}, u32[]{:S(2)}) copy-start(s32[32,8]{0,1:T(8,128)} %param.7) | copy-start | bytes 3076
  2.0 19.9 %all-to-all-start = ((s32[32,1,128]{2,1,0:T(1,128)}), s32[32,1,128]{2,1,0:T(1,128)S(1)}, u32[]{:S(2)}, u32[]{:S(2)}) async-start(s32[32,1,128]{2,1,0:T(1,128)} %bitcast.20), calls=%async_computation | async-start | bytes 32768 | tf_op jit(solution)/shard_map/all_to_all | solution.py:328
  13.3 1.0 %copy-start.3 = (bf16[32,4096]{1,0:T(8,128)(2,1)S(1)}, bf16[32,4096]{1,0:T(8,128)(2,1)}, u32[]{:S(2)}) copy-start(bf16[32,4096]{1,0:T(8,128)(2,1)} %p_ref.3) | copy-start | bytes 786436
  14.8 19.8 %copy-start = (bf16[32,32,128]{2,1,0:T(8,128)(2,1)}, bf16[32,32,128]{2,1,0:T(8,128)(2,1)S(1)}, u32[]{:S(2)}) copy-start(bf16[32,32,128]{2,1,0:T(8,128)(2,1)S(1)} %prepare.1.pq_ref) | copy-start | bytes 786436
  23.7 31.5 %all-to-all-start.1 = ((bf16[32,4,32,128]{3,2,1,0:T(8,128)(2,1)}), bf16[32,4,32,128]{3,2,1,0:T(8,128)(2,1)S(1)}, u32[]{:S(2)}, u32[]{:S(2)}) async-start(bf16[32,4,32,128]{3,2,1,0:T(8,128)(2,1)} %bitcast.6), calls=%async_computation.1 | async-start | bytes 2097152 | tf_op jit(solution)/shard_map/all_to_all | solution.py:340
  28.7 3.9 %collective-permute-start.1 = (bf16[32,32,128]{2,1,0:T(8,128)(2,1)S(1)}, bf16[32,32,128]{2,1,0:T(8,128)(2,1)S(1)}, u32[]{:S(2)}, u32[]{:S(2)}) collective-permute-start(bf16[32,32,128]{2,1,0:T(8,128)(2,1)S(1)} %prepare.1.pq_ref), channel_id=1, source_target_pairs={{32,0},{64,32},{96,64},{128,96},{160,128},{192,160},{224,192},{0,2... | collective-permute-start | bytes 786440 | tf_op jit(solution)/shard_map/ppermute | solution.py:335
  28.7 5.8 %collective-permute-start = (bf16[32,32,128]{2,1,0:T(8,128)(2,1)S(1)}, bf16[32,32,128]{2,1,0:T(8,128)(2,1)S(1)}, u32[]{:S(2)}, u32[]{:S(2)}) collective-permute-start(bf16[32,32,128]{2,1,0:T(8,128)(2,1)S(1)} %prepare.1.pq_ref), channel_id=1, source_target_pairs={{0,32},{32,64},{64,96},{96,128},{128,160},{160,192},{192,224},{224... | collective-permute-start | bytes 786440 | tf_op jit(solution)/shard_map/ppermute | solution.py:334
  34.5 1.0 %copy-start.1 = (bf16[32,32,128]{2,1,0:T(8,128)(2,1)S(1)}, bf16[32,32,128]{2,1,0:T(8,128)(2,1)}, u32[]{:S(2)}) copy-start(bf16[32,32,128]{2,1,0:T(8,128)(2,1)} %copy-done) | copy-start | bytes 786436
  35.5 1.6 %copy-start.2 = (bf16[32,8,4096]{2,1,0:T(8,128)(2,1)S(1)}, bf16[32,8,4096]{2,1,0:T(8,128)(2,1)}, u32[]{:S(2)}) copy-start(bf16[32,8,4096]{2,1,0:T(8,128)(2,1)} %a_ref.1) | copy-start | bytes 6291460
  37.1 0.9 %copy-start.4 = (bf16[32,4096]{1,0:T(8,128)(2,1)S(1)}, bf16[32,4096]{1,0:T(8,128)(2,1)}, u32[]{:S(2)}) copy-start(bf16[32,4096]{1,0:T(8,128)(2,1)} %p_ref.3) | copy-start | bytes 786436

commit v4 on v3

--- a/solution.py
+++ b/solution.py
@@ -14,6 +14,7 @@
 SLOT_DEV = 8
 CAP2 = 4
 STEPS = (64, 32)
+ASK, ROWS, SUMS = (tuple(reversed(range(32))),) * 3
 QUARTERS = 4
 VMEM_LIMIT = 12 * 1024 * 1024
 WIDE_LIMIT = 40 * 1024 * 1024
@@ -72,6 +73,17 @@
     return result
 
 
+def place_in(order, member):
+    result = jnp.zeros_like(member)
+    for at, who in enumerate(order):
+        result = jnp.where(member == who, at, result)
+    return result
+
+
+def exchange(x, order):
+    return lax.all_to_all(x, "row", 0, 0, tiled=True, axis_index_groups=[list(order)])
+
+
 def split_cols(cols, rows, members):
     device_of = cols // rows
     return cols % rows, device_of // members, device_of % members
@@ -83,15 +95,20 @@
     live = row_of((per_row, rows)) < count_ref[...]
     slots = slot_ref[...]
     wanted = live & (group == lax.axis_index("grp")) & (member != lax.axis_index("row"))
-    present, rank = table_of(member, local, wanted, members, rows)
+    present, rank = table_of(place_in(ASK, member), local, wanted, members, rows)
     want = chosen(present, rank, CAP, 0, jnp.zeros((members, LANES), jnp.int32))
-    present, rank = table_of(slots // SLOT_DEV % members, slots % SLOT_DEV, live, members, SLOT_DEV)
+    holder = place_in(ASK, slots // SLOT_DEV % members)
+    present, rank = table_of(holder, slots % SLOT_DEV, live, members, SLOT_DEV)
     want_ref[...] = chosen(present, rank, CAP2, CAP, want)
 
 
 def lists_kernel(members, groups, cols_ref, count_ref, slot_ref, asked_ref, lists_ref, spread_ref):
     places = members * CAP2 * QUARTERS
-    from_member = ones(row_of((members, places)) == lane_of((members, places)) // (CAP2 * QUARTERS))
+    sender = lane_of((members, places)) // (CAP2 * QUARTERS)
+    from_member = jnp.zeros((members, places), jnp.bool_)
+    for at, who in enumerate(SUMS):
+        from_member = from_member | ((sender == at) & (row_of((members, places)) == ASK.index(who)))
+    from_member = ones(from_member)
     names = asked_ref[...][:, :SLOT_DEV].astype(F32).astype(BF16)
     named = dot(names, from_member, (0, 0))
     at = lane_of((SLOT_DEV, places))
@@ -110,14 +127,14 @@
     in_group = group == group_at
     far = in_group & (member != lax.axis_index("row"))
     _, rank = table_of(member, local, live & far, members, rows)
-    far_source = member * CAP + jnp.clip(rank_of(member, local, rank), 0, CAP - 1)
+    far_source = place_in(ROWS, member) * CAP + jnp.clip(rank_of(member, local, rank), 0, CAP - 1)
     low = group == lax.rem(group_at + groups - 1, groups)
     near_source = jnp.where(in_group, local, jnp.where(low, rows + local, 2 * rows + local))
     source = jnp.where(far, far_source, near_source)
 
     owner, slot = slots // SLOT_DEV % members, slots % SLOT_DEV
     _, rank = table_of(owner, slot, live, members, SLOT_DEV)
-    target = owner * CAP2 + jnp.clip(rank_of(owner, slot, rank), 0, CAP2 - 1)
+    target = place_in(SUMS, owner) * CAP2 + jnp.clip(rank_of(owner, slot, rank), 0, CAP2 - 1)
 
     entry = lane_of((per_row, rows)) * per_row + at_k
     before = ones(row_of((rows, rows)) < lane_of((rows, rows)))
@@ -286,9 +303,9 @@
 
 
 def pack_kernel(members, asked_ref, pq_ref, out_ref):
-    for member in range(members):
+    for at in range(members):
         for s in range(CAP):
-            out_ref[member * CAP + s] = pq_ref[asked_ref[member, s]]
+            out_ref[at * CAP + s] = pq_ref[asked_ref[ASK.index(ROWS[at]), s]]
 
 
 def sum_kernel(spread_ref, got_ref, out_ref):
@@ -325,7 +342,7 @@
     want = call(
         functools.partial(plan_kernel, members), "plan", [vmem] * 3, ints(members, LANES), [], 2, limit=PLAN_LIMIT
     )(*entry)
-    asked = lax.all_to_all(want.reshape(members, 1, LANES), "row", 0, 0, tiled=True).reshape(members, LANES)
+    asked = exchange(want.reshape(members, 1, LANES), ASK).reshape(members, LANES)
 
     pq = call(
         prepare_kernel, "prepare", [vmem], blocks(rows), [pltpu.VMEM((PAIRS * rows, LANES), F32)], 0.1
@@ -337,9 +354,7 @@
     send = call(
         functools.partial(pack_kernel, members), "pack", [smem, vmem], blocks(members * CAP), [], 2
     )(asked, pq)
-    got = lax.all_to_all(
-        send.reshape(members, CAP, PAIRS, LANES), "row", 0, 0, tiled=True
-    ).reshape(members * CAP, PAIRS, LANES)
+    got = exchange(send.reshape(members, CAP, PAIRS, LANES), ROWS).reshape(members * CAP, PAIRS, LANES)
 
     lists, spread = call(
         functools.partial(lists_kernel, members, groups),
@@ -379,7 +394,7 @@
         6,
         limit=WIDE_LIMIT,
     )(lists, work, got, near)
-    parts = lax.all_to_all(sums, "row", 0, 0, tiled=True).reshape(-1, area // QUARTERS)
+    parts = exchange(sums, SUMS).reshape(-1, area // QUARTERS)
 
     return call(
         sum_kernel, "holders", [vmem, vmem], jax.ShapeDtypeStruct((SLOT_DEV, area), F32), [], 2

time: 93.4 us -> 90.6 us (0.970)
  waiting for transfers between devices: 22.1 us -> 15.8 us
  starting transfers between devices: 16.9 us -> 21.1 us
    all_to_all x2, waiting for transfers between devices: 18.2 us -> 11.9 us  [exchange(): lax.all_to_all(x, 'row', 0, 0, tiled=True, axis_index_groups=[list(order)])]
    all_to_all x2, starting transfers between devices: 16.4 us -> 20.6 us  [exchange(): lax.all_to_all(x, 'row', 0, 0, tiled=True, axis_index_groups=[list(order)])]
where the time goes in v4:
time: 90.6 us; the launch traced here: 90.1 us
  blocking collectives  32.3 us (36%)
  starting transfers between devices  21.1 us (23%)
  Pallas kernels  16.3 us (18%)
  waiting for transfers between devices  15.8 us (17%)
  local copies, waits for them, and re-layouts  4.45 us (5%)
    all_to_all x1, blocking collectives, exchange(): lax.all_to_all(x, 'row', 0, 0, tiled=True, axis_index_groups=[list(order)])  32.3 us
    all_to_all x2, starting transfers between devices, exchange(): lax.all_to_all(x, 'row', 0, 0, tiled=True, axis_index_groups=[list(order)])  20.6 us
    all_to_all x2, waiting for transfers between devices, exchange(): lax.all_to_all(x, 'row', 0, 0, tiled=True, axis_index_groups=[list(order)])  11.9 us
    pallas_call x1, Pallas kernels, body(): call(functools.partial(near_kernel, per_row), 'near', [smem, vmem, vmem,...  5.96 us
    unnamed x16, local copies, waits for them, and re-layouts  4.45 us
    pallas_call x1, Pallas kernels, body(): call(functools.partial(far_kernel, per_row), 'far', [vmem, vmem, vmem, hb...  3.69 us
    pallas_call x1, Pallas kernels, body(): call(functools.partial(plan_kernel, members), 'plan', [vmem] * 3, ints(me...  1.96 us
    ppermute x1, waiting for transfers between devices, body(): lax.ppermute(pq, 'grp', [(target, source) for source, target in forward])  1.95 us
  transfers between devices with their start and end apart: 4, of which 4 were waited for; matrix products, arithmetic and copies ran while one was open for 0% of the time, Pallas kernels for 9%

profile of v4, /device:TPU:38, one launch (start us, length us, event | category | flops | bytes accessed | tf_op | source)
XLA Modules:
  0.0 90.1 jit_solution(5390418233758804208)
XLA Ops:
  0.0 0.0 copy-start.6
  0.0 0.0 copy-start.7
  0.0 0.0 copy-start.5
  0.0 2.0 %plan.1 = s32[32,128]{1,0:T(8,128)} custom-call(s32[8,32]{1,0:T(8,128)} %bitcast.14, s32[1,32]{1,0:T(1,128)} %bitcast.18, s32[8,32]{1,0:T(8,128)} %bitcast.16), custom_call_target="tpu_custom_call" | custom-call | bytes 6000000 | tf_op jit(solution)/shard_map/plan/pallas_call | solution.py:342
  2.0 11.9 %all-to-all-start = ((s32[32,1,128]{2,1,0:T(1,128)}), s32[32,1,128]{2,1,0:T(1,128)S(1)}, u32[]{:S(2)}, u32[]{:S(2)}) async-start(s32[32,1,128]{2,1,0:T(1,128)} %bitcast.20), calls=%async_computation | async-start | bytes 32768 | tf_op jit(solution)/shard_map/all_to_all | solution.py:84
  13.9 0.0 copy-start.3
  13.9 0.9 %copy-done.3 = bf16[32,4096]{1,0:T(8,128)(2,1)S(1)} copy-done((bf16[32,4096]{1,0:T(8,128)(2,1)S(1)}, bf16[32,4096]{1,0:T(8,128)(2,1)}, u32[]{:S(2)}) %copy-start.3) | copy-done | bytes 262168
  14.8 0.5 prepare.1.pq_ref
  15.3 0.0 copy-start
  15.3 3.5 %all-to-all-done = s32[32,1,128]{2,1,0:T(1,128)S(1)} async-done(((s32[32,1,128]{2,1,0:T(1,128)}), s32[32,1,128]{2,1,0:T(1,128)S(1)}, u32[]{:S(2)}, u32[]{:S(2)}) %all-to-all-start) | async-done | bytes 16416 | tf_op jit(solution)/shard_map/all_to_all | solution.py:84
  18.8 1.9 %pack.1 = bf16[128,32,128]{2,1,0:T(8,128)(2,1)} custom-call(s32[32,128]{1,0:T(8,128)S(1)} %bitcast.12, bf16[32,32,128]{2,1,0:T(8,128)(2,1)S(1)} %prepare.1.pq_ref), custom_call_target="tpu_custom_call" | custom-call | bytes 6000000 | tf_op jit(solution)/shard_map/pack/pallas_call | solution.py:354
  20.7 8.7 %all-to-all-start.1 = ((bf16[32,4,32,128]{3,2,1,0:T(8,128)(2,1)}), bf16[32,4,32,128]{3,2,1,0:T(8,128)(2,1)S(1)}, u32[]{:S(2)}, u32[]{:S(2)}) async-start(bf16[32,4,32,128]{3,2,1,0:T(8,128)(2,1)} %bitcast.6), calls=%async_computation.1 | async-start | bytes 2097152 | tf_op jit(solution)/shard_map/all_to_all | solution.py:84
  29.4 0.0 collective-permute-start.1
  29.4 0.5 collective-permute-start
  29.9 0.0 copy-done.6
  29.9 0.0 copy-done.7
  29.9 0.0 copy-done.5
  29.9 1.4 %lists.1 = (s32[8,256]{1,0:T(8,128)S(1)}, bf16[32,512]{1,0:T(8,128)(2,1)S(1)}) custom-call(s32[8,32]{1,0:T(8,128)S(1)} %bitcast.15, s32[1,32]{1,0:T(1,128)S(1)} %bitcast.19, s32[8,32]{1,0:T(8,128)S(1)} %bitcast.17, s32[32,128]{1,0:T(8,128)S(1)} %bitcast.13), custom_call_target="tpu_custom_call" | custom-call | bytes 300000 | tf_op jit(solution)/shard_map/lists/pallas_call | solution.py:359
  31.3 2.0 %collective-permute-done.1.high_ref = bf16[32,32,128]{2,1,0:T(8,128)(2,1)S(1)} collective-permute-done((bf16[32,32,128]{2,1,0:T(8,128)(2,1)S(1)}, bf16[32,32,128]{2,1,0:T(8,128)(2,1)S(1)}, u32[]{:S(2)}, u32[]{:S(2)}) %collective-permute-start.1) | collective-permute-done | bytes 262176 | tf_op jit(solution)/shard_map/ppermute | solution.py:352
  33.3 1.9 %collective-permute-done.low_ref = bf16[32,32,128]{2,1,0:T(8,128)(2,1)S(1)} collective-permute-done((bf16[32,32,128]{2,1,0:T(8,128)(2,1)S(1)}, bf16[32,32,128]{2,1,0:T(8,128)(2,1)S(1)}, u32[]{:S(2)}, u32[]{:S(2)}) %collective-permute-start) | collective-permute-done | bytes 262176 | tf_op jit(solution)/shard_map/ppermute | solution.py:351
  35.2 0.0 copy-done
  35.2 0.0 copy-start.1
  35.2 0.9 %copy-done.1 = bf16[32,32,128]{2,1,0:T(8,128)(2,1)S(1)} copy-done((bf16[32,32,128]{2,1,0:T(8,128)(2,1)S(1)}, bf16[32,32,128]{2,1,0:T(8,128)(2,1)}, u32[]{:S(2)}) %copy-start.1) | copy-done | bytes 262168
  36.2 0.0 copy-start.2
  36.2 1.6 %copy-done.2 = bf16[32,8,4096]{2,1,0:T(8,128)(2,1)S(1)} copy-done((bf16[32,8,4096]{2,1,0:T(8,128)(2,1)S(1)}, bf16[32,8,4096]{2,1,0:T(8,128)(2,1)}, u32[]{:S(2)}) %copy-start.2) | copy-done | bytes 2097176
  37.8 0.0 copy-start.4
  37.8 0.9 %copy-done.4 = bf16[32,4096]{1,0:T(8,128)(2,1)S(1)} copy-done((bf16[32,4096]{1,0:T(8,128)(2,1)S(1)}, bf16[32,4096]{1,0:T(8,128)(2,1)}, u32[]{:S(2)}) %copy-start.4) | copy-done | bytes 262168
  38.7 6.0 %near.1 = (bf16[288,32,128]{2,1,0:T(8,128)(2,1)S(1)}, f32[1664,32,128]{2,1,0:T(8,128)}) custom-call(s32[8,256]{1,0:T(8,128)S(1)} %get-tuple-element.10.lists_ref.lists_from, bf16[32,8,4096]{2,1,0:T(8,128)(2,1)S(1)} %copy-done.2, bf16[32,4096]{1,0:T(8,128)(2,1)S(1)} %copy-done.4, bf16[32,32,128]{2,1,0:T(8,128)(2,1)S(1)} %copy-done.1, ...), custom_call_target="tpu_custom_call" | custom-call | bytes 300000 | tf_op jit(solution)/shard_map/near/pallas_call | solution.py:368
  44.7 8.4 %all-to-all-done.1 = bf16[32,4,32,128]{3,2,1,0:T(8,128)(2,1)S(1)} async-done(((bf16[32,4,32,128]{3,2,1,0:T(8,128)(2,1)}), bf16[32,4,32,128]{3,2,1,0:T(8,128)(2,1)S(1)}, u32[]{:S(2)}, u32[]{:S(2)}) %all-to-all-start.1) | async-done | bytes 1048608 | tf_op jit(solution)/shard_map/all_to_all | solution.py:84
  53.1 3.7 %far.1 = bf16[32,16,1024]{2,1,0:T(8,128)(2,1)S(1)} custom-call(s32[8,256]{1,0:T(8,128)S(1)} %get-tuple-element.10.lists_ref.lists_from, bf16[288,32,128]{2,1,0:T(8,128)(2,1)S(1)} %get-tuple-element.11.work_ref, bf16[128,32,128]{2,1,0:T(8,128)(2,1)S(1)} %bitcast.10, f32[1664,32,128]{2,1,0:T(8,128)} %get-tuple-element.12.near_ref), custom_call_target="tpu_custom_call" | custom-call | bytes 18000000 | tf_op jit(solution)/shard_map/far/pallas_call | solution.py:384
  56.8 32.3 %all_to_all.15 = bf16[32,16,1024]{2,1,0:T(8,128)(2,1)S(1)} all-to-all(bf16[32,16,1024]{2,1,0:T(8,128)(2,1)S(1)} %far.1), channel_id=1, replica_groups={{31,30,29,28,27,26,25,24,23,22,21,20,19,18,17,16,15,14,13,12,11,10,9,8,..., dimensions={0} | all-to-all | bytes 2097152 | tf_op jit(solution)/shard_map/all_to_all | solution.py:84
  89.2 0.9 %holders.1 = f32[8,4096]{1,0:T(8,128)} custom-call(bf16[32,512]{1,0:T(8,128)(2,1)S(1)} %get-tuple-element.9.spread_ref, bf16[512,1024]{1,0:T(8,128)(2,1)S(1)} %bitcast.11), custom_call_target="tpu_custom_call" | custom-call | bytes 6000000 | tf_op jit(solution)/shard_map/holders/pallas_call | solution.py:399
Async XLA Ops:
  0.0 29.9 %copy-start.6 = (s32[32,8]{0,1:T(8,128)S(1)}, s32[32,8]{0,1:T(8,128)}, u32[]{:S(2)}) copy-start(s32[32,8]{0,1:T(8,128)} %param.9) | copy-start | bytes 3076
  0.0 29.9 %copy-start.7 = (s32[32]{0:T(128)S(1)}, s32[32]{0:T(128)}, u32[]{:S(2)}) copy-start(s32[32]{0:T(128)} %param.8) | copy-start | bytes 388
  0.0 29.9 %copy-start.5 = (s32[32,8]{0,1:T(8,128)S(1)}, s32[32,8]{0,1:T(8,128)}, u32[]{:S(2)}) copy-start(s32[32,8]{0,1:T(8,128)} %param.7) | copy-start | bytes 3076
  2.0 16.8 %all-to-all-start = ((s32[32,1,128]{2,1,0:T(1,128)}), s32[32,1,128]{2,1,0:T(1,128)S(1)}, u32[]{:S(2)}, u32[]{:S(2)}) async-start(s32[32,1,128]{2,1,0:T(1,128)} %bitcast.20), calls=%async_computation | async-start | bytes 32768 | tf_op jit(solution)/shard_map/all_to_all | solution.py:84
  13.9 1.0 %copy-start.3 = (bf16[32,4096]{1,0:T(8,128)(2,1)S(1)}, bf16[32,4096]{1,0:T(8,128)(2,1)}, u32[]{:S(2)}) copy-start(bf16[32,4096]{1,0:T(8,128)(2,1)} %p_ref.3) | copy-start | bytes 786436
  15.3 19.9 %copy-start = (bf16[32,32,128]{2,1,0:T(8,128)(2,1)}, bf16[32,32,128]{2,1,0:T(8,128)(2,1)S(1)}, u32[]{:S(2)}) copy-start(bf16[32,32,128]{2,1,0:T(8,128)(2,1)S(1)} %prepare.1.pq_ref) | copy-start | bytes 786436
  20.7 32.4 %all-to-all-start.1 = ((bf16[32,4,32,128]{3,2,1,0:T(8,128)(2,1)}), bf16[32,4,32,128]{3,2,1,0:T(8,128)(2,1)S(1)}, u32[]{:S(2)}, u32[]{:S(2)}) async-start(bf16[32,4,32,128]{3,2,1,0:T(8,128)(2,1)} %bitcast.6), calls=%async_computation.1 | async-start | bytes 2097152 | tf_op jit(solution)/shard_map/all_to_all | solution.py:84
  29.4 3.9 %collective-permute-start.1 = (bf16[32,32,128]{2,1,0:T(8,128)(2,1)S(1)}, bf16[32,32,128]{2,1,0:T(8,128)(2,1)S(1)}, u32[]{:S(2)}, u32[]{:S(2)}) collective-permute-start(bf16[32,32,128]{2,1,0:T(8,128)(2,1)S(1)} %prepare.1.pq_ref), channel_id=1, source_target_pairs={{32,0},{64,32},{96,64},{128,96},{160,128},{192,160},{224,192},{0,2... | collective-permute-start | bytes 786440 | tf_op jit(solution)/shard_map/ppermute | solution.py:352
  29.4 5.8 %collective-permute-start = (bf16[32,32,128]{2,1,0:T(8,128)(2,1)S(1)}, bf16[32,32,128]{2,1,0:T(8,128)(2,1)S(1)}, u32[]{:S(2)}, u32[]{:S(2)}) collective-permute-start(bf16[32,32,128]{2,1,0:T(8,128)(2,1)S(1)} %prepare.1.pq_ref), channel_id=1, source_target_pairs={{0,32},{32,64},{64,96},{96,128},{128,160},{160,192},{192,224},{224... | collective-permute-start | bytes 786440 | tf_op jit(solution)/shard_map/ppermute | solution.py:351
  35.2 1.0 %copy-start.1 = (bf16[32,32,128]{2,1,0:T(8,128)(2,1)S(1)}, bf16[32,32,128]{2,1,0:T(8,128)(2,1)}, u32[]{:S(2)}) copy-start(bf16[32,32,128]{2,1,0:T(8,128)(2,1)} %copy-done) | copy-start | bytes 786436
  36.2 1.6 %copy-start.2 = (bf16[32,8,4096]{2,1,0:T(8,128)(2,1)S(1)}, bf16[32,8,4096]{2,1,0:T(8,128)(2,1)}, u32[]{:S(2)}) copy-start(bf16[32,8,4096]{2,1,0:T(8,128)(2,1)} %a_ref.1) | copy-start | bytes 6291460
  37.8 0.9 %copy-start.4 = (bf16[32,4096]{1,0:T(8,128)(2,1)S(1)}, bf16[32,4096]{1,0:T(8,128)(2,1)}, u32[]{:S(2)}) copy-start(bf16[32,4096]{1,0:T(8,128)(2,1)} %p_ref.3) | copy-start | bytes 786436

commit v5 on v4

--- a/solution.py
+++ b/solution.py
@@ -13,6 +13,7 @@
 CAP = 4
 SLOT_DEV = 8
 CAP2 = 4
+COUNTS = 6
 STEPS = (64, 32)
 ASK, ROWS, SUMS = (tuple(reversed(range(32))),) * 3
 QUARTERS = 4
@@ -139,7 +140,8 @@
     entry = lane_of((per_row, rows)) * per_row + at_k
     before = ones(row_of((rows, rows)) < lane_of((rows, rows)))
     above = ones(lane_of((per_row, per_row)) < row_of((per_row, per_row)))
-    result = jnp.zeros((SLOT_DEV, entries), jnp.int32)
+    halves = entries // LANES
+    result = jnp.zeros((SLOT_DEV, LANES), jnp.int32)
     for which, mask in enumerate((live & ~far, live & far)):
         inside = dot(ones(mask), before, (1, 0))
         totals = jnp.sum(jnp.where(mask, 1.0, 0.0), axis=1, keepdims=True)
@@ -156,9 +158,11 @@
         code = placed[:1] * 65536 + placed[1:2] * 256 + placed[2:3]
         lanes = lane_of((1, entries))
         code = jnp.where(lanes < count, code, members * CAP2)
-        kind = row_of((SLOT_DEV, entries))
-        result = jnp.where(kind == which, code, result)
-        result = jnp.where(kind == 2 + which, count, result)
+        kind = row_of((SLOT_DEV, LANES))
+        for half in range(halves):
+            part = code[:, half * LANES : (half + 1) * LANES]
+            result = jnp.where(kind == which * halves + half, part, result)
+        result = jnp.where(kind == COUNTS + which, count, result)
     lists_ref[...] = result
 
 
@@ -225,9 +229,13 @@
     return [both[:PAIRS, :LANES], both[PAIRS:, LANES:]]
 
 
-def add_tiles(codes_ref, count, per_row, table_ref, pairs_ref, own_ref, total_ref):
+def add_tiles(lists_ref, which, per_row, table_ref, pairs_ref, own_ref, total_ref):
+    count = lists_ref[COUNTS + which, 0]
+    first = which * (pairs_ref.shape[0] // LANES)
+
     def step(start, group):
-        codes = [codes_ref[start + n] for n in range(group)]
+        row, lane = first + start // LANES, lax.rem(start, LANES)
+        codes = [lists_ref[row, lane + n] for n in range(group)]
         halves, tiles = [], []
         for n in range(0, group, 2):
             rights = [twice(table_ref[(code >> 8) & 255]) for code in codes[n : n + 2]]
@@ -254,7 +262,8 @@
     lax.fori_loop(0, (rest + small - 1) // small, one_small, 0)
 
 
-def views(work_ref, entries, per_row):
+def views(work_ref, per_row):
+    entries = work_ref.shape[0] // (per_row + 1) * per_row
     return work_ref.at[pl.ds(0, entries)], work_ref.at[pl.ds(entries, entries // per_row)]
 
 
@@ -268,13 +277,13 @@
 
 def near_kernel(per_row, lists_ref, a_ref, p_ref, pq_ref, low_ref, high_ref, work_ref, near_ref,
                 table, stage, own_stage, total_ref, sem):
-    pairs_ref, own_ref = views(work_ref, lists_ref.shape[1], per_row)
+    pairs_ref, own_ref = views(work_ref, per_row)
     relay(a_ref, p_ref, pairs_ref, own_ref, stage, own_stage)
     rows = pq_ref.shape[0]
     for at, ref in enumerate((pq_ref, low_ref, high_ref)):
         table[pl.ds(at * rows, rows)] = ref[...]
     clear(total_ref)
-    add_tiles(lists_ref.at[0], lists_ref[2, 0], per_row, table, pairs_ref, own_ref, total_ref)
+    add_tiles(lists_ref, 0, per_row, table, pairs_ref, own_ref, total_ref)
     sums = total_ref.shape[0] - 1
     copy = pltpu.make_async_copy(total_ref.at[pl.ds(0, sums)], near_ref.at[pl.ds(0, sums)], sem)
     copy.start()
@@ -290,10 +299,10 @@
     for copy in copies:
         copy.start()
     total[blocks] = jnp.zeros((PAIRS, LANES), F32)
-    pairs_ref, own_ref = views(work_ref, lists_ref.shape[1], per_row)
+    pairs_ref, own_ref = views(work_ref, per_row)
     for copy in copies:
         copy.wait()
-    add_tiles(lists_ref.at[1], lists_ref[3, 0], per_row, got_ref, pairs_ref, own_ref, total)
+    add_tiles(lists_ref, 1, per_row, got_ref, pairs_ref, own_ref, total)
     for member in range(out_ref.shape[0]):
         for at in range(PAIRS // QUARTERS):
             rows = total.at[pl.ds(member * CAP2, CAP2)].reshape(CAP2 * PAIRS, LANES)[
@@ -360,7 +369,7 @@
         functools.partial(lists_kernel, members, groups),
         "lists",
         [vmem] * 4,
-        (ints(SLOT_DEV, entries), jax.ShapeDtypeStruct((QUARTERS * SLOT_DEV, members * CAP2 * QUARTERS), BF16)),
+        (ints(SLOT_DEV, LANES), jax.ShapeDtypeStruct((QUARTERS * SLOT_DEV, members * CAP2 * QUARTERS), BF16)),
         [],
         0.1,
         (vmem, vmem),
@@ -388,7 +397,7 @@
         jax.ShapeDtypeStruct((members, CAP2 * QUARTERS, area // QUARTERS), BF16),
         [
             pltpu.VMEM((members * CAP2 + 1, PAIRS, LANES), F32),
-            pltpu.SMEM((SLOT_DEV, entries), jnp.int32),
+            pltpu.SMEM((SLOT_DEV, LANES), jnp.int32),
             pltpu.SemaphoreType.DMA((2,)),
         ],
         6,

time: 90.6 us -> 90.6 us (level)
  no operation moved by 1% of the time
where the time goes in v5:
time: 90.6 us; the launch traced here: 89.8 us
  blocking collectives  31.5 us (35%)
  starting transfers between devices  21.1 us (23%)
  Pallas kernels  16.8 us (19%)
  waiting for transfers between devices  15.8 us (17%)
  local copies, waits for them, and re-layouts  4.45 us (5%)
    all_to_all x1, blocking collectives, exchange(): lax.all_to_all(x, 'row', 0, 0, tiled=True, axis_index_groups=[list(order)])  31.5 us
    all_to_all x2, starting transfers between devices, exchange(): lax.all_to_all(x, 'row', 0, 0, tiled=True, axis_index_groups=[list(order)])  20.6 us
    all_to_all x2, waiting for transfers between devices, exchange(): lax.all_to_all(x, 'row', 0, 0, tiled=True, axis_index_groups=[list(order)])  11.9 us
    pallas_call x1, Pallas kernels, body(): call(functools.partial(near_kernel, per_row), 'near', [smem, vmem, vmem,...  5.96 us
    unnamed x16, local copies, waits for them, and re-layouts  4.45 us
    pallas_call x1, Pallas kernels, body(): call(functools.partial(far_kernel, per_row), 'far', [vmem, vmem, vmem, hb...  4.17 us
    pallas_call x1, Pallas kernels, body(): call(functools.partial(plan_kernel, members), 'plan', [vmem] * 3, ints(me...  1.96 us
    ppermute x1, waiting for transfers between devices, body(): lax.ppermute(pq, 'grp', [(target, source) for source, target in forward])  1.95 us
  transfers between devices with their start and end apart: 4, of which 4 were waited for; matrix products, arithmetic and copies ran while one was open for 0% of the time, Pallas kernels for 9%

profile of v5, /device:TPU:38, one launch (start us, length us, event | category | flops | bytes accessed | tf_op | source)
XLA Modules:
  0.0 89.8 jit_solution(12722339684565276651)
XLA Ops:
  0.0 0.0 copy-start.6
  0.0 0.0 copy-start.7
  0.0 0.0 copy-start.5
  0.0 2.0 %plan.1 = s32[32,128]{1,0:T(8,128)} custom-call(s32[8,32]{1,0:T(8,128)} %bitcast.14, s32[1,32]{1,0:T(1,128)} %bitcast.18, s32[8,32]{1,0:T(8,128)} %bitcast.16), custom_call_target="tpu_custom_call" | custom-call | bytes 6000000 | tf_op jit(solution)/shard_map/plan/pallas_call | solution.py:351
  2.0 11.9 %all-to-all-start = ((s32[32,1,128]{2,1,0:T(1,128)}), s32[32,1,128]{2,1,0:T(1,128)S(1)}, u32[]{:S(2)}, u32[]{:S(2)}) async-start(s32[32,1,128]{2,1,0:T(1,128)} %bitcast.20), calls=%async_computation | async-start | bytes 32768 | tf_op jit(solution)/shard_map/all_to_all | solution.py:85
  13.9 0.0 copy-start.3
  13.9 0.9 %copy-done.3 = bf16[32,4096]{1,0:T(8,128)(2,1)S(1)} copy-done((bf16[32,4096]{1,0:T(8,128)(2,1)S(1)}, bf16[32,4096]{1,0:T(8,128)(2,1)}, u32[]{:S(2)}) %copy-start.3) | copy-done | bytes 262168
  14.8 0.5 prepare.1.pq_ref
  15.3 0.0 copy-start
  15.3 3.5 %all-to-all-done = s32[32,1,128]{2,1,0:T(1,128)S(1)} async-done(((s32[32,1,128]{2,1,0:T(1,128)}), s32[32,1,128]{2,1,0:T(1,128)S(1)}, u32[]{:S(2)}, u32[]{:S(2)}) %all-to-all-start) | async-done | bytes 16416 | tf_op jit(solution)/shard_map/all_to_all | solution.py:85
  18.8 1.9 %pack.1 = bf16[128,32,128]{2,1,0:T(8,128)(2,1)} custom-call(s32[32,128]{1,0:T(8,128)S(1)} %bitcast.12, bf16[32,32,128]{2,1,0:T(8,128)(2,1)S(1)} %prepare.1.pq_ref), custom_call_target="tpu_custom_call" | custom-call | bytes 6000000 | tf_op jit(solution)/shard_map/pack/pallas_call | solution.py:363
  20.7 8.7 %all-to-all-start.1 = ((bf16[32,4,32,128]{3,2,1,0:T(8,128)(2,1)}), bf16[32,4,32,128]{3,2,1,0:T(8,128)(2,1)S(1)}, u32[]{:S(2)}, u32[]{:S(2)}) async-start(bf16[32,4,32,128]{3,2,1,0:T(8,128)(2,1)} %bitcast.6), calls=%async_computation.1 | async-start | bytes 2097152 | tf_op jit(solution)/shard_map/all_to_all | solution.py:85
  29.4 0.0 collective-permute-start.1
  29.4 0.5 collective-permute-start
  29.9 0.0 copy-done.6
  29.9 0.0 copy-done.7
  29.9 0.0 copy-done.5
  29.9 1.4 %lists.1 = (s32[8,128]{1,0:T(8,128)S(1)}, bf16[32,512]{1,0:T(8,128)(2,1)S(1)}) custom-call(s32[8,32]{1,0:T(8,128)S(1)} %bitcast.15, s32[1,32]{1,0:T(1,128)S(1)} %bitcast.19, s32[8,32]{1,0:T(8,128)S(1)} %bitcast.17, s32[32,128]{1,0:T(8,128)S(1)} %bitcast.13), custom_call_target="tpu_custom_call" | custom-call | bytes 300000 | tf_op jit(solution)/shard_map/lists/pallas_call | solution.py:368
  31.3 2.0 %collective-permute-done.1.high_ref = bf16[32,32,128]{2,1,0:T(8,128)(2,1)S(1)} collective-permute-done((bf16[32,32,128]{2,1,0:T(8,128)(2,1)S(1)}, bf16[32,32,128]{2,1,0:T(8,128)(2,1)S(1)}, u32[]{:S(2)}, u32[]{:S(2)}) %collective-permute-start.1) | collective-permute-done | bytes 262176 | tf_op jit(solution)/shard_map/ppermute | solution.py:361
  33.3 1.9 %collective-permute-done.low_ref = bf16[32,32,128]{2,1,0:T(8,128)(2,1)S(1)} collective-permute-done((bf16[32,32,128]{2,1,0:T(8,128)(2,1)S(1)}, bf16[32,32,128]{2,1,0:T(8,128)(2,1)S(1)}, u32[]{:S(2)}, u32[]{:S(2)}) %collective-permute-start) | collective-permute-done | bytes 262176 | tf_op jit(solution)/shard_map/ppermute | solution.py:360
  35.2 0.0 copy-done
  35.2 0.0 copy-start.1
  35.2 0.9 %copy-done.1 = bf16[32,32,128]{2,1,0:T(8,128)(2,1)S(1)} copy-done((bf16[32,32,128]{2,1,0:T(8,128)(2,1)S(1)}, bf16[32,32,128]{2,1,0:T(8,128)(2,1)}, u32[]{:S(2)}) %copy-start.1) | copy-done | bytes 262168
  36.2 0.0 copy-start.2
  36.2 1.6 %copy-done.2 = bf16[32,8,4096]{2,1,0:T(8,128)(2,1)S(1)} copy-done((bf16[32,8,4096]{2,1,0:T(8,128)(2,1)S(1)}, bf16[32,8,4096]{2,1,0:T(8,128)(2,1)}, u32[]{:S(2)}) %copy-start.2) | copy-done | bytes 2097176
  37.8 0.0 copy-start.4
  37.8 0.9 %copy-done.4 = bf16[32,4096]{1,0:T(8,128)(2,1)S(1)} copy-done((bf16[32,4096]{1,0:T(8,128)(2,1)S(1)}, bf16[32,4096]{1,0:T(8,128)(2,1)}, u32[]{:S(2)}) %copy-start.4) | copy-done | bytes 262168
  38.7 6.0 %near.1 = (bf16[288,32,128]{2,1,0:T(8,128)(2,1)S(1)}, f32[1664,32,128]{2,1,0:T(8,128)}) custom-call(s32[8,128]{1,0:T(8,128)S(1)} %get-tuple-element.10.lists_ref.lists_from, bf16[32,8,4096]{2,1,0:T(8,128)(2,1)S(1)} %copy-done.2, bf16[32,4096]{1,0:T(8,128)(2,1)S(1)} %copy-done.4, bf16[32,32,128]{2,1,0:T(8,128)(2,1)S(1)} %copy-done.1, ...), custom_call_target="tpu_custom_call" | custom-call | bytes 300000 | tf_op jit(solution)/shard_map/near/pallas_call | solution.py:377
  44.7 8.4 %all-to-all-done.1 = bf16[32,4,32,128]{3,2,1,0:T(8,128)(2,1)S(1)} async-done(((bf16[32,4,32,128]{3,2,1,0:T(8,128)(2,1)}), bf16[32,4,32,128]{3,2,1,0:T(8,128)(2,1)S(1)}, u32[]{:S(2)}, u32[]{:S(2)}) %all-to-all-start.1) | async-done | bytes 1048608 | tf_op jit(solution)/shard_map/all_to_all | solution.py:85
  53.1 4.2 %far.1 = bf16[32,16,1024]{2,1,0:T(8,128)(2,1)S(1)} custom-call(s32[8,128]{1,0:T(8,128)S(1)} %get-tuple-element.10.lists_ref.lists_from, bf16[288,32,128]{2,1,0:T(8,128)(2,1)S(1)} %get-tuple-element.11.work_ref, bf16[128,32,128]{2,1,0:T(8,128)(2,1)S(1)} %bitcast.10, f32[1664,32,128]{2,1,0:T(8,128)} %get-tuple-element.12.near_ref), custom_call_target="tpu_custom_call" | custom-call | bytes 18000000 | tf_op jit(solution)/shard_map/far/pallas_call | solution.py:393
  57.3 31.5 %all_to_all.15 = bf16[32,16,1024]{2,1,0:T(8,128)(2,1)S(1)} all-to-all(bf16[32,16,1024]{2,1,0:T(8,128)(2,1)S(1)} %far.1), channel_id=1, replica_groups={{31,30,29,28,27,26,25,24,23,22,21,20,19,18,17,16,15,14,13,12,11,10,9,8,..., dimensions={0} | all-to-all | bytes 2097152 | tf_op jit(solution)/shard_map/all_to_all | solution.py:85
  88.8 0.9 %holders.1 = f32[8,4096]{1,0:T(8,128)} custom-call(bf16[32,512]{1,0:T(8,128)(2,1)S(1)} %get-tuple-element.9.spread_ref, bf16[512,1024]{1,0:T(8,128)(2,1)S(1)} %bitcast.11), custom_call_target="tpu_custom_call" | custom-call | bytes 6000000 | tf_op jit(solution)/shard_map/holders/pallas_call | solution.py:408
Async XLA Ops:
  0.0 29.9 %copy-start.6 = (s32[32,8]{0,1:T(8,128)S(1)}, s32[32,8]{0,1:T(8,128)}, u32[]{:S(2)}) copy-start(s32[32,8]{0,1:T(8,128)} %param.9) | copy-start | bytes 3076
  0.0 29.9 %copy-start.7 = (s32[32]{0:T(128)S(1)}, s32[32]{0:T(128)}, u32[]{:S(2)}) copy-start(s32[32]{0:T(128)} %param.8) | copy-start | bytes 388
  0.0 29.9 %copy-start.5 = (s32[32,8]{0,1:T(8,128)S(1)}, s32[32,8]{0,1:T(8,128)}, u32[]{:S(2)}) copy-start(s32[32,8]{0,1:T(8,128)} %param.7) | copy-start | bytes 3076
  2.0 16.8 %all-to-all-start = ((s32[32,1,128]{2,1,0:T(1,128)}), s32[32,1,128]{2,1,0:T(1,128)S(1)}, u32[]{:S(2)}, u32[]{:S(2)}) async-start(s32[32,1,128]{2,1,0:T(1,128)} %bitcast.20), calls=%async_computation | async-start | bytes 32768 | tf_op jit(solution)/shard_map/all_to_all | solution.py:85
  13.9 1.0 %copy-start.3 = (bf16[32,4096]{1,0:T(8,128)(2,1)S(1)}, bf16[32,4096]{1,0:T(8,128)(2,1)}, u32[]{:S(2)}) copy-start(bf16[32,4096]{1,0:T(8,128)(2,1)} %p_ref.3) | copy-start | bytes 786436
  15.3 19.9 %copy-start = (bf16[32,32,128]{2,1,0:T(8,128)(2,1)}, bf16[32,32,128]{2,1,0:T(8,128)(2,1)S(1)}, u32[]{:S(2)}) copy-start(bf16[32,32,128]{2,1,0:T(8,128)(2,1)S(1)} %prepare.1.pq_ref) | copy-start | bytes 786436
  20.7 32.4 %all-to-all-start.1 = ((bf16[32,4,32,128]{3,2,1,0:T(8,128)(2,1)}), bf16[32,4,32,128]{3,2,1,0:T(8,128)(2,1)S(1)}, u32[]{:S(2)}, u32[]{:S(2)}) async-start(bf16[32,4,32,128]{3,2,1,0:T(8,128)(2,1)} %bitcast.6), calls=%async_computation.1 | async-start | bytes 2097152 | tf_op jit(solution)/shard_map/all_to_all | solution.py:85
  29.4 3.9 %collective-permute-start.1 = (bf16[32,32,128]{2,1,0:T(8,128)(2,1)S(1)}, bf16[32,32,128]{2,1,0:T(8,128)(2,1)S(1)}, u32[]{:S(2)}, u32[]{:S(2)}) collective-permute-start(bf16[32,32,128]{2,1,0:T(8,128)(2,1)S(1)} %prepare.1.pq_ref), channel_id=1, source_target_pairs={{32,0},{64,32},{96,64},{128,96},{160,128},{192,160},{224,192},{0,2... | collective-permute-start | bytes 786440 | tf_op jit(solution)/shard_map/ppermute | solution.py:361
  29.4 5.8 %collective-permute-start = (bf16[32,32,128]{2,1,0:T(8,128)(2,1)S(1)}, bf16[32,32,128]{2,1,0:T(8,128)(2,1)S(1)}, u32[]{:S(2)}, u32[]{:S(2)}) collective-permute-start(bf16[32,32,128]{2,1,0:T(8,128)(2,1)S(1)} %prepare.1.pq_ref), channel_id=1, source_target_pairs={{0,32},{32,64},{64,96},{96,128},{128,160},{160,192},{192,224},{224... | collective-permute-start | bytes 786440 | tf_op jit(solution)/shard_map/ppermute | solution.py:360
  35.2 1.0 %copy-start.1 = (bf16[32,32,128]{2,1,0:T(8,128)(2,1)S(1)}, bf16[32,32,128]{2,1,0:T(8,128)(2,1)}, u32[]{:S(2)}) copy-start(bf16[32,32,128]{2,1,0:T(8,128)(2,1)} %copy-done) | copy-start | bytes 786436
  36.2 1.6 %copy-start.2 = (bf16[32,8,4096]{2,1,0:T(8,128)(2,1)S(1)}, bf16[32,8,4096]{2,1,0:T(8,128)(2,1)}, u32[]{:S(2)}) copy-start(bf16[32,8,4096]{2,1,0:T(8,128)(2,1)} %a_ref.1) | copy-start | bytes 6291460
  37.8 0.9 %copy-start.4 = (bf16[32,4096]{1,0:T(8,128)(2,1)S(1)}, bf16[32,4096]{1,0:T(8,128)(2,1)}, u32[]{:S(2)}) copy-start(bf16[32,4096]{1,0:T(8,128)(2,1)} %p_ref.3) | copy-start | bytes 786436

commit v6 on v5

--- a/solution.py
+++ b/solution.py
@@ -15,7 +15,8 @@
 CAP2 = 4
 COUNTS = 6
 STEPS = (64, 32)
-ASK, ROWS, SUMS = (tuple(reversed(range(32))),) * 3
+ASK = SUMS = tuple(reversed(range(32)))
+ROWS = tuple(range(32))
 QUARTERS = 4
 VMEM_LIMIT = 12 * 1024 * 1024
 WIDE_LIMIT = 40 * 1024 * 1024

time: 90.6 us -> 90.2 us (level)
  waiting for transfers between devices: 15.8 us -> 18.1 us
  starting transfers between devices: 21.1 us -> 19.5 us
    all_to_all x2, waiting for transfers between devices: 11.9 us -> 14.2 us  [exchange(): lax.all_to_all(x, 'row', 0, 0, tiled=True, axis_index_groups=[list(order)])]
    all_to_all x2, starting transfers between devices: 20.6 us -> 19 us  [exchange(): lax.all_to_all(x, 'row', 0, 0, tiled=True, axis_index_groups=[list(order)])]
    all_to_all x1, blocking collectives: 31.5 us -> 30.6 us  [exchange(): lax.all_to_all(x, 'row', 0, 0, tiled=True, axis_index_groups=[list(order)])]
where the time goes in v6:
time: 90.2 us; the launch traced here: 89.5 us
  blocking collectives  30.6 us (34%)
  starting transfers between devices  19.5 us (22%)
  waiting for transfers between devices  18.1 us (20%)
  Pallas kernels  16.8 us (19%)
  local copies, waits for them, and re-layouts  4.45 us (5%)
    all_to_all x1, blocking collectives, exchange(): lax.all_to_all(x, 'row', 0, 0, tiled=True, axis_index_groups=[list(order)])  30.6 us
    all_to_all x2, starting transfers between devices, exchange(): lax.all_to_all(x, 'row', 0, 0, tiled=True, axis_index_groups=[list(order)])  19 us
    all_to_all x2, waiting for transfers between devices, exchange(): lax.all_to_all(x, 'row', 0, 0, tiled=True, axis_index_groups=[list(order)])  14.2 us
    pallas_call x1, Pallas kernels, body(): call(functools.partial(near_kernel, per_row), 'near', [smem, vmem, vmem,...  5.96 us
    unnamed x16, local copies, waits for them, and re-layouts  4.45 us
    pallas_call x1, Pallas kernels, body(): call(functools.partial(far_kernel, per_row), 'far', [vmem, vmem, vmem, hb...  4.19 us
    pallas_call x1, Pallas kernels, body(): call(functools.partial(plan_kernel, members), 'plan', [vmem] * 3, ints(me...  1.96 us
    ppermute x1, waiting for transfers between devices, body(): lax.ppermute(pq, 'grp', [(target, source) for source, target in forward])  1.95 us
  transfers between devices with their start and end apart: 4, of which 4 were waited for; matrix products, arithmetic and copies ran while one was open for 0% of the time, Pallas kernels for 9%

profile of v6, /device:TPU:38, one launch (start us, length us, event | category | flops | bytes accessed | tf_op | source)
XLA Modules:
  0.0 89.5 jit_solution(12277772462604182932)
XLA Ops:
  0.0 0.0 copy-start.6
  0.0 0.0 copy-start.7
  0.0 0.0 copy-start.5
  0.0 2.0 %plan.1 = s32[32,128]{1,0:T(8,128)} custom-call(s32[8,32]{1,0:T(8,128)} %bitcast.14, s32[1,32]{1,0:T(1,128)} %bitcast.18, s32[8,32]{1,0:T(8,128)} %bitcast.16), custom_call_target="tpu_custom_call" | custom-call | bytes 6000000 | tf_op jit(solution)/shard_map/plan/pallas_call | solution.py:352
  2.0 11.9 %all-to-all-start = ((s32[32,1,128]{2,1,0:T(1,128)}), s32[32,1,128]{2,1,0:T(1,128)S(1)}, u32[]{:S(2)}, u32[]{:S(2)}) async-start(s32[32,1,128]{2,1,0:T(1,128)} %bitcast.20), calls=%async_computation | async-start | bytes 32768 | tf_op jit(solution)/shard_map/all_to_all | solution.py:86
  13.9 0.0 copy-start.3
  13.9 0.9 %copy-done.3 = bf16[32,4096]{1,0:T(8,128)(2,1)S(1)} copy-done((bf16[32,4096]{1,0:T(8,128)(2,1)S(1)}, bf16[32,4096]{1,0:T(8,128)(2,1)}, u32[]{:S(2)}) %copy-start.3) | copy-done | bytes 262168
  14.8 0.5 prepare.1.pq_ref
  15.3 0.0 copy-start
  15.3 3.5 %all-to-all-done = s32[32,1,128]{2,1,0:T(1,128)S(1)} async-done(((s32[32,1,128]{2,1,0:T(1,128)}), s32[32,1,128]{2,1,0:T(1,128)S(1)}, u32[]{:S(2)}, u32[]{:S(2)}) %all-to-all-start) | async-done | bytes 16416 | tf_op jit(solution)/shard_map/all_to_all | solution.py:86
  18.8 1.9 %pack.1 = bf16[128,32,128]{2,1,0:T(8,128)(2,1)} custom-call(s32[32,128]{1,0:T(8,128)S(1)} %bitcast.12, bf16[32,32,128]{2,1,0:T(8,128)(2,1)S(1)} %prepare.1.pq_ref), custom_call_target="tpu_custom_call" | custom-call | bytes 6000000 | tf_op jit(solution)/shard_map/pack/pallas_call | solution.py:364
  20.7 7.1 %all-to-all-start.1 = ((bf16[32,4,32,128]{3,2,1,0:T(8,128)(2,1)}), bf16[32,4,32,128]{3,2,1,0:T(8,128)(2,1)S(1)}, u32[]{:S(2)}, u32[]{:S(2)}) async-start(bf16[32,4,32,128]{3,2,1,0:T(8,128)(2,1)} %bitcast.6), calls=%async_computation.1 | async-start | bytes 2097152 | tf_op jit(solution)/shard_map/all_to_all | solution.py:86
  27.7 0.0 collective-permute-start.1
  27.8 0.5 collective-permute-start
  28.3 0.0 copy-done.6
  28.3 0.0 copy-done.7
  28.3 0.0 copy-done.5
  28.3 1.4 %lists.1 = (s32[8,128]{1,0:T(8,128)S(1)}, bf16[32,512]{1,0:T(8,128)(2,1)S(1)}) custom-call(s32[8,32]{1,0:T(8,128)S(1)} %bitcast.15, s32[1,32]{1,0:T(1,128)S(1)} %bitcast.19, s32[8,32]{1,0:T(8,128)S(1)} %bitcast.17, s32[32,128]{1,0:T(8,128)S(1)} %bitcast.13), custom_call_target="tpu_custom_call" | custom-call | bytes 300000 | tf_op jit(solution)/shard_map/lists/pallas_call | solution.py:369
  29.7 2.0 %collective-permute-done.1.high_ref = bf16[32,32,128]{2,1,0:T(8,128)(2,1)S(1)} collective-permute-done((bf16[32,32,128]{2,1,0:T(8,128)(2,1)S(1)}, bf16[32,32,128]{2,1,0:T(8,128)(2,1)S(1)}, u32[]{:S(2)}, u32[]{:S(2)}) %collective-permute-start.1) | collective-permute-done | bytes 262176 | tf_op jit(solution)/shard_map/ppermute | solution.py:362
  31.7 1.9 %collective-permute-done.low_ref = bf16[32,32,128]{2,1,0:T(8,128)(2,1)S(1)} collective-permute-done((bf16[32,32,128]{2,1,0:T(8,128)(2,1)S(1)}, bf16[32,32,128]{2,1,0:T(8,128)(2,1)S(1)}, u32[]{:S(2)}, u32[]{:S(2)}) %collective-permute-start) | collective-permute-done | bytes 262176 | tf_op jit(solution)/shard_map/ppermute | solution.py:361
  33.6 0.0 copy-done
  33.6 0.0 copy-start.1
  33.6 0.9 %copy-done.1 = bf16[32,32,128]{2,1,0:T(8,128)(2,1)S(1)} copy-done((bf16[32,32,128]{2,1,0:T(8,128)(2,1)S(1)}, bf16[32,32,128]{2,1,0:T(8,128)(2,1)}, u32[]{:S(2)}) %copy-start.1) | copy-done | bytes 262168
  34.5 0.0 copy-start.2
  34.5 1.6 %copy-done.2 = bf16[32,8,4096]{2,1,0:T(8,128)(2,1)S(1)} copy-done((bf16[32,8,4096]{2,1,0:T(8,128)(2,1)S(1)}, bf16[32,8,4096]{2,1,0:T(8,128)(2,1)}, u32[]{:S(2)}) %copy-start.2) | copy-done | bytes 2097176
  36.1 0.0 copy-start.4
  36.1 0.9 %copy-done.4 = bf16[32,4096]{1,0:T(8,128)(2,1)S(1)} copy-done((bf16[32,4096]{1,0:T(8,128)(2,1)S(1)}, bf16[32,4096]{1,0:T(8,128)(2,1)}, u32[]{:S(2)}) %copy-start.4) | copy-done | bytes 262168
  37.1 6.0 %near.1 = (bf16[288,32,128]{2,1,0:T(8,128)(2,1)S(1)}, f32[1664,32,128]{2,1,0:T(8,128)}) custom-call(s32[8,128]{1,0:T(8,128)S(1)} %get-tuple-element.10.lists_ref.lists_from, bf16[32,8,4096]{2,1,0:T(8,128)(2,1)S(1)} %copy-done.2, bf16[32,4096]{1,0:T(8,128)(2,1)S(1)} %copy-done.4, bf16[32,32,128]{2,1,0:T(8,128)(2,1)S(1)} %copy-done.1, ...), custom_call_target="tpu_custom_call" | custom-call | bytes 300000 | tf_op jit(solution)/shard_map/near/pallas_call | solution.py:378
  43.0 10.8 %all-to-all-done.1 = bf16[32,4,32,128]{3,2,1,0:T(8,128)(2,1)S(1)} async-done(((bf16[32,4,32,128]{3,2,1,0:T(8,128)(2,1)}), bf16[32,4,32,128]{3,2,1,0:T(8,128)(2,1)S(1)}, u32[]{:S(2)}, u32[]{:S(2)}) %all-to-all-start.1) | async-done | bytes 1048608 | tf_op jit(solution)/shard_map/all_to_all | solution.py:86
  53.8 4.2 %far.1 = bf16[32,16,1024]{2,1,0:T(8,128)(2,1)S(1)} custom-call(s32[8,128]{1,0:T(8,128)S(1)} %get-tuple-element.10.lists_ref.lists_from, bf16[288,32,128]{2,1,0:T(8,128)(2,1)S(1)} %get-tuple-element.11.work_ref, bf16[128,32,128]{2,1,0:T(8,128)(2,1)S(1)} %bitcast.10, f32[1664,32,128]{2,1,0:T(8,128)} %get-tuple-element.12.near_ref), custom_call_target="tpu_custom_call" | custom-call | bytes 18000000 | tf_op jit(solution)/shard_map/far/pallas_call | solution.py:394
  58.0 30.6 %all_to_all.15 = bf16[32,16,1024]{2,1,0:T(8,128)(2,1)S(1)} all-to-all(bf16[32,16,1024]{2,1,0:T(8,128)(2,1)S(1)} %far.1), channel_id=1, replica_groups={{31,30,29,28,27,26,25,24,23,22,21,20,19,18,17,16,15,14,13,12,11,10,9,8,..., dimensions={0} | all-to-all | bytes 2097152 | tf_op jit(solution)/shard_map/all_to_all | solution.py:86
  88.6 0.9 %holders.1 = f32[8,4096]{1,0:T(8,128)} custom-call(bf16[32,512]{1,0:T(8,128)(2,1)S(1)} %get-tuple-element.9.spread_ref, bf16[512,1024]{1,0:T(8,128)(2,1)S(1)} %bitcast.11), custom_call_target="tpu_custom_call" | custom-call | bytes 6000000 | tf_op jit(solution)/shard_map/holders/pallas_call | solution.py:409
Async XLA Ops:
  0.0 28.3 %copy-start.6 = (s32[32,8]{0,1:T(8,128)S(1)}, s32[32,8]{0,1:T(8,128)}, u32[]{:S(2)}) copy-start(s32[32,8]{0,1:T(8,128)} %param.9) | copy-start | bytes 3076
  0.0 28.3 %copy-start.7 = (s32[32]{0:T(128)S(1)}, s32[32]{0:T(128)}, u32[]{:S(2)}) copy-start(s32[32]{0:T(128)} %param.8) | copy-start | bytes 388
  0.0 28.3 %copy-start.5 = (s32[32,8]{0,1:T(8,128)S(1)}, s32[32,8]{0,1:T(8,128)}, u32[]{:S(2)}) copy-start(s32[32,8]{0,1:T(8,128)} %param.7) | copy-start | bytes 3076
  2.0 16.8 %all-to-all-start = ((s32[32,1,128]{2,1,0:T(1,128)}), s32[32,1,128]{2,1,0:T(1,128)S(1)}, u32[]{:S(2)}, u32[]{:S(2)}) async-start(s32[32,1,128]{2,1,0:T(1,128)} %bitcast.20), calls=%async_computation | async-start | bytes 32768 | tf_op jit(solution)/shard_map/all_to_all | solution.py:86
  13.9 1.0 %copy-start.3 = (bf16[32,4096]{1,0:T(8,128)(2,1)S(1)}, bf16[32,4096]{1,0:T(8,128)(2,1)}, u32[]{:S(2)}) copy-start(bf16[32,4096]{1,0:T(8,128)(2,1)} %p_ref.3) | copy-start | bytes 786436
  15.3 18.3 %copy-start = (bf16[32,32,128]{2,1,0:T(8,128)(2,1)}, bf16[32,32,128]{2,1,0:T(8,128)(2,1)S(1)}, u32[]{:S(2)}) copy-start(bf16[32,32,128]{2,1,0:T(8,128)(2,1)S(1)} %prepare.1.pq_ref) | copy-start | bytes 786436
  20.7 33.1 %all-to-all-start.1 = ((bf16[32,4,32,128]{3,2,1,0:T(8,128)(2,1)}), bf16[32,4,32,128]{3,2,1,0:T(8,128)(2,1)S(1)}, u32[]{:S(2)}, u32[]{:S(2)}) async-start(bf16[32,4,32,128]{3,2,1,0:T(8,128)(2,1)} %bitcast.6), calls=%async_computation.1 | async-start | bytes 2097152 | tf_op jit(solution)/shard_map/all_to_all | solution.py:86
  27.7 3.9 %collective-permute-start.1 = (bf16[32,32,128]{2,1,0:T(8,128)(2,1)S(1)}, bf16[32,32,128]{2,1,0:T(8,128)(2,1)S(1)}, u32[]{:S(2)}, u32[]{:S(2)}) collective-permute-start(bf16[32,32,128]{2,1,0:T(8,128)(2,1)S(1)} %prepare.1.pq_ref), channel_id=1, source_target_pairs={{32,0},{64,32},{96,64},{128,96},{160,128},{192,160},{224,192},{0,2... | collective-permute-start | bytes 786440 | tf_op jit(solution)/shard_map/ppermute | solution.py:362
  27.8 5.8 %collective-permute-start = (bf16[32,32,128]{2,1,0:T(8,128)(2,1)S(1)}, bf16[32,32,128]{2,1,0:T(8,128)(2,1)S(1)}, u32[]{:S(2)}, u32[]{:S(2)}) collective-permute-start(bf16[32,32,128]{2,1,0:T(8,128)(2,1)S(1)} %prepare.1.pq_ref), channel_id=1, source_target_pairs={{0,32},{32,64},{64,96},{96,128},{128,160},{160,192},{192,224},{224... | collective-permute-start | bytes 786440 | tf_op jit(solution)/shard_map/ppermute | solution.py:361
  33.6 1.0 %copy-start.1 = (bf16[32,32,128]{2,1,0:T(8,128)(2,1)S(1)}, bf16[32,32,128]{2,1,0:T(8,128)(2,1)}, u32[]{:S(2)}) copy-start(bf16[32,32,128]{2,1,0:T(8,128)(2,1)} %copy-done) | copy-start | bytes 786436
  34.5 1.6 %copy-start.2 = (bf16[32,8,4096]{2,1,0:T(8,128)(2,1)S(1)}, bf16[32,8,4096]{2,1,0:T(8,128)(2,1)}, u32[]{:S(2)}) copy-start(bf16[32,8,4096]{2,1,0:T(8,128)(2,1)} %a_ref.1) | copy-start | bytes 6291460
  36.1 0.9 %copy-start.4 = (bf16[32,4096]{1,0:T(8,128)(2,1)S(1)}, bf16[32,4096]{1,0:T(8,128)(2,1)}, u32[]{:S(2)}) copy-start(bf16[32,4096]{1,0:T(8,128)(2,1)} %p_ref.3) | copy-start | bytes 786436

commit v7 on v6

--- a/solution.py
+++ b/solution.py
@@ -17,6 +17,7 @@
 STEPS = (64, 32)
 ASK = SUMS = tuple(reversed(range(32)))
 ROWS = tuple(range(32))
+PARTS = 4
 QUARTERS = 4
 VMEM_LIMIT = 12 * 1024 * 1024
 WIDE_LIMIT = 40 * 1024 * 1024
@@ -312,10 +313,22 @@
             out_ref[member, :, at * LANES : (at + 1) * LANES] = rows.astype(BF16)
 
 
-def pack_kernel(members, asked_ref, pq_ref, out_ref):
-    for at in range(members):
-        for s in range(CAP):
-            out_ref[at * CAP + s] = pq_ref[asked_ref[ASK.index(ROWS[at]), s]]
+def pack_kernel(members, asked_from, pq_ref, out_ref, asked_ref, sem):
+    share = members // PARTS
+    copies = [
+        pltpu.make_async_copy(
+            asked_from.at[pl.ds(n * share, share)], asked_ref.at[pl.ds(n * share, share)], sem.at[n]
+        )
+        for n in range(PARTS)
+    ]
+    for copy in copies:
+        copy.start()
+    for n, copy in enumerate(copies):
+        copy.wait()
+        for row in range(n * share, (n + 1) * share):
+            at = ROWS.index(ASK[row])
+            for s in range(CAP):
+                out_ref[at * CAP + s] = pq_ref[asked_ref[row, s]]
 
 
 def sum_kernel(spread_ref, got_ref, out_ref):
@@ -355,14 +368,15 @@
     asked = exchange(want.reshape(members, 1, LANES), ASK).reshape(members, LANES)
 
     pq = call(
-        prepare_kernel, "prepare", [vmem], blocks(rows), [pltpu.VMEM((PAIRS * rows, LANES), F32)], 0.1
+        prepare_kernel, "prepare", [vmem], blocks(rows), [pltpu.VMEM(((PAIRS + 1) * rows, LANES), F32)], 0.1
     )(p_blocks)
     forward = [(i, (i + 1) % groups) for i in range(groups)]
     low = lax.ppermute(pq, "grp", forward)
     high = lax.ppermute(pq, "grp", [(target, source) for source, target in forward])
 
     send = call(
-        functools.partial(pack_kernel, members), "pack", [smem, vmem], blocks(members * CAP), [], 2
+        functools.partial(pack_kernel, members), "pack", [vmem, vmem], blocks(members * CAP),
+        [pltpu.SMEM((members, LANES), jnp.int32), pltpu.SemaphoreType.DMA((PARTS,))], 2
     )(asked, pq)
     got = exchange(send.reshape(members, CAP, PAIRS, LANES), ROWS).reshape(members * CAP, PAIRS, LANES)
 
@@ -382,8 +396,8 @@
         (blocks(entries + rows), blocks(SPARE, F32)),
         [
             pltpu.VMEM((3 * rows, PAIRS, LANES), BF16),
-            pltpu.VMEM((2, PAIRS * per_row, LANES), F32),
-            pltpu.VMEM((PAIRS * rows, LANES), F32),
+            pltpu.VMEM((2, (PAIRS + 1) * per_row, LANES), F32),
+            pltpu.VMEM(((PAIRS + 1) * rows, LANES), F32),
             pltpu.VMEM((members * CAP2 + 1, PAIRS, LANES), F32),
             pltpu.SemaphoreType.DMA,
         ],

time: 90.2 us -> 90.1 us (level)
  no operation moved by 1% of the time
where the time goes in v7:
time: 90.1 us; the launch traced here: 89.4 us
  blocking collectives  30.9 us (34%)
  starting transfers between devices  19.5 us (22%)
  waiting for transfers between devices  18.1 us (20%)
  Pallas kernels  16.4 us (18%)
  local copies, waits for them, and re-layouts  4.45 us (5%)
    all_to_all x1, blocking collectives, exchange(): lax.all_to_all(x, 'row', 0, 0, tiled=True, axis_index_groups=[list(order)])  30.9 us
    all_to_all x2, starting transfers between devices, exchange(): lax.all_to_all(x, 'row', 0, 0, tiled=True, axis_index_groups=[list(order)])  19 us
    all_to_all x2, waiting for transfers between devices, exchange(): lax.all_to_all(x, 'row', 0, 0, tiled=True, axis_index_groups=[list(order)])  14.2 us
    pallas_call x1, Pallas kernels, body(): call(functools.partial(near_kernel, per_row), 'near', [smem, vmem, vmem,...  5.97 us
    unnamed x16, local copies, waits for them, and re-layouts  4.45 us
    pallas_call x1, Pallas kernels, body(): call(functools.partial(far_kernel, per_row), 'far', [vmem, vmem, vmem, hb...  3.77 us
    pallas_call x1, Pallas kernels, body(): call(functools.partial(plan_kernel, members), 'plan', [vmem] * 3, ints(me...  1.96 us
    ppermute x1, waiting for transfers between devices, body(): lax.ppermute(pq, 'grp', [(target, source) for source, target in forward])  1.95 us
  transfers between devices with their start and end apart: 4, of which 4 were waited for; matrix products, arithmetic and copies ran while one was open for 0% of the time, Pallas kernels for 9%

profile of v7, /device:TPU:38, one launch (start us, length us, event | category | flops | bytes accessed | tf_op | source)
XLA Modules:
  0.0 89.4 jit_solution(14956123959694383534)
XLA Ops:
  0.0 0.0 copy-start.6
  0.0 0.0 copy-start.7
  0.0 0.0 copy-start.5
  0.0 2.0 %plan.1 = s32[32,128]{1,0:T(8,128)} custom-call(s32[8,32]{1,0:T(8,128)} %bitcast.14, s32[1,32]{1,0:T(1,128)} %bitcast.18, s32[8,32]{1,0:T(8,128)} %bitcast.16), custom_call_target="tpu_custom_call" | custom-call | bytes 6000000 | tf_op jit(solution)/shard_map/plan/pallas_call | solution.py:365
  2.0 11.9 %all-to-all-start = ((s32[32,1,128]{2,1,0:T(1,128)}), s32[32,1,128]{2,1,0:T(1,128)S(1)}, u32[]{:S(2)}, u32[]{:S(2)}) async-start(s32[32,1,128]{2,1,0:T(1,128)} %bitcast.20), calls=%async_computation | async-start | bytes 32768 | tf_op jit(solution)/shard_map/all_to_all | solution.py:87
  13.9 0.0 copy-start.3
  13.9 0.9 %copy-done.3 = bf16[32,4096]{1,0:T(8,128)(2,1)S(1)} copy-done((bf16[32,4096]{1,0:T(8,128)(2,1)S(1)}, bf16[32,4096]{1,0:T(8,128)(2,1)}, u32[]{:S(2)}) %copy-start.3) | copy-done | bytes 262168
  14.8 0.5 prepare.1.pq_ref
  15.3 0.0 copy-start
  15.3 3.5 %all-to-all-done = s32[32,1,128]{2,1,0:T(1,128)S(1)} async-done(((s32[32,1,128]{2,1,0:T(1,128)}), s32[32,1,128]{2,1,0:T(1,128)S(1)}, u32[]{:S(2)}, u32[]{:S(2)}) %all-to-all-start) | async-done | bytes 16416 | tf_op jit(solution)/shard_map/all_to_all | solution.py:87
  18.8 1.8 %pack.1 = bf16[128,32,128]{2,1,0:T(8,128)(2,1)} custom-call(s32[32,128]{1,0:T(8,128)S(1)} %bitcast.12, bf16[32,32,128]{2,1,0:T(8,128)(2,1)S(1)} %prepare.1.pq_ref), custom_call_target="tpu_custom_call" | custom-call | bytes 6000000 | tf_op jit(solution)/shard_map/pack/pallas_call | solution.py:377
  20.6 7.1 %all-to-all-start.1 = ((bf16[32,4,32,128]{3,2,1,0:T(8,128)(2,1)}), bf16[32,4,32,128]{3,2,1,0:T(8,128)(2,1)S(1)}, u32[]{:S(2)}, u32[]{:S(2)}) async-start(bf16[32,4,32,128]{3,2,1,0:T(8,128)(2,1)} %bitcast.6), calls=%async_computation.1 | async-start | bytes 2097152 | tf_op jit(solution)/shard_map/all_to_all | solution.py:87
  27.7 0.0 collective-permute-start.1
  27.7 0.5 collective-permute-start
  28.2 0.0 copy-done.6
  28.2 0.0 copy-done.7
  28.2 0.0 copy-done.5
  28.2 1.4 %lists.1 = (s32[8,128]{1,0:T(8,128)S(1)}, bf16[32,512]{1,0:T(8,128)(2,1)S(1)}) custom-call(s32[8,32]{1,0:T(8,128)S(1)} %bitcast.15, s32[1,32]{1,0:T(1,128)S(1)} %bitcast.19, s32[8,32]{1,0:T(8,128)S(1)} %bitcast.17, s32[32,128]{1,0:T(8,128)S(1)} %bitcast.13), custom_call_target="tpu_custom_call" | custom-call | bytes 300000 | tf_op jit(solution)/shard_map/lists/pallas_call | solution.py:383
  29.7 2.0 %collective-permute-done.1.high_ref = bf16[32,32,128]{2,1,0:T(8,128)(2,1)S(1)} collective-permute-done((bf16[32,32,128]{2,1,0:T(8,128)(2,1)S(1)}, bf16[32,32,128]{2,1,0:T(8,128)(2,1)S(1)}, u32[]{:S(2)}, u32[]{:S(2)}) %collective-permute-start.1) | collective-permute-done | bytes 262176 | tf_op jit(solution)/shard_map/ppermute | solution.py:375
  31.6 1.9 %collective-permute-done.low_ref = bf16[32,32,128]{2,1,0:T(8,128)(2,1)S(1)} collective-permute-done((bf16[32,32,128]{2,1,0:T(8,128)(2,1)S(1)}, bf16[32,32,128]{2,1,0:T(8,128)(2,1)S(1)}, u32[]{:S(2)}, u32[]{:S(2)}) %collective-permute-start) | collective-permute-done | bytes 262176 | tf_op jit(solution)/shard_map/ppermute | solution.py:374
  33.6 0.0 copy-done
  33.6 0.0 copy-start.1
  33.6 0.9 %copy-done.1 = bf16[32,32,128]{2,1,0:T(8,128)(2,1)S(1)} copy-done((bf16[32,32,128]{2,1,0:T(8,128)(2,1)S(1)}, bf16[32,32,128]{2,1,0:T(8,128)(2,1)}, u32[]{:S(2)}) %copy-start.1) | copy-done | bytes 262168
  34.5 0.0 copy-start.2
  34.5 1.6 %copy-done.2 = bf16[32,8,4096]{2,1,0:T(8,128)(2,1)S(1)} copy-done((bf16[32,8,4096]{2,1,0:T(8,128)(2,1)S(1)}, bf16[32,8,4096]{2,1,0:T(8,128)(2,1)}, u32[]{:S(2)}) %copy-start.2) | copy-done | bytes 2097176
  36.1 0.0 copy-start.4
  36.1 0.9 %copy-done.4 = bf16[32,4096]{1,0:T(8,128)(2,1)S(1)} copy-done((bf16[32,4096]{1,0:T(8,128)(2,1)S(1)}, bf16[32,4096]{1,0:T(8,128)(2,1)}, u32[]{:S(2)}) %copy-start.4) | copy-done | bytes 262168
  37.0 6.0 %near.1 = (bf16[288,32,128]{2,1,0:T(8,128)(2,1)S(1)}, f32[1664,32,128]{2,1,0:T(8,128)}) custom-call(s32[8,128]{1,0:T(8,128)S(1)} %get-tuple-element.10.lists_ref.lists_from, bf16[32,8,4096]{2,1,0:T(8,128)(2,1)S(1)} %copy-done.2, bf16[32,4096]{1,0:T(8,128)(2,1)S(1)} %copy-done.4, bf16[32,32,128]{2,1,0:T(8,128)(2,1)S(1)} %copy-done.1, ...), custom_call_target="tpu_custom_call" | custom-call | bytes 300000 | tf_op jit(solution)/shard_map/near/pallas_call | solution.py:392
  43.0 10.7 %all-to-all-done.1 = bf16[32,4,32,128]{3,2,1,0:T(8,128)(2,1)S(1)} async-done(((bf16[32,4,32,128]{3,2,1,0:T(8,128)(2,1)}), bf16[32,4,32,128]{3,2,1,0:T(8,128)(2,1)S(1)}, u32[]{:S(2)}, u32[]{:S(2)}) %all-to-all-start.1) | async-done | bytes 1048608 | tf_op jit(solution)/shard_map/all_to_all | solution.py:87
  53.8 3.8 %far.1 = bf16[32,16,1024]{2,1,0:T(8,128)(2,1)S(1)} custom-call(s32[8,128]{1,0:T(8,128)S(1)} %get-tuple-element.10.lists_ref.lists_from, bf16[288,32,128]{2,1,0:T(8,128)(2,1)S(1)} %get-tuple-element.11.work_ref, bf16[128,32,128]{2,1,0:T(8,128)(2,1)S(1)} %bitcast.10, f32[1664,32,128]{2,1,0:T(8,128)} %get-tuple-element.12.near_ref), custom_call_target="tpu_custom_call" | custom-call | bytes 18000000 | tf_op jit(solution)/shard_map/far/pallas_call | solution.py:408
  57.5 30.9 %all_to_all.15 = bf16[32,16,1024]{2,1,0:T(8,128)(2,1)S(1)} all-to-all(bf16[32,16,1024]{2,1,0:T(8,128)(2,1)S(1)} %far.1), channel_id=1, replica_groups={{31,30,29,28,27,26,25,24,23,22,21,20,19,18,17,16,15,14,13,12,11,10,9,8,..., dimensions={0} | all-to-all | bytes 2097152 | tf_op jit(solution)/shard_map/all_to_all | solution.py:87
  88.4 0.9 %holders.1 = f32[8,4096]{1,0:T(8,128)} custom-call(bf16[32,512]{1,0:T(8,128)(2,1)S(1)} %get-tuple-element.9.spread_ref, bf16[512,1024]{1,0:T(8,128)(2,1)S(1)} %bitcast.11), custom_call_target="tpu_custom_call" | custom-call | bytes 6000000 | tf_op jit(solution)/shard_map/holders/pallas_call | solution.py:423
Async XLA Ops:
  0.0 28.2 %copy-start.6 = (s32[32,8]{0,1:T(8,128)S(1)}, s32[32,8]{0,1:T(8,128)}, u32[]{:S(2)}) copy-start(s32[32,8]{0,1:T(8,128)} %param.9) | copy-start | bytes 3076
  0.0 28.2 %copy-start.7 = (s32[32]{0:T(128)S(1)}, s32[32]{0:T(128)}, u32[]{:S(2)}) copy-start(s32[32]{0:T(128)} %param.8) | copy-start | bytes 388
  0.0 28.2 %copy-start.5 = (s32[32,8]{0,1:T(8,128)S(1)}, s32[32,8]{0,1:T(8,128)}, u32[]{:S(2)}) copy-start(s32[32,8]{0,1:T(8,128)} %param.7) | copy-start | bytes 3076
  2.0 16.8 %all-to-all-start = ((s32[32,1,128]{2,1,0:T(1,128)}), s32[32,1,128]{2,1,0:T(1,128)S(1)}, u32[]{:S(2)}, u32[]{:S(2)}) async-start(s32[32,1,128]{2,1,0:T(1,128)} %bitcast.20), calls=%async_computation | async-start | bytes 32768 | tf_op jit(solution)/shard_map/all_to_all | solution.py:87
  13.9 1.0 %copy-start.3 = (bf16[32,4096]{1,0:T(8,128)(2,1)S(1)}, bf16[32,4096]{1,0:T(8,128)(2,1)}, u32[]{:S(2)}) copy-start(bf16[32,4096]{1,0:T(8,128)(2,1)} %p_ref.3) | copy-start | bytes 786436
  15.3 18.2 %copy-start = (bf16[32,32,128]{2,1,0:T(8,128)(2,1)}, bf16[32,32,128]{2,1,0:T(8,128)(2,1)S(1)}, u32[]{:S(2)}) copy-start(bf16[32,32,128]{2,1,0:T(8,128)(2,1)S(1)} %prepare.1.pq_ref) | copy-start | bytes 786436
  20.6 33.1 %all-to-all-start.1 = ((bf16[32,4,32,128]{3,2,1,0:T(8,128)(2,1)}), bf16[32,4,32,128]{3,2,1,0:T(8,128)(2,1)S(1)}, u32[]{:S(2)}, u32[]{:S(2)}) async-start(bf16[32,4,32,128]{3,2,1,0:T(8,128)(2,1)} %bitcast.6), calls=%async_computation.1 | async-start | bytes 2097152 | tf_op jit(solution)/shard_map/all_to_all | solution.py:87
  27.7 3.9 %collective-permute-start.1 = (bf16[32,32,128]{2,1,0:T(8,128)(2,1)S(1)}, bf16[32,32,128]{2,1,0:T(8,128)(2,1)S(1)}, u32[]{:S(2)}, u32[]{:S(2)}) collective-permute-start(bf16[32,32,128]{2,1,0:T(8,128)(2,1)S(1)} %prepare.1.pq_ref), channel_id=1, source_target_pairs={{32,0},{64,32},{96,64},{128,96},{160,128},{192,160},{224,192},{0,2... | collective-permute-start | bytes 786440 | tf_op jit(solution)/shard_map/ppermute | solution.py:375
  27.7 5.8 %collective-permute-start = (bf16[32,32,128]{2,1,0:T(8,128)(2,1)S(1)}, bf16[32,32,128]{2,1,0:T(8,128)(2,1)S(1)}, u32[]{:S(2)}, u32[]{:S(2)}) collective-permute-start(bf16[32,32,128]{2,1,0:T(8,128)(2,1)S(1)} %prepare.1.pq_ref), channel_id=1, source_target_pairs={{0,32},{32,64},{64,96},{96,128},{128,160},{160,192},{192,224},{224... | collective-permute-start | bytes 786440 | tf_op jit(solution)/shard_map/ppermute | solution.py:374
  33.6 1.0 %copy-start.1 = (bf16[32,32,128]{2,1,0:T(8,128)(2,1)S(1)}, bf16[32,32,128]{2,1,0:T(8,128)(2,1)}, u32[]{:S(2)}) copy-start(bf16[32,32,128]{2,1,0:T(8,128)(2,1)} %copy-done) | copy-start | bytes 786436
  34.5 1.6 %copy-start.2 = (bf16[32,8,4096]{2,1,0:T(8,128)(2,1)S(1)}, bf16[32,8,4096]{2,1,0:T(8,128)(2,1)}, u32[]{:S(2)}) copy-start(bf16[32,8,4096]{2,1,0:T(8,128)(2,1)} %a_ref.1) | copy-start | bytes 6291460
  36.1 0.9 %copy-start.4 = (bf16[32,4096]{1,0:T(8,128)(2,1)S(1)}, bf16[32,4096]{1,0:T(8,128)(2,1)}, u32[]{:S(2)}) copy-start(bf16[32,4096]{1,0:T(8,128)(2,1)} %p_ref.3) | copy-start | bytes 786436

commit v8 on v7

--- a/solution.py
+++ b/solution.py
@@ -15,7 +15,8 @@
 CAP2 = 4
 COUNTS = 6
 STEPS = (64, 32)
-ASK = SUMS = tuple(reversed(range(32)))
+ASK = tuple(reversed(range(32)))
+SUMS = tuple(z * 4 + y for z in reversed(range(8)) for y in range(4))
 ROWS = tuple(range(32))
 PARTS = 4
 QUARTERS = 4

time: 90.1 us -> 91.2 us (1.012)
  blocking collectives: 30.9 us -> 32 us
    all_to_all x1, blocking collectives: 30.9 us -> 32 us  [exchange(): lax.all_to_all(x, 'row', 0, 0, tiled=True, axis_index_groups=[list(order)])]
where the time goes in v8:
time: 91.2 us; the launch traced here: 90.5 us
  blocking collectives  32 us (35%)
  starting transfers between devices  19.5 us (21%)
  waiting for transfers between devices  18.1 us (20%)
  Pallas kernels  16.3 us (18%)
  local copies, waits for them, and re-layouts  4.45 us (5%)
    all_to_all x1, blocking collectives, exchange(): lax.all_to_all(x, 'row', 0, 0, tiled=True, axis_index_groups=[list(order)])  32 us
    all_to_all x2, starting transfers between devices, exchange(): lax.all_to_all(x, 'row', 0, 0, tiled=True, axis_index_groups=[list(order)])  19 us
    all_to_all x2, waiting for transfers between devices, exchange(): lax.all_to_all(x, 'row', 0, 0, tiled=True, axis_index_groups=[list(order)])  14.2 us
    pallas_call x1, Pallas kernels, body(): call(functools.partial(near_kernel, per_row), 'near', [smem, vmem, vmem,...  5.96 us
    unnamed x16, local copies, waits for them, and re-layouts  4.45 us
    pallas_call x1, Pallas kernels, body(): call(functools.partial(far_kernel, per_row), 'far', [vmem, vmem, vmem, hb...  3.73 us
    pallas_call x1, Pallas kernels, body(): call(functools.partial(plan_kernel, members), 'plan', [vmem] * 3, ints(me...  1.96 us
    ppermute x1, waiting for transfers between devices, body(): lax.ppermute(pq, 'grp', [(target, source) for source, target in forward])  1.95 us
  transfers between devices with their start and end apart: 4, of which 4 were waited for; matrix products, arithmetic and copies ran while one was open for 0% of the time, Pallas kernels for 9%

profile of v8, /device:TPU:38, one launch (start us, length us, event | category | flops | bytes accessed | tf_op | source)
XLA Modules:
  0.0 90.5 jit_solution(3063859862633410454)
XLA Ops:
  0.0 0.0 copy-start.6
  0.0 0.0 copy-start.7
  0.0 0.0 copy-start.5
  0.0 2.0 %plan.1 = s32[32,128]{1,0:T(8,128)} custom-call(s32[8,32]{1,0:T(8,128)} %bitcast.14, s32[1,32]{1,0:T(1,128)} %bitcast.18, s32[8,32]{1,0:T(8,128)} %bitcast.16), custom_call_target="tpu_custom_call" | custom-call | bytes 6000000 | tf_op jit(solution)/shard_map/plan/pallas_call | solution.py:366
  2.0 11.9 %all-to-all-start = ((s32[32,1,128]{2,1,0:T(1,128)}), s32[32,1,128]{2,1,0:T(1,128)S(1)}, u32[]{:S(2)}, u32[]{:S(2)}) async-start(s32[32,1,128]{2,1,0:T(1,128)} %bitcast.20), calls=%async_computation | async-start | bytes 32768 | tf_op jit(solution)/shard_map/all_to_all | solution.py:88
  13.9 0.0 copy-start.3
  13.9 0.9 %copy-done.3 = bf16[32,4096]{1,0:T(8,128)(2,1)S(1)} copy-done((bf16[32,4096]{1,0:T(8,128)(2,1)S(1)}, bf16[32,4096]{1,0:T(8,128)(2,1)}, u32[]{:S(2)}) %copy-start.3) | copy-done | bytes 262168
  14.8 0.5 prepare.1.pq_ref
  15.3 0.0 copy-start
  15.3 3.5 %all-to-all-done = s32[32,1,128]{2,1,0:T(1,128)S(1)} async-done(((s32[32,1,128]{2,1,0:T(1,128)}), s32[32,1,128]{2,1,0:T(1,128)S(1)}, u32[]{:S(2)}, u32[]{:S(2)}) %all-to-all-start) | async-done | bytes 16416 | tf_op jit(solution)/shard_map/all_to_all | solution.py:88
  18.8 1.8 %pack.1 = bf16[128,32,128]{2,1,0:T(8,128)(2,1)} custom-call(s32[32,128]{1,0:T(8,128)S(1)} %bitcast.12, bf16[32,32,128]{2,1,0:T(8,128)(2,1)S(1)} %prepare.1.pq_ref), custom_call_target="tpu_custom_call" | custom-call | bytes 6000000 | tf_op jit(solution)/shard_map/pack/pallas_call | solution.py:378
  20.6 7.1 %all-to-all-start.1 = ((bf16[32,4,32,128]{3,2,1,0:T(8,128)(2,1)}), bf16[32,4,32,128]{3,2,1,0:T(8,128)(2,1)S(1)}, u32[]{:S(2)}, u32[]{:S(2)}) async-start(bf16[32,4,32,128]{3,2,1,0:T(8,128)(2,1)} %bitcast.6), calls=%async_computation.1 | async-start | bytes 2097152 | tf_op jit(solution)/shard_map/all_to_all | solution.py:88
  27.7 0.0 collective-permute-start.1
  27.7 0.5 collective-permute-start
  28.2 0.0 copy-done.6
  28.2 0.0 copy-done.7
  28.2 0.0 copy-done.5
  28.2 1.4 %lists.1 = (s32[8,128]{1,0:T(8,128)S(1)}, bf16[32,512]{1,0:T(8,128)(2,1)S(1)}) custom-call(s32[8,32]{1,0:T(8,128)S(1)} %bitcast.15, s32[1,32]{1,0:T(1,128)S(1)} %bitcast.19, s32[8,32]{1,0:T(8,128)S(1)} %bitcast.17, s32[32,128]{1,0:T(8,128)S(1)} %bitcast.13), custom_call_target="tpu_custom_call" | custom-call | bytes 300000 | tf_op jit(solution)/shard_map/lists/pallas_call | solution.py:384
  29.7 2.0 %collective-permute-done.1.high_ref = bf16[32,32,128]{2,1,0:T(8,128)(2,1)S(1)} collective-permute-done((bf16[32,32,128]{2,1,0:T(8,128)(2,1)S(1)}, bf16[32,32,128]{2,1,0:T(8,128)(2,1)S(1)}, u32[]{:S(2)}, u32[]{:S(2)}) %collective-permute-start.1) | collective-permute-done | bytes 262176 | tf_op jit(solution)/shard_map/ppermute | solution.py:376
  31.6 1.9 %collective-permute-done.low_ref = bf16[32,32,128]{2,1,0:T(8,128)(2,1)S(1)} collective-permute-done((bf16[32,32,128]{2,1,0:T(8,128)(2,1)S(1)}, bf16[32,32,128]{2,1,0:T(8,128)(2,1)S(1)}, u32[]{:S(2)}, u32[]{:S(2)}) %collective-permute-start) | collective-permute-done | bytes 262176 | tf_op jit(solution)/shard_map/ppermute | solution.py:375
  33.6 0.0 copy-done
  33.6 0.0 copy-start.1
  33.6 0.9 %copy-done.1 = bf16[32,32,128]{2,1,0:T(8,128)(2,1)S(1)} copy-done((bf16[32,32,128]{2,1,0:T(8,128)(2,1)S(1)}, bf16[32,32,128]{2,1,0:T(8,128)(2,1)}, u32[]{:S(2)}) %copy-start.1) | copy-done | bytes 262168
  34.5 0.0 copy-start.2
  34.5 1.6 %copy-done.2 = bf16[32,8,4096]{2,1,0:T(8,128)(2,1)S(1)} copy-done((bf16[32,8,4096]{2,1,0:T(8,128)(2,1)S(1)}, bf16[32,8,4096]{2,1,0:T(8,128)(2,1)}, u32[]{:S(2)}) %copy-start.2) | copy-done | bytes 2097176
  36.1 0.0 copy-start.4
  36.1 0.9 %copy-done.4 = bf16[32,4096]{1,0:T(8,128)(2,1)S(1)} copy-done((bf16[32,4096]{1,0:T(8,128)(2,1)S(1)}, bf16[32,4096]{1,0:T(8,128)(2,1)}, u32[]{:S(2)}) %copy-start.4) | copy-done | bytes 262168
  37.0 6.0 %near.1 = (bf16[288,32,128]{2,1,0:T(8,128)(2,1)S(1)}, f32[1664,32,128]{2,1,0:T(8,128)}) custom-call(s32[8,128]{1,0:T(8,128)S(1)} %get-tuple-element.10.lists_ref.lists_from, bf16[32,8,4096]{2,1,0:T(8,128)(2,1)S(1)} %copy-done.2, bf16[32,4096]{1,0:T(8,128)(2,1)S(1)} %copy-done.4, bf16[32,32,128]{2,1,0:T(8,128)(2,1)S(1)} %copy-done.1, ...), custom_call_target="tpu_custom_call" | custom-call | bytes 300000 | tf_op jit(solution)/shard_map/near/pallas_call | solution.py:393
  43.0 10.8 %all-to-all-done.1 = bf16[32,4,32,128]{3,2,1,0:T(8,128)(2,1)S(1)} async-done(((bf16[32,4,32,128]{3,2,1,0:T(8,128)(2,1)}), bf16[32,4,32,128]{3,2,1,0:T(8,128)(2,1)S(1)}, u32[]{:S(2)}, u32[]{:S(2)}) %all-to-all-start.1) | async-done | bytes 1048608 | tf_op jit(solution)/shard_map/all_to_all | solution.py:88
  53.8 3.7 %far.1 = bf16[32,16,1024]{2,1,0:T(8,128)(2,1)S(1)} custom-call(s32[8,128]{1,0:T(8,128)S(1)} %get-tuple-element.10.lists_ref.lists_from, bf16[288,32,128]{2,1,0:T(8,128)(2,1)S(1)} %get-tuple-element.11.work_ref, bf16[128,32,128]{2,1,0:T(8,128)(2,1)S(1)} %bitcast.10, f32[1664,32,128]{2,1,0:T(8,128)} %get-tuple-element.12.near_ref), custom_call_target="tpu_custom_call" | custom-call | bytes 18000000 | tf_op jit(solution)/shard_map/far/pallas_call | solution.py:409
  57.5 32.0 %all_to_all.15 = bf16[32,16,1024]{2,1,0:T(8,128)(2,1)S(1)} all-to-all(bf16[32,16,1024]{2,1,0:T(8,128)(2,1)S(1)} %far.1), channel_id=1, replica_groups={{28,29,30,31,24,25,26,27,20,21,22,23,16,17,18,19,12,13,14,15,8,9,10,11,..., dimensions={0} | all-to-all | bytes 2097152 | tf_op jit(solution)/shard_map/all_to_all | solution.py:88
  89.5 0.9 %holders.1 = f32[8,4096]{1,0:T(8,128)} custom-call(bf16[32,512]{1,0:T(8,128)(2,1)S(1)} %get-tuple-element.9.spread_ref, bf16[512,1024]{1,0:T(8,128)(2,1)S(1)} %bitcast.11), custom_call_target="tpu_custom_call" | custom-call | bytes 6000000 | tf_op jit(solution)/shard_map/holders/pallas_call | solution.py:424
Async XLA Ops:
  0.0 28.2 %copy-start.6 = (s32[32,8]{0,1:T(8,128)S(1)}, s32[32,8]{0,1:T(8,128)}, u32[]{:S(2)}) copy-start(s32[32,8]{0,1:T(8,128)} %param.9) | copy-start | bytes 3076
  0.0 28.2 %copy-start.7 = (s32[32]{0:T(128)S(1)}, s32[32]{0:T(128)}, u32[]{:S(2)}) copy-start(s32[32]{0:T(128)} %param.8) | copy-start | bytes 388
  0.0 28.2 %copy-start.5 = (s32[32,8]{0,1:T(8,128)S(1)}, s32[32,8]{0,1:T(8,128)}, u32[]{:S(2)}) copy-start(s32[32,8]{0,1:T(8,128)} %param.7) | copy-start | bytes 3076
  2.0 16.8 %all-to-all-start = ((s32[32,1,128]{2,1,0:T(1,128)}), s32[32,1,128]{2,1,0:T(1,128)S(1)}, u32[]{:S(2)}, u32[]{:S(2)}) async-start(s32[32,1,128]{2,1,0:T(1,128)} %bitcast.20), calls=%async_computation | async-start | bytes 32768 | tf_op jit(solution)/shard_map/all_to_all | solution.py:88
  13.9 1.0 %copy-start.3 = (bf16[32,4096]{1,0:T(8,128)(2,1)S(1)}, bf16[32,4096]{1,0:T(8,128)(2,1)}, u32[]{:S(2)}) copy-start(bf16[32,4096]{1,0:T(8,128)(2,1)} %p_ref.3) | copy-start | bytes 786436
  15.3 18.2 %copy-start = (bf16[32,32,128]{2,1,0:T(8,128)(2,1)}, bf16[32,32,128]{2,1,0:T(8,128)(2,1)S(1)}, u32[]{:S(2)}) copy-start(bf16[32,32,128]{2,1,0:T(8,128)(2,1)S(1)} %prepare.1.pq_ref) | copy-start | bytes 786436
  20.6 33.1 %all-to-all-start.1 = ((bf16[32,4,32,128]{3,2,1,0:T(8,128)(2,1)}), bf16[32,4,32,128]{3,2,1,0:T(8,128)(2,1)S(1)}, u32[]{:S(2)}, u32[]{:S(2)}) async-start(bf16[32,4,32,128]{3,2,1,0:T(8,128)(2,1)} %bitcast.6), calls=%async_computation.1 | async-start | bytes 2097152 | tf_op jit(solution)/shard_map/all_to_all | solution.py:88
  27.7 3.9 %collective-permute-start.1 = (bf16[32,32,128]{2,1,0:T(8,128)(2,1)S(1)}, bf16[32,32,128]{2,1,0:T(8,128)(2,1)S(1)}, u32[]{:S(2)}, u32[]{:S(2)}) collective-permute-start(bf16[32,32,128]{2,1,0:T(8,128)(2,1)S(1)} %prepare.1.pq_ref), channel_id=1, source_target_pairs={{32,0},{64,32},{96,64},{128,96},{160,128},{192,160},{224,192},{0,2... | collective-permute-start | bytes 786440 | tf_op jit(solution)/shard_map/ppermute | solution.py:376
  27.7 5.8 %collective-permute-start = (bf16[32,32,128]{2,1,0:T(8,128)(2,1)S(1)}, bf16[32,32,128]{2,1,0:T(8,128)(2,1)S(1)}, u32[]{:S(2)}, u32[]{:S(2)}) collective-permute-start(bf16[32,32,128]{2,1,0:T(8,128)(2,1)S(1)} %prepare.1.pq_ref), channel_id=1, source_target_pairs={{0,32},{32,64},{64,96},{96,128},{128,160},{160,192},{192,224},{224... | collective-permute-start | bytes 786440 | tf_op jit(solution)/shard_map/ppermute | solution.py:375
  33.6 1.0 %copy-start.1 = (bf16[32,32,128]{2,1,0:T(8,128)(2,1)S(1)}, bf16[32,32,128]{2,1,0:T(8,128)(2,1)}, u32[]{:S(2)}) copy-start(bf16[32,32,128]{2,1,0:T(8,128)(2,1)} %copy-done) | copy-start | bytes 786436
  34.5 1.6 %copy-start.2 = (bf16[32,8,4096]{2,1,0:T(8,128)(2,1)S(1)}, bf16[32,8,4096]{2,1,0:T(8,128)(2,1)}, u32[]{:S(2)}) copy-start(bf16[32,8,4096]{2,1,0:T(8,128)(2,1)} %a_ref.1) | copy-start | bytes 6291460
  36.1 0.9 %copy-start.4 = (bf16[32,4096]{1,0:T(8,128)(2,1)S(1)}, bf16[32,4096]{1,0:T(8,128)(2,1)}, u32[]{:S(2)}) copy-start(bf16[32,4096]{1,0:T(8,128)(2,1)} %p_ref.3) | copy-start | bytes 786436

commit v9 on v7

--- a/solution.py
+++ b/solution.py
@@ -77,6 +77,11 @@
 
 
 def place_in(order, member):
+    natural = tuple(range(len(order)))
+    if order == natural:
+        return member
+    if order == natural[::-1]:
+        return len(order) - 1 - member
     result = jnp.zeros_like(member)
     for at, who in enumerate(order):
         result = jnp.where(member == who, at, result)

time: 90.1 us -> 90.1 us (level)
  no operation moved by 1% of the time
where the time goes in v9:
time: 90.1 us; the launch traced here: 89.3 us
  blocking collectives  30.4 us (34%)
  starting transfers between devices  19.5 us (22%)
  waiting for transfers between devices  18.1 us (20%)
  Pallas kernels  16.8 us (19%)
  local copies, waits for them, and re-layouts  4.45 us (5%)
    all_to_all x1, blocking collectives, exchange(): lax.all_to_all(x, 'row', 0, 0, tiled=True, axis_index_groups=[list(order)])  30.4 us
    all_to_all x2, starting transfers between devices, exchange(): lax.all_to_all(x, 'row', 0, 0, tiled=True, axis_index_groups=[list(order)])  19 us
    all_to_all x2, waiting for transfers between devices, exchange(): lax.all_to_all(x, 'row', 0, 0, tiled=True, axis_index_groups=[list(order)])  14.2 us
    pallas_call x1, Pallas kernels, body(): call(functools.partial(near_kernel, per_row), 'near', [smem, vmem, vmem,...  5.96 us
    unnamed x16, local copies, waits for them, and re-layouts  4.45 us
    pallas_call x1, Pallas kernels, body(): call(functools.partial(far_kernel, per_row), 'far', [vmem, vmem, vmem, hb...  4.19 us
    ppermute x1, waiting for transfers between devices, body(): lax.ppermute(pq, 'grp', [(target, source) for source, target in forward])  1.95 us
    pallas_call x1, Pallas kernels, body(): call(functools.partial(plan_kernel, members), 'plan', [vmem] * 3, ints(me...  1.95 us
  transfers between devices with their start and end apart: 4, of which 4 were waited for; matrix products, arithmetic and copies ran while one was open for 0% of the time, Pallas kernels for 9%

profile of v9, /device:TPU:38, one launch (start us, length us, event | category | flops | bytes accessed | tf_op | source)
XLA Modules:
  0.0 89.3 jit_solution(2262623271541768377)
XLA Ops:
  0.0 0.0 copy-start.6
  0.0 0.0 copy-start.7
  0.0 0.0 copy-start.5
  0.0 1.9 %plan.1 = s32[32,128]{1,0:T(8,128)} custom-call(s32[8,32]{1,0:T(8,128)} %bitcast.14, s32[1,32]{1,0:T(1,128)} %bitcast.18, s32[8,32]{1,0:T(8,128)} %bitcast.16), custom_call_target="tpu_custom_call" | custom-call | bytes 6000000 | tf_op jit(solution)/shard_map/plan/pallas_call | solution.py:370
  2.0 11.9 %all-to-all-start = ((s32[32,1,128]{2,1,0:T(1,128)}), s32[32,1,128]{2,1,0:T(1,128)S(1)}, u32[]{:S(2)}, u32[]{:S(2)}) async-start(s32[32,1,128]{2,1,0:T(1,128)} %bitcast.20), calls=%async_computation | async-start | bytes 32768 | tf_op jit(solution)/shard_map/all_to_all | solution.py:92
  13.9 0.0 copy-start.3
  13.9 0.9 %copy-done.3 = bf16[32,4096]{1,0:T(8,128)(2,1)S(1)} copy-done((bf16[32,4096]{1,0:T(8,128)(2,1)S(1)}, bf16[32,4096]{1,0:T(8,128)(2,1)}, u32[]{:S(2)}) %copy-start.3) | copy-done | bytes 262168
  14.8 0.5 prepare.1.pq_ref
  15.3 0.0 copy-start
  15.3 3.5 %all-to-all-done = s32[32,1,128]{2,1,0:T(1,128)S(1)} async-done(((s32[32,1,128]{2,1,0:T(1,128)}), s32[32,1,128]{2,1,0:T(1,128)S(1)}, u32[]{:S(2)}, u32[]{:S(2)}) %all-to-all-start) | async-done | bytes 16416 | tf_op jit(solution)/shard_map/all_to_all | solution.py:92
  18.8 1.8 %pack.1 = bf16[128,32,128]{2,1,0:T(8,128)(2,1)} custom-call(s32[32,128]{1,0:T(8,128)S(1)} %bitcast.12, bf16[32,32,128]{2,1,0:T(8,128)(2,1)S(1)} %prepare.1.pq_ref), custom_call_target="tpu_custom_call" | custom-call | bytes 6000000 | tf_op jit(solution)/shard_map/pack/pallas_call | solution.py:382
  20.6 7.1 %all-to-all-start.1 = ((bf16[32,4,32,128]{3,2,1,0:T(8,128)(2,1)}), bf16[32,4,32,128]{3,2,1,0:T(8,128)(2,1)S(1)}, u32[]{:S(2)}, u32[]{:S(2)}) async-start(bf16[32,4,32,128]{3,2,1,0:T(8,128)(2,1)} %bitcast.6), calls=%async_computation.1 | async-start | bytes 2097152 | tf_op jit(solution)/shard_map/all_to_all | solution.py:92
  27.7 0.0 collective-permute-start.1
  27.7 0.5 collective-permute-start
  28.2 0.0 copy-done.6
  28.2 0.0 copy-done.7
  28.2 0.0 copy-done.5
  28.2 1.4 %lists.1 = (s32[8,128]{1,0:T(8,128)S(1)}, bf16[32,512]{1,0:T(8,128)(2,1)S(1)}) custom-call(s32[8,32]{1,0:T(8,128)S(1)} %bitcast.15, s32[1,32]{1,0:T(1,128)S(1)} %bitcast.19, s32[8,32]{1,0:T(8,128)S(1)} %bitcast.17, s32[32,128]{1,0:T(8,128)S(1)} %bitcast.13), custom_call_target="tpu_custom_call" | custom-call | bytes 300000 | tf_op jit(solution)/shard_map/lists/pallas_call | solution.py:388
  29.7 2.0 %collective-permute-done.1.high_ref = bf16[32,32,128]{2,1,0:T(8,128)(2,1)S(1)} collective-permute-done((bf16[32,32,128]{2,1,0:T(8,128)(2,1)S(1)}, bf16[32,32,128]{2,1,0:T(8,128)(2,1)S(1)}, u32[]{:S(2)}, u32[]{:S(2)}) %collective-permute-start.1) | collective-permute-done | bytes 262176 | tf_op jit(solution)/shard_map/ppermute | solution.py:380
  31.6 1.9 %collective-permute-done.low_ref = bf16[32,32,128]{2,1,0:T(8,128)(2,1)S(1)} collective-permute-done((bf16[32,32,128]{2,1,0:T(8,128)(2,1)S(1)}, bf16[32,32,128]{2,1,0:T(8,128)(2,1)S(1)}, u32[]{:S(2)}, u32[]{:S(2)}) %collective-permute-start) | collective-permute-done | bytes 262176 | tf_op jit(solution)/shard_map/ppermute | solution.py:379
  33.5 0.0 copy-done
  33.5 0.0 copy-start.1
  33.5 0.9 %copy-done.1 = bf16[32,32,128]{2,1,0:T(8,128)(2,1)S(1)} copy-done((bf16[32,32,128]{2,1,0:T(8,128)(2,1)S(1)}, bf16[32,32,128]{2,1,0:T(8,128)(2,1)}, u32[]{:S(2)}) %copy-start.1) | copy-done | bytes 262168
  34.5 0.0 copy-start.2
  34.5 1.6 %copy-done.2 = bf16[32,8,4096]{2,1,0:T(8,128)(2,1)S(1)} copy-done((bf16[32,8,4096]{2,1,0:T(8,128)(2,1)S(1)}, bf16[32,8,4096]{2,1,0:T(8,128)(2,1)}, u32[]{:S(2)}) %copy-start.2) | copy-done | bytes 2097176
  36.1 0.0 copy-start.4
  36.1 0.9 %copy-done.4 = bf16[32,4096]{1,0:T(8,128)(2,1)S(1)} copy-done((bf16[32,4096]{1,0:T(8,128)(2,1)S(1)}, bf16[32,4096]{1,0:T(8,128)(2,1)}, u32[]{:S(2)}) %copy-start.4) | copy-done | bytes 262168
  37.0 6.0 %near.1 = (bf16[288,32,128]{2,1,0:T(8,128)(2,1)S(1)}, f32[1664,32,128]{2,1,0:T(8,128)}) custom-call(s32[8,128]{1,0:T(8,128)S(1)} %get-tuple-element.10.lists_ref.lists_from, bf16[32,8,4096]{2,1,0:T(8,128)(2,1)S(1)} %copy-done.2, bf16[32,4096]{1,0:T(8,128)(2,1)S(1)} %copy-done.4, bf16[32,32,128]{2,1,0:T(8,128)(2,1)S(1)} %copy-done.1, ...), custom_call_target="tpu_custom_call" | custom-call | bytes 300000 | tf_op jit(solution)/shard_map/near/pallas_call | solution.py:397
  43.0 10.8 %all-to-all-done.1 = bf16[32,4,32,128]{3,2,1,0:T(8,128)(2,1)S(1)} async-done(((bf16[32,4,32,128]{3,2,1,0:T(8,128)(2,1)}), bf16[32,4,32,128]{3,2,1,0:T(8,128)(2,1)S(1)}, u32[]{:S(2)}, u32[]{:S(2)}) %all-to-all-start.1) | async-done | bytes 1048608 | tf_op jit(solution)/shard_map/all_to_all | solution.py:92
  53.8 4.2 %far.1 = bf16[32,16,1024]{2,1,0:T(8,128)(2,1)S(1)} custom-call(s32[8,128]{1,0:T(8,128)S(1)} %get-tuple-element.10.lists_ref.lists_from, bf16[288,32,128]{2,1,0:T(8,128)(2,1)S(1)} %get-tuple-element.11.work_ref, bf16[128,32,128]{2,1,0:T(8,128)(2,1)S(1)} %bitcast.10, f32[1664,32,128]{2,1,0:T(8,128)} %get-tuple-element.12.near_ref), custom_call_target="tpu_custom_call" | custom-call | bytes 18000000 | tf_op jit(solution)/shard_map/far/pallas_call | solution.py:413
  58.0 30.4 %all_to_all.15 = bf16[32,16,1024]{2,1,0:T(8,128)(2,1)S(1)} all-to-all(bf16[32,16,1024]{2,1,0:T(8,128)(2,1)S(1)} %far.1), channel_id=1, replica_groups={{31,30,29,28,27,26,25,24,23,22,21,20,19,18,17,16,15,14,13,12,11,10,9,8,..., dimensions={0} | all-to-all | bytes 2097152 | tf_op jit(solution)/shard_map/all_to_all | solution.py:92
  88.3 0.9 %holders.1 = f32[8,4096]{1,0:T(8,128)} custom-call(bf16[32,512]{1,0:T(8,128)(2,1)S(1)} %get-tuple-element.9.spread_ref, bf16[512,1024]{1,0:T(8,128)(2,1)S(1)} %bitcast.11), custom_call_target="tpu_custom_call" | custom-call | bytes 6000000 | tf_op jit(solution)/shard_map/holders/pallas_call | solution.py:428
Async XLA Ops:
  0.0 28.2 %copy-start.6 = (s32[32,8]{0,1:T(8,128)S(1)}, s32[32,8]{0,1:T(8,128)}, u32[]{:S(2)}) copy-start(s32[32,8]{0,1:T(8,128)} %param.9) | copy-start | bytes 3076
  0.0 28.2 %copy-start.7 = (s32[32]{0:T(128)S(1)}, s32[32]{0:T(128)}, u32[]{:S(2)}) copy-start(s32[32]{0:T(128)} %param.8) | copy-start | bytes 388
  0.0 28.2 %copy-start.5 = (s32[32,8]{0,1:T(8,128)S(1)}, s32[32,8]{0,1:T(8,128)}, u32[]{:S(2)}) copy-start(s32[32,8]{0,1:T(8,128)} %param.7) | copy-start | bytes 3076
  2.0 16.8 %all-to-all-start = ((s32[32,1,128]{2,1,0:T(1,128)}), s32[32,1,128]{2,1,0:T(1,128)S(1)}, u32[]{:S(2)}, u32[]{:S(2)}) async-start(s32[32,1,128]{2,1,0:T(1,128)} %bitcast.20), calls=%async_computation | async-start | bytes 32768 | tf_op jit(solution)/shard_map/all_to_all | solution.py:92
  13.9 1.0 %copy-start.3 = (bf16[32,4096]{1,0:T(8,128)(2,1)S(1)}, bf16[32,4096]{1,0:T(8,128)(2,1)}, u32[]{:S(2)}) copy-start(bf16[32,4096]{1,0:T(8,128)(2,1)} %p_ref.3) | copy-start | bytes 786436
  15.3 18.2 %copy-start = (bf16[32,32,128]{2,1,0:T(8,128)(2,1)}, bf16[32,32,128]{2,1,0:T(8,128)(2,1)S(1)}, u32[]{:S(2)}) copy-start(bf16[32,32,128]{2,1,0:T(8,128)(2,1)S(1)} %prepare.1.pq_ref) | copy-start | bytes 786436
  20.6 33.1 %all-to-all-start.1 = ((bf16[32,4,32,128]{3,2,1,0:T(8,128)(2,1)}), bf16[32,4,32,128]{3,2,1,0:T(8,128)(2,1)S(1)}, u32[]{:S(2)}, u32[]{:S(2)}) async-start(bf16[32,4,32,128]{3,2,1,0:T(8,128)(2,1)} %bitcast.6), calls=%async_computation.1 | async-start | bytes 2097152 | tf_op jit(solution)/shard_map/all_to_all | solution.py:92
  27.7 3.9 %collective-permute-start.1 = (bf16[32,32,128]{2,1,0:T(8,128)(2,1)S(1)}, bf16[32,32,128]{2,1,0:T(8,128)(2,1)S(1)}, u32[]{:S(2)}, u32[]{:S(2)}) collective-permute-start(bf16[32,32,128]{2,1,0:T(8,128)(2,1)S(1)} %prepare.1.pq_ref), channel_id=1, source_target_pairs={{32,0},{64,32},{96,64},{128,96},{160,128},{192,160},{224,192},{0,2... | collective-permute-start | bytes 786440 | tf_op jit(solution)/shard_map/ppermute | solution.py:380
  27.7 5.8 %collective-permute-start = (bf16[32,32,128]{2,1,0:T(8,128)(2,1)S(1)}, bf16[32,32,128]{2,1,0:T(8,128)(2,1)S(1)}, u32[]{:S(2)}, u32[]{:S(2)}) collective-permute-start(bf16[32,32,128]{2,1,0:T(8,128)(2,1)S(1)} %prepare.1.pq_ref), channel_id=1, source_target_pairs={{0,32},{32,64},{64,96},{96,128},{128,160},{160,192},{192,224},{224... | collective-permute-start | bytes 786440 | tf_op jit(solution)/shard_map/ppermute | solution.py:379
  33.5 1.0 %copy-start.1 = (bf16[32,32,128]{2,1,0:T(8,128)(2,1)S(1)}, bf16[32,32,128]{2,1,0:T(8,128)(2,1)}, u32[]{:S(2)}) copy-start(bf16[32,32,128]{2,1,0:T(8,128)(2,1)} %copy-done) | copy-start | bytes 786436
  34.5 1.6 %copy-start.2 = (bf16[32,8,4096]{2,1,0:T(8,128)(2,1)S(1)}, bf16[32,8,4096]{2,1,0:T(8,128)(2,1)}, u32[]{:S(2)}) copy-start(bf16[32,8,4096]{2,1,0:T(8,128)(2,1)} %a_ref.1) | copy-start | bytes 6291460
  36.1 0.9 %copy-start.4 = (bf16[32,4096]{1,0:T(8,128)(2,1)S(1)}, bf16[32,4096]{1,0:T(8,128)(2,1)}, u32[]{:S(2)}) copy-start(bf16[32,4096]{1,0:T(8,128)(2,1)} %p_ref.3) | copy-start | bytes 786436

commit v10 on v7

--- a/solution.py
+++ b/solution.py
@@ -14,7 +14,7 @@
 SLOT_DEV = 8
 CAP2 = 4
 COUNTS = 6
-STEPS = (64, 32)
+STEPS = (128, 64)
 ASK = SUMS = tuple(reversed(range(32)))
 ROWS = tuple(range(32))
 PARTS = 4

time: 90.1 us -> 90.1 us (level)
  no operation moved by 1% of the time
where the time goes in v10:
time: 90.1 us; the launch traced here: 89.6 us
  blocking collectives  30.8 us (34%)
  starting transfers between devices  19.5 us (22%)
  waiting for transfers between devices  17.7 us (20%)
  Pallas kernels  17.1 us (19%)
  local copies, waits for them, and re-layouts  4.45 us (5%)
    all_to_all x1, blocking collectives, exchange(): lax.all_to_all(x, 'row', 0, 0, tiled=True, axis_index_groups=[list(order)])  30.8 us
    all_to_all x2, starting transfers between devices, exchange(): lax.all_to_all(x, 'row', 0, 0, tiled=True, axis_index_groups=[list(order)])  19 us
    all_to_all x2, waiting for transfers between devices, exchange(): lax.all_to_all(x, 'row', 0, 0, tiled=True, axis_index_groups=[list(order)])  13.8 us
    pallas_call x1, Pallas kernels, body(): call(functools.partial(near_kernel, per_row), 'near', [smem, vmem, vmem,...  6.35 us
    unnamed x16, local copies, waits for them, and re-layouts  4.45 us
    pallas_call x1, Pallas kernels, body(): call(functools.partial(far_kernel, per_row), 'far', [vmem, vmem, vmem, hb...  4.13 us
    pallas_call x1, Pallas kernels, body(): call(functools.partial(plan_kernel, members), 'plan', [vmem] * 3, ints(me...  1.96 us
    ppermute x1, waiting for transfers between devices, body(): lax.ppermute(pq, 'grp', [(target, source) for source, target in forward])  1.95 us
  transfers between devices with their start and end apart: 4, of which 4 were waited for; matrix products, arithmetic and copies ran while one was open for 0% of the time, Pallas kernels for 9%

profile of v10, /device:TPU:38, one launch (start us, length us, event | category | flops | bytes accessed | tf_op | source)
XLA Modules:
  0.0 89.6 jit_solution(13680478875001476395)
XLA Ops:
  0.0 0.0 copy-start.6
  0.0 0.0 copy-start.7
  0.0 0.0 copy-start.5
  0.0 2.0 %plan.1 = s32[32,128]{1,0:T(8,128)} custom-call(s32[8,32]{1,0:T(8,128)} %bitcast.14, s32[1,32]{1,0:T(1,128)} %bitcast.18, s32[8,32]{1,0:T(8,128)} %bitcast.16), custom_call_target="tpu_custom_call" | custom-call | bytes 6000000 | tf_op jit(solution)/shard_map/plan/pallas_call | solution.py:365
  2.0 11.9 %all-to-all-start = ((s32[32,1,128]{2,1,0:T(1,128)}), s32[32,1,128]{2,1,0:T(1,128)S(1)}, u32[]{:S(2)}, u32[]{:S(2)}) async-start(s32[32,1,128]{2,1,0:T(1,128)} %bitcast.20), calls=%async_computation | async-start | bytes 32768 | tf_op jit(solution)/shard_map/all_to_all | solution.py:87
  13.9 0.0 copy-start.3
  13.9 0.9 %copy-done.3 = bf16[32,4096]{1,0:T(8,128)(2,1)S(1)} copy-done((bf16[32,4096]{1,0:T(8,128)(2,1)S(1)}, bf16[32,4096]{1,0:T(8,128)(2,1)}, u32[]{:S(2)}) %copy-start.3) | copy-done | bytes 262168
  14.8 0.5 prepare.1.pq_ref
  15.3 0.0 copy-start
  15.3 3.5 %all-to-all-done = s32[32,1,128]{2,1,0:T(1,128)S(1)} async-done(((s32[32,1,128]{2,1,0:T(1,128)}), s32[32,1,128]{2,1,0:T(1,128)S(1)}, u32[]{:S(2)}, u32[]{:S(2)}) %all-to-all-start) | async-done | bytes 16416 | tf_op jit(solution)/shard_map/all_to_all | solution.py:87
  18.8 1.8 %pack.1 = bf16[128,32,128]{2,1,0:T(8,128)(2,1)} custom-call(s32[32,128]{1,0:T(8,128)S(1)} %bitcast.12, bf16[32,32,128]{2,1,0:T(8,128)(2,1)S(1)} %prepare.1.pq_ref), custom_call_target="tpu_custom_call" | custom-call | bytes 6000000 | tf_op jit(solution)/shard_map/pack/pallas_call | solution.py:377
  20.6 7.1 %all-to-all-start.1 = ((bf16[32,4,32,128]{3,2,1,0:T(8,128)(2,1)}), bf16[32,4,32,128]{3,2,1,0:T(8,128)(2,1)S(1)}, u32[]{:S(2)}, u32[]{:S(2)}) async-start(bf16[32,4,32,128]{3,2,1,0:T(8,128)(2,1)} %bitcast.6), calls=%async_computation.1 | async-start | bytes 2097152 | tf_op jit(solution)/shard_map/all_to_all | solution.py:87
  27.7 0.0 collective-permute-start.1
  27.7 0.5 collective-permute-start
  28.2 0.0 copy-done.6
  28.2 0.0 copy-done.7
  28.2 0.0 copy-done.5
  28.2 1.4 %lists.1 = (s32[8,128]{1,0:T(8,128)S(1)}, bf16[32,512]{1,0:T(8,128)(2,1)S(1)}) custom-call(s32[8,32]{1,0:T(8,128)S(1)} %bitcast.15, s32[1,32]{1,0:T(1,128)S(1)} %bitcast.19, s32[8,32]{1,0:T(8,128)S(1)} %bitcast.17, s32[32,128]{1,0:T(8,128)S(1)} %bitcast.13), custom_call_target="tpu_custom_call" | custom-call | bytes 300000 | tf_op jit(solution)/shard_map/lists/pallas_call | solution.py:383
  29.7 2.0 %collective-permute-done.1.high_ref = bf16[32,32,128]{2,1,0:T(8,128)(2,1)S(1)} collective-permute-done((bf16[32,32,128]{2,1,0:T(8,128)(2,1)S(1)}, bf16[32,32,128]{2,1,0:T(8,128)(2,1)S(1)}, u32[]{:S(2)}, u32[]{:S(2)}) %collective-permute-start.1) | collective-permute-done | bytes 262176 | tf_op jit(solution)/shard_map/ppermute | solution.py:375
  31.6 1.9 %collective-permute-done.low_ref = bf16[32,32,128]{2,1,0:T(8,128)(2,1)S(1)} collective-permute-done((bf16[32,32,128]{2,1,0:T(8,128)(2,1)S(1)}, bf16[32,32,128]{2,1,0:T(8,128)(2,1)S(1)}, u32[]{:S(2)}, u32[]{:S(2)}) %collective-permute-start) | collective-permute-done | bytes 262176 | tf_op jit(solution)/shard_map/ppermute | solution.py:374
  33.6 0.0 copy-done
  33.6 0.0 copy-start.1
  33.6 0.9 %copy-done.1 = bf16[32,32,128]{2,1,0:T(8,128)(2,1)S(1)} copy-done((bf16[32,32,128]{2,1,0:T(8,128)(2,1)S(1)}, bf16[32,32,128]{2,1,0:T(8,128)(2,1)}, u32[]{:S(2)}) %copy-start.1) | copy-done | bytes 262168
  34.5 0.0 copy-start.2
  34.5 1.6 %copy-done.2 = bf16[32,8,4096]{2,1,0:T(8,128)(2,1)S(1)} copy-done((bf16[32,8,4096]{2,1,0:T(8,128)(2,1)S(1)}, bf16[32,8,4096]{2,1,0:T(8,128)(2,1)}, u32[]{:S(2)}) %copy-start.2) | copy-done | bytes 2097176
  36.1 0.0 copy-start.4
  36.1 0.9 %copy-done.4 = bf16[32,4096]{1,0:T(8,128)(2,1)S(1)} copy-done((bf16[32,4096]{1,0:T(8,128)(2,1)S(1)}, bf16[32,4096]{1,0:T(8,128)(2,1)}, u32[]{:S(2)}) %copy-start.4) | copy-done | bytes 262168
  37.0 6.3 %near.1 = (bf16[288,32,128]{2,1,0:T(8,128)(2,1)S(1)}, f32[1664,32,128]{2,1,0:T(8,128)}) custom-call(s32[8,128]{1,0:T(8,128)S(1)} %get-tuple-element.10.lists_ref.lists_from, bf16[32,8,4096]{2,1,0:T(8,128)(2,1)S(1)} %copy-done.2, bf16[32,4096]{1,0:T(8,128)(2,1)S(1)} %copy-done.4, bf16[32,32,128]{2,1,0:T(8,128)(2,1)S(1)} %copy-done.1, ...), custom_call_target="tpu_custom_call" | custom-call | bytes 300000 | tf_op jit(solution)/shard_map/near/pallas_call | solution.py:392
  43.4 10.4 %all-to-all-done.1 = bf16[32,4,32,128]{3,2,1,0:T(8,128)(2,1)S(1)} async-done(((bf16[32,4,32,128]{3,2,1,0:T(8,128)(2,1)}), bf16[32,4,32,128]{3,2,1,0:T(8,128)(2,1)S(1)}, u32[]{:S(2)}, u32[]{:S(2)}) %all-to-all-start.1) | async-done | bytes 1048608 | tf_op jit(solution)/shard_map/all_to_all | solution.py:87
  53.8 4.1 %far.1 = bf16[32,16,1024]{2,1,0:T(8,128)(2,1)S(1)} custom-call(s32[8,128]{1,0:T(8,128)S(1)} %get-tuple-element.10.lists_ref.lists_from, bf16[288,32,128]{2,1,0:T(8,128)(2,1)S(1)} %get-tuple-element.11.work_ref, bf16[128,32,128]{2,1,0:T(8,128)(2,1)S(1)} %bitcast.10, f32[1664,32,128]{2,1,0:T(8,128)} %get-tuple-element.12.near_ref), custom_call_target="tpu_custom_call" | custom-call | bytes 18000000 | tf_op jit(solution)/shard_map/far/pallas_call | solution.py:408
  57.9 30.8 %all_to_all.15 = bf16[32,16,1024]{2,1,0:T(8,128)(2,1)S(1)} all-to-all(bf16[32,16,1024]{2,1,0:T(8,128)(2,1)S(1)} %far.1), channel_id=1, replica_groups={{31,30,29,28,27,26,25,24,23,22,21,20,19,18,17,16,15,14,13,12,11,10,9,8,..., dimensions={0} | all-to-all | bytes 2097152 | tf_op jit(solution)/shard_map/all_to_all | solution.py:87
  88.7 0.9 %holders.1 = f32[8,4096]{1,0:T(8,128)} custom-call(bf16[32,512]{1,0:T(8,128)(2,1)S(1)} %get-tuple-element.9.spread_ref, bf16[512,1024]{1,0:T(8,128)(2,1)S(1)} %bitcast.11), custom_call_target="tpu_custom_call" | custom-call | bytes 6000000 | tf_op jit(solution)/shard_map/holders/pallas_call | solution.py:423
Async XLA Ops:
  0.0 28.2 %copy-start.6 = (s32[32,8]{0,1:T(8,128)S(1)}, s32[32,8]{0,1:T(8,128)}, u32[]{:S(2)}) copy-start(s32[32,8]{0,1:T(8,128)} %param.9) | copy-start | bytes 3076
  0.0 28.2 %copy-start.7 = (s32[32]{0:T(128)S(1)}, s32[32]{0:T(128)}, u32[]{:S(2)}) copy-start(s32[32]{0:T(128)} %param.8) | copy-start | bytes 388
  0.0 28.2 %copy-start.5 = (s32[32,8]{0,1:T(8,128)S(1)}, s32[32,8]{0,1:T(8,128)}, u32[]{:S(2)}) copy-start(s32[32,8]{0,1:T(8,128)} %param.7) | copy-start | bytes 3076
  2.0 16.8 %all-to-all-start = ((s32[32,1,128]{2,1,0:T(1,128)}), s32[32,1,128]{2,1,0:T(1,128)S(1)}, u32[]{:S(2)}, u32[]{:S(2)}) async-start(s32[32,1,128]{2,1,0:T(1,128)} %bitcast.20), calls=%async_computation | async-start | bytes 32768 | tf_op jit(solution)/shard_map/all_to_all | solution.py:87
  13.9 1.0 %copy-start.3 = (bf16[32,4096]{1,0:T(8,128)(2,1)S(1)}, bf16[32,4096]{1,0:T(8,128)(2,1)}, u32[]{:S(2)}) copy-start(bf16[32,4096]{1,0:T(8,128)(2,1)} %p_ref.3) | copy-start | bytes 786436
  15.3 18.2 %copy-start = (bf16[32,32,128]{2,1,0:T(8,128)(2,1)}, bf16[32,32,128]{2,1,0:T(8,128)(2,1)S(1)}, u32[]{:S(2)}) copy-start(bf16[32,32,128]{2,1,0:T(8,128)(2,1)S(1)} %prepare.1.pq_ref) | copy-start | bytes 786436
  20.6 33.1 %all-to-all-start.1 = ((bf16[32,4,32,128]{3,2,1,0:T(8,128)(2,1)}), bf16[32,4,32,128]{3,2,1,0:T(8,128)(2,1)S(1)}, u32[]{:S(2)}, u32[]{:S(2)}) async-start(bf16[32,4,32,128]{3,2,1,0:T(8,128)(2,1)} %bitcast.6), calls=%async_computation.1 | async-start | bytes 2097152 | tf_op jit(solution)/shard_map/all_to_all | solution.py:87
  27.7 3.9 %collective-permute-start.1 = (bf16[32,32,128]{2,1,0:T(8,128)(2,1)S(1)}, bf16[32,32,128]{2,1,0:T(8,128)(2,1)S(1)}, u32[]{:S(2)}, u32[]{:S(2)}) collective-permute-start(bf16[32,32,128]{2,1,0:T(8,128)(2,1)S(1)} %prepare.1.pq_ref), channel_id=1, source_target_pairs={{32,0},{64,32},{96,64},{128,96},{160,128},{192,160},{224,192},{0,2... | collective-permute-start | bytes 786440 | tf_op jit(solution)/shard_map/ppermute | solution.py:375
  27.7 5.8 %collective-permute-start = (bf16[32,32,128]{2,1,0:T(8,128)(2,1)S(1)}, bf16[32,32,128]{2,1,0:T(8,128)(2,1)S(1)}, u32[]{:S(2)}, u32[]{:S(2)}) collective-permute-start(bf16[32,32,128]{2,1,0:T(8,128)(2,1)S(1)} %prepare.1.pq_ref), channel_id=1, source_target_pairs={{0,32},{32,64},{64,96},{96,128},{128,160},{160,192},{192,224},{224... | collective-permute-start | bytes 786440 | tf_op jit(solution)/shard_map/ppermute | solution.py:374
  33.6 1.0 %copy-start.1 = (bf16[32,32,128]{2,1,0:T(8,128)(2,1)S(1)}, bf16[32,32,128]{2,1,0:T(8,128)(2,1)}, u32[]{:S(2)}) copy-start(bf16[32,32,128]{2,1,0:T(8,128)(2,1)} %copy-done) | copy-start | bytes 786436
  34.5 1.6 %copy-start.2 = (bf16[32,8,4096]{2,1,0:T(8,128)(2,1)S(1)}, bf16[32,8,4096]{2,1,0:T(8,128)(2,1)}, u32[]{:S(2)}) copy-start(bf16[32,8,4096]{2,1,0:T(8,128)(2,1)} %a_ref.1) | copy-start | bytes 6291460
  36.1 0.9 %copy-start.4 = (bf16[32,4096]{1,0:T(8,128)(2,1)S(1)}, bf16[32,4096]{1,0:T(8,128)(2,1)}, u32[]{:S(2)}) copy-start(bf16[32,4096]{1,0:T(8,128)(2,1)} %p_ref.3) | copy-start | bytes 786436
